TPU v7x, 128 devices: a whole 4x4x4 slice. The times are simulated.
128 devices in a mesh: rcv: 16 (over y, x), freq: 8 (over z, core).
Axes of the slice: x: 4, y: 4, z: 4, core: 2. Of those that a mesh axis runs over, the one named last changes fastest.
Arguments:
- kernel: bfloat16 [2, 32, 4096, 4096], P(None, 'freq', 'rcv'), may hold values from -0.09375 to 0.09375
- data: float32 [2, 32, 4096, 32], P(None, 'freq', 'rcv'), may hold values from -6 to 6
- cutoffs: int32 [4096], P('rcv'), may hold values from 128 to 1024
Outputs:
- model: float32 [2, 32, 4096, 32], P(None, 'freq', 'rcv')
- residual: float32 [2, 32, 4096, 32], P(None, 'freq', 'rcv')
All inputs are finite; a program needn't handle non-finite values.
Results may differ from a plain program's by a relative error of at most 0.018.
Values may be sent and summed in bfloat16 or wider, within the bound.
No kernel may reach another device: no remote copies, remote signals or barrier semaphores. Data moves between devices by JAX's collectives and lax.ppermute only.
A program may use at most 256 MiB of HBM per device.

v0:
```python
import math

import jax
import jax.numpy as jnp
from jax import lax
from jax.sharding import PartitionSpec as P

NT = 1024
ITERS = 2


def for_sending(array):

    def short(part):
        return part.astype(jnp.bfloat16) if part.dtype == jnp.float32 else part

    return jax.tree.map(short, array)


def make_table(count_f, samples):
    steps_t = jnp.arange(samples, dtype=jnp.int32)
    bins = jnp.arange(count_f, dtype=jnp.int32) + 1
    phase = (steps_t[:, None] * bins[None, :] % samples).astype(jnp.float32) * (
        2.0 * math.pi / samples
    )
    scale = math.sqrt(2.0 / samples)
    return (scale * jnp.cos(phase), -scale * jnp.sin(phase))


def body(kernel, data, cutoffs):
    fdev = kernel.shape[1]
    local_points = cutoffs.shape[0]
    columns = data.shape[3]
    nfreq = lax.axis_size("freq")
    fcount = fdev * nfreq
    cosine, sine = make_table(fcount, NT)
    table = jnp.concatenate([cosine, sine], axis=1)
    sample_ids = jnp.arange(NT, dtype=jnp.int32)

    def window(values):
        share = local_points // nfreq
        start = lax.axis_index("freq") * share
        cut = lax.dynamic_slice_in_dim(cutoffs, start, share)
        keep = (sample_ids[:, None] < cut[None, :]).astype(jnp.float32)
        block = lax.all_to_all(
            for_sending(values), "freq", split_axis=2, concat_axis=1, tiled=True
        ).astype(values.dtype)
        items = block.shape[3]
        flat = block.reshape(2 * fcount, share * items)
        times = jnp.dot(table, flat, precision=lax.Precision.HIGHEST)
        times = (times.reshape(NT, share, items) * keep[:, :, None]).reshape(NT, share * items)
        back = jnp.dot(table.T, times, precision=lax.Precision.HIGHEST).reshape(
            2, fcount, share, items
        )
        return lax.all_to_all(
            for_sending(back), "freq", split_axis=1, concat_axis=2, tiled=True
        ).astype(back.dtype)

    def adjoint(rounded):
        joined = jnp.concatenate([rounded[0], rounded[1]], axis=-1)
        left = jnp.einsum("frv,frc->fvc", kernel[0], joined, preferred_element_type=jnp.float32)
        right = jnp.einsum("frv,frc->fvc", kernel[1], joined, preferred_element_type=jnp.float32)
        term = jnp.stack(
            [left[..., :columns] + right[..., columns:], left[..., columns:] - right[..., :columns]]
        )
        return lax.psum_scatter(
            term.astype(jnp.bfloat16), "rcv", scatter_dimension=2, tiled=True
        ).astype(jnp.float32)

    def model_norm(values):
        return lax.psum(jnp.sum(values * values), ("rcv", "freq"))

    model = jnp.zeros((2, fdev, local_points, columns), jnp.float32)
    residual = data
    grad = window(adjoint(residual.astype(jnp.bfloat16)))
    gamma = model_norm(grad)
    direction = grad
    for step in range(ITERS):
        shaped = window(direction).astype(jnp.bfloat16)
        piece = lax.all_gather(shaped, "rcv", axis=2, tiled=True)
        accumulate_joined = jnp.concatenate([piece[0], piece[1]], axis=-1)
        accumulate_left = jnp.einsum(
            "frv,fvc->frc", kernel[0], accumulate_joined, preferred_element_type=jnp.float32
        )
        accumulate_right = jnp.einsum(
            "frv,fvc->frc", kernel[1], accumulate_joined, preferred_element_type=jnp.float32
        )
        image = jnp.stack(
            [
                accumulate_left[..., :columns] - accumulate_right[..., columns:],
                accumulate_left[..., columns:] + accumulate_right[..., :columns],
            ]
        )
        delta = lax.psum(jnp.sum(image * image), ("rcv", "freq"))
        alpha = gamma / delta
        model = model + alpha * direction
        residual = residual - alpha * image
        if step + 1 < ITERS:
            grad = window(adjoint(residual.astype(jnp.bfloat16)))
            fresh = model_norm(grad)
            direction = grad + fresh / gamma * direction
            gamma = fresh
    return (model, residual)


def solution(mesh):
    placed = (P(None, "freq", "rcv", None), P(None, "freq", "rcv", None), P("rcv"))
    return jax.shard_map(
        body,
        mesh=mesh,
        in_specs=placed,
        out_specs=(P(None, "freq", "rcv", None), P(None, "freq", "rcv", None)),
        check_vma=False,
    )
```

profile of v0, /device:TPU:1, one launch (start us, length us, event | category | flops | bytes accessed | tf_op | source)
XLA Modules:
  0.0 641.0 jit_solution(10507525848396417946)
XLA Ops:
  7.2 1.0 convert_element_type.75
  8.2 5.0 fusion.22
  13.2 5.0 fusion.16
  18.1 0.8 fusion.80
  18.9 1.5 pad_maximum_fusion
  21.2 75.2 %reduce-scatter.3.cloned.1.call-done = bf16[2,4,256,32]{2,3,1,0:T(8,128)(2,1)} async-done(((bf16[2,4,4096,32]{2,3,1,0:T(8,128)(2,1)}), bf16[2,4,256,32]{2,3,1,0:T(8,128)(2,1)}) %reduce-scatter.3.cloned.1.call-update) | async-done | bytes 131088 | tf_op jit(solution)/shard_map/reduce_scatter | solution.py:66
  96.4 1.2 copy.22
  97.6 1.2 reshape.97
  98.8 6.7 %all-to-all-start = ((bf16[8,2,4096]{2,1,0:T(2,128)(2,1)}), bf16[8,2,4096]{2,1,0:T(2,128)(2,1)S(1)}, u32[]{:S(2)}, u32[]{:S(2)}) async-start(bf16[8,2,4096]{2,1,0:T(2,128)(2,1)} %reshape.97), calls=%async_computation.1 | async-start | bytes 262144 | tf_op jit(solution)/shard_map/all_to_all | solution.py:45
  105.8 5.0 all-to-all-done
  111.9 1.8 fusion.92
  113.7 10.4 %fusion.56 = bf16[2,32,32,32]{3,1,2,0:T(8,128)(2,1)S(1)} fusion(f32[2,32,1024,1]{2,1,3,0:T(8,128)S(1)} %bitcast.233, f32[1024,32,32]{0,2,1:T(8,128)S(1)} %fusion.92, f32[1024,32]{0,1:T(8,128)S(1)} %fusion.105), kind=kOutput, calls=%fused_computation.56 | convolution fusion | flops 806420480 | bytes 4718592 | tf_op jit(solution)/shard_map/dot_general | solution.py:52
  124.8 8.5 %all_to_all.123 = bf16[8,2,4096]{2,1,0:T(2,128)(2,1)S(1)} all-to-all(bf16[8,2,4096]{2,1,0:T(2,128)(2,1)S(1)} %reshape.99), channel_id=1, replica_groups=mesh['rcv'=16,'freq'=8] {'freq'}, dimensions={0} | all-to-all | bytes 262144 | tf_op jit(solution)/shard_map/all_to_all | solution.py:55
  135.1 9.0 %all_to_all.124 = bf16[8,2,4096]{2,1,0:T(2,128)(2,1)S(1)} all-to-all(bf16[8,2,4096]{2,1,0:T(2,128)(2,1)S(1)} %reshape.101), channel_id=1, replica_groups=mesh['rcv'=16,'freq'=8] {'freq'}, dimensions={0} | all-to-all | bytes 262144 | tf_op jit(solution)/shard_map/all_to_all | solution.py:45
  145.3 1.8 fusion.90
  147.1 10.4 %fusion.59 = bf16[2,32,32,32]{3,1,2,0:T(8,128)(2,1)S(1)} fusion(f32[2,32,1024,1]{2,1,3,0:T(8,128)S(1)} %bitcast.234, f32[1024,32,32]{0,2,1:T(8,128)S(1)} %fusion.90, f32[1024,32]{0,1:T(8,128)S(1)} %fusion.105), kind=kOutput, calls=%fused_computation.57 | convolution fusion | flops 806420480 | bytes 4718592 | tf_op jit(solution)/shard_map/dot_general | solution.py:52
  158.2 8.5 %all_to_all.125 = bf16[8,2,4096]{2,1,0:T(2,128)(2,1)S(1)} all-to-all(bf16[8,2,4096]{2,1,0:T(2,128)(2,1)S(1)} %reshape.103), channel_id=1, replica_groups=mesh['rcv'=16,'freq'=8] {'freq'}, dimensions={0} | all-to-all | bytes 262144 | tf_op jit(solution)/shard_map/all_to_all | solution.py:55
  167.4 1.0 all_to_all.103
  168.6 0.9 multiply_reduce_fusion.1
  169.5 43.2 %all-gather.3.cloned.1.call-done = bf16[2,4,4096,32]{2,3,1,0:T(8,128)(2,1)} async-done(((bf16[2,4,256,32]{2,3,1,0:T(8,128)(2,1)}), bf16[2,4,4096,32]{2,3,1,0:T(8,128)(2,1)}) %all-gather.3.cloned.1.call-update) | async-done | bytes 2097168 | tf_op jit(solution)/shard_map/all_gather | solution.py:80
  212.7 1.7 slice_bitcast_fusion.3
  214.4 5.0 fusion.74
  219.4 5.0 fusion.68
  224.5 0.7 multiply_reduce_fusion.3
  225.2 65.3 %all-reduce = (f32[]{:T(128)}, f32[]{:T(128)}) all-reduce(f32[]{:T(128)} %multiply_reduce_fusion.1, f32[]{:T(128)} %multiply_reduce_fusion.3), channel_id=1, replica_groups=mesh['rcv'=16,'freq'=8] {'rcv','freq'}, use_global_device_ids=true, to_apply=%region_2.3 | all-reduce | flops 2 | bytes 16 | tf_op jit(solution)/shard_map/psum | solution.py:71
  292.0 5.0 fusion.25
  296.9 5.0 fusion.19
  301.9 0.8 fusion.82
  302.7 1.5 pad_maximum_fusion.2
  304.3 69.1 %reduce-scatter.5.cloned.1.call-done = bf16[2,4,256,32]{2,3,1,0:T(8,128)(2,1)} async-done(((bf16[2,4,4096,32]{2,3,1,0:T(8,128)(2,1)}), bf16[2,4,256,32]{2,3,1,0:T(8,128)(2,1)}) %reduce-scatter.5.cloned.1.call-update) | async-done | bytes 131088 | tf_op jit(solution)/shard_map/reduce_scatter | solution.py:66
  373.3 1.2 copy.32
  375.1 12.0 %all_to_all.126 = bf16[8,2,4096]{2,1,0:T(2,128)(2,1)S(1)} all-to-all(bf16[8,2,4096]{2,1,0:T(2,128)(2,1)S(1)} %reshape.105), channel_id=1, replica_groups=mesh['rcv'=16,'freq'=8] {'freq'}, dimensions={0} | all-to-all | bytes 262144 | tf_op jit(solution)/shard_map/all_to_all | solution.py:45
  388.2 1.8 fusion.88
  390.0 10.4 %fusion.62 = bf16[2,32,32,32]{3,1,2,0:T(8,128)(2,1)S(1)} fusion(f32[2,32,1024,1]{2,1,3,0:T(8,128)S(1)} %bitcast.235, f32[1024,32,32]{0,2,1:T(8,128)S(1)} %fusion.88, f32[1024,32]{0,1:T(8,128)S(1)} %fusion.105), kind=kOutput, calls=%fused_computation.58 | convolution fusion | flops 806420480 | bytes 4718592 | tf_op jit(solution)/shard_map/dot_general | solution.py:52
  401.1 8.5 %all_to_all.127 = bf16[8,2,4096]{2,1,0:T(2,128)(2,1)S(1)} all-to-all(bf16[8,2,4096]{2,1,0:T(2,128)(2,1)S(1)} %reshape.107), channel_id=1, replica_groups=mesh['rcv'=16,'freq'=8] {'freq'}, dimensions={0} | all-to-all | bytes 262144 | tf_op jit(solution)/shard_map/all_to_all | solution.py:55
  409.9 0.9 multiply_reduce_fusion
  410.8 64.5 %psum.30 = f32[]{:T(128)} all-reduce(f32[]{:T(128)} %multiply_reduce_fusion), channel_id=1, replica_groups=mesh['rcv'=16,'freq'=8] {'rcv','freq'}, use_global_device_ids=true, to_apply=%region_7.8 | all-reduce | flops 1 | bytes 8 | tf_op jit(solution)/shard_map/psum | solution.py:71
  478.1 8.9 %all_to_all.128 = bf16[8,2,4096]{2,1,0:T(2,128)(2,1)S(1)} all-to-all(bf16[8,2,4096]{2,1,0:T(2,128)(2,1)S(1)} %reshape.109), channel_id=1, replica_groups=mesh['rcv'=16,'freq'=8] {'freq'}, dimensions={0} | all-to-all | bytes 262144 | tf_op jit(solution)/shard_map/all_to_all | solution.py:45
  488.1 1.8 fusion.86
  489.9 10.4 %fusion.65 = bf16[2,32,32,32]{3,1,2,0:T(8,128)(2,1)S(1)} fusion(f32[2,32,1024,1]{2,1,3,0:T(8,128)S(1)} %bitcast.236, f32[1024,32,32]{0,2,1:T(8,128)S(1)} %fusion.86, f32[1024,32]{0,1:T(8,128)S(1)} %fusion.105), kind=kOutput, calls=%fused_computation.59 | convolution fusion | flops 806420480 | bytes 4718592 | tf_op jit(solution)/shard_map/dot_general | solution.py:52
  501.0 8.7 %all_to_all.129 = bf16[8,2,4096]{2,1,0:T(2,128)(2,1)S(1)} all-to-all(bf16[8,2,4096]{2,1,0:T(2,128)(2,1)S(1)} %reshape.111), channel_id=1, replica_groups=mesh['rcv'=16,'freq'=8] {'freq'}, dimensions={0} | all-to-all | bytes 262144 | tf_op jit(solution)/shard_map/all_to_all | solution.py:55
  510.3 1.0 all_to_all.114
  511.4 42.9 %all-gather.5.cloned.1.call-done = bf16[2,4,4096,32]{2,3,1,0:T(8,128)(2,1)} async-done(((bf16[2,4,256,32]{2,3,1,0:T(8,128)(2,1)}), bf16[2,4,4096,32]{2,3,1,0:T(8,128)(2,1)}) %all-gather.5.cloned.1.call-update) | async-done | bytes 2097168 | tf_op jit(solution)/shard_map/all_gather | solution.py:80
  554.3 1.7 slice_bitcast_fusion.1
  556.0 5.0 fusion.77
  561.0 5.0 fusion.71
  566.7 65.4 %psum.31 = f32[]{:T(128)} all-reduce(f32[]{:T(128)} %multiply_reduce_fusion.2), channel_id=1, replica_groups=mesh['rcv'=16,'freq'=8] {'rcv','freq'}, use_global_device_ids=true, to_apply=%region_9.10 | all-reduce | flops 1 | bytes 8 | tf_op jit(solution)/shard_map/psum | solution.py:94
  633.4 0.9 fusion.84
  (63 shorter events, 14.6 us)
Async XLA Ops:
  7.2 89.2 %reduce-scatter.3.cloned.1.call-start = ((), (), s32[]{:S(2)}) async-start(), calls=%async_computation.10 | async-start | bytes 2228224 | tf_op jit(solution)/shard_map/reduce_scatter | solution.py:66
  18.9 1.6 copy-start.1
  98.8 12.0 %all-to-all-start = ((bf16[8,2,4096]{2,1,0:T(2,128)(2,1)}), bf16[8,2,4096]{2,1,0:T(2,128)(2,1)S(1)}, u32[]{:S(2)}, u32[]{:S(2)}) async-start(bf16[8,2,4096]{2,1,0:T(2,128)(2,1)} %reshape.97), calls=%async_computation.1 | async-start | bytes 262144 | tf_op jit(solution)/shard_map/all_to_all | solution.py:45
  105.5 107.2 %all-gather.3.cloned.1.call-start = ((), (), s32[]{:S(2)}) async-start(), calls=%async_computation.11 | async-start | bytes 2228224 | tf_op jit(solution)/shard_map/all_gather | solution.py:80
  168.4 204.9 %reduce-scatter.5.cloned.1.call-start = ((), (), s32[]{:S(2)}) async-start(), calls=%async_computation.12 | async-start | bytes 2228224 | tf_op jit(solution)/shard_map/reduce_scatter | solution.py:66
  219.4 72.5 %copy-start = (f32[2,4,256,32]{2,3,1,0:T(8,128)S(1)}, f32[2,4,256,32]{2,3,1,0:T(8,128)}, u32[]{:S(2)}) copy-start(f32[2,4,256,32]{2,3,1,0:T(8,128)} %param.4) | copy-start | bytes 786436
  304.2 250.1 %all-gather.5.cloned.1.call-start = ((), (), s32[]{:S(2)}) async-start(), calls=%async_computation.13 | async-start | bytes 2228224 | tf_op jit(solution)/shard_map/all_gather | solution.py:80
Sparse Core Ops, SparseCore 0:
  20.6 75.7 reduce-scatter.2
  168.5 44.1 all-gather.2
  304.3 68.9 reduce-scatter.4
  511.5 42.7 all-gather.4
where the time goes:
time: 646 us; the launch traced here: 641 us
  blocking collectives  259 us (40%)
  waiting for transfers between devices  235 us (36%)
  matrix products  88.8 us (14%)
  local copies, waits for them, and re-layouts  21.4 us (3%)
  between operations  18.4 us (3%)
  other arithmetic  10.4 us (2%)
  starting transfers between devices  7.32 us (1%)
    reduce_scatter x2, waiting for transfers between devices, adjoint(): lax.psum_scatter(term.astype(jnp.bfloat16), 'rcv', scatter_dimension=2, t...  144 us
    psum x2, blocking collectives, model_norm(): return lax.psum(jnp.sum(values * values), ('rcv', 'freq'))  130 us
    all_gather x2, waiting for transfers between devices, body(): piece = lax.all_gather(shaped, 'rcv', axis=2, tiled=True)  86.1 us
    psum x1, blocking collectives, body(): delta = lax.psum(jnp.sum(image * image), ('rcv', 'freq'))  65.4 us
    dot_general x4, matrix products, window(): jnp.dot(table.T, times, precision=lax.Precision.HIGHEST)  41.6 us
    all_to_all x4, blocking collectives, window(): lax.all_to_all(for_sending(back), 'freq', split_axis=1, concat_axis=2, ti...  34.2 us
    all_to_all x3, blocking collectives, window(): lax.all_to_all(for_sending(values), 'freq', split_axis=2, concat_axis=1,...  30 us
  transfers between devices with their start and end apart: 5, of which 5 were waited for; matrix products, arithmetic and copies ran while one was open for 0% of the time, Pallas kernels for 0%

commit v1 on v0

v1 whole, which is shorter than its diff:
```python
import math

import jax
import jax.numpy as jnp
import numpy as np
from jax import lax
from jax.experimental import pallas as pl
from jax.experimental.pallas import tpu as pltpu
from jax.sharding import PartitionSpec as P

NT = 1024
F = 32
AXES = ("rcv", "freq")
BF = jnp.bfloat16
F32 = jnp.float32
VMEM = pl.BlockSpec(memory_space=pltpu.VMEM)
SMEM = pl.BlockSpec(memory_space=pltpu.SMEM)
NT_DIMS = (((1,), (1,)), ((), ()))


def index(y, x, z, c):
    return (y * 4 + x) * 8 + z * 2 + c


DEVICES = [(y, x, z, c) for y in range(4) for x in range(4) for z in range(4) for c in range(2)]


def move(value, target):
    pairs = [(index(*d), index(*target(*d))) for d in DEVICES]
    return lax.ppermute(value, AXES, pairs)


def along_big(step):
    def target(y, x, z, c):
        return ((y + step) % 4, x, z, c) if c == 0 else (y, (x + step) % 4, z, c)

    return target


def along_small(step):
    def target(y, x, z, c):
        return (y, (x + step) % 4, z, c) if c == 0 else ((y + step) % 4, x, z, c)

    return target


def along_z(step):
    return lambda y, x, z, c: (y, x, (z + step) % 4, c)


def other_core(y, x, z, c):
    return (y, x, z, 1 - c)


def window_matrix():
    bins = np.arange(1, F + 1)
    theta = 2.0 * np.pi / NT

    def ratio(k):
        half = theta * k / 2.0
        safe = np.where(k == 0, 1.0, half)
        return np.where(k == 0, 0.0, 0.5 - 0.5j / np.tan(safe))

    direct = ratio(bins[:, None] - bins[None, :]) / NT
    mirror = ratio(bins[:, None] + bins[None, :]) / NT
    top = np.concatenate([direct.real + mirror.real, -direct.imag + mirror.imag], axis=1)
    low = np.concatenate([direct.imag + mirror.imag, direct.real - mirror.real], axis=1)
    return np.concatenate([top, low], axis=0).astype(np.float32)


def adjoint_kernel(j_ref, u_ref, k_ref, own_ref, oth_ref):
    def group(kb, carry):
        for ks in range(4):
            j = j_ref[kb * 4 + ks]
            cols = pl.ds(pl.multiple_of(j * 256, 256), 256)
            for f in range(4):
                u = u_ref[f]
                v = jnp.concatenate([u[16:32], -u[0:16], u[48:64], -u[32:48]], axis=0)
                r = jnp.dot(u, k_ref[0, f, :, cols], preferred_element_type=F32)
                r = r + jnp.dot(v, k_ref[1, f, :, cols], preferred_element_type=F32)
                r = r.astype(BF)
                own_ref[kb * 4 + ks, f] = r[:32]
                oth_ref[ks * 4 + kb, f] = r[32:]
        return carry

    lax.fori_loop(0, 4, group, 0)


def adjoint(table, u, kernel):
    shape = jax.ShapeDtypeStruct((16, 4, 32, 256), BF)
    return pl.pallas_call(
        adjoint_kernel,
        in_specs=[SMEM, VMEM, VMEM],
        out_specs=[VMEM, VMEM],
        out_shape=[shape, shape],
        compiler_params=pltpu.CompilerParams(vmem_limit_bytes=12 << 20),
        cost_estimate=pl.CostEstimate(flops=2 << 30, bytes_accessed=4 << 20, transcendentals=0),
        name="adjoint",
    )(table, u, kernel)


def forward_kernel(j_ref, own_ref, oth_ref, k_ref, out_ref):
    def one(f, carry):
        acc = jnp.zeros((256, 64), F32)
        for kb in range(4):
            for ks in range(4):
                j = j_ref[kb * 4 + ks]
                cols = pl.ds(pl.multiple_of(j * 256, 256), 256)
                a = own_ref[kb * 4 + ks, f]
                b = oth_ref[ks * 4 + kb, f]
                x = jnp.concatenate([a, b], axis=0)
                t = jnp.concatenate([-a[16:], a[:16], -b[16:], b[:16]], axis=0)
                acc = acc + lax.dot_general(
                    k_ref[0, f, :, cols], x, NT_DIMS, preferred_element_type=F32
                )
                acc = acc + lax.dot_general(
                    k_ref[1, f, :, cols], t, NT_DIMS, preferred_element_type=F32
                )
        out_ref[f] = acc.T
        return carry

    lax.fori_loop(0, 4, one, 0)


def forward(table, own, oth, kernel):
    return pl.pallas_call(
        forward_kernel,
        in_specs=[SMEM, VMEM, VMEM, VMEM],
        out_specs=VMEM,
        out_shape=jax.ShapeDtypeStruct((4, 64, 256), F32),
        compiler_params=pltpu.CompilerParams(vmem_limit_bytes=12 << 20),
        cost_estimate=pl.CostEstimate(flops=2 << 30, bytes_accessed=4 << 20, transcendentals=0),
        name="forward",
    )(table, own, oth, kernel)


def window_kernel(place_ref, a0, a1, a2, a3, m_ref, cos_ref, sin_ref, n_ref, g_ref, s_ref, y, g, s):
    z = place_ref[0]
    core = place_ref[1]
    for k, a in enumerate((a0, a1, a2, a3)):
        base = lax.rem(z + k, 4) * 256
        for half in range(2):
            start = base + (half + core - 2 * half * core) * 128
            rows = pl.ds(pl.multiple_of(start, 128), 128)
            part = a[pl.ds(half * 128, 128), :].astype(F32)
            y[0, rows, :] = part[:, :128]
            y[1, rows, :] = part[:, 128:]

    matrix = m_ref[...]
    cos = cos_ref[...]
    sin = sin_ref[...]
    share = n_ref[...]

    def apply(re, im):
        turned = jnp.concatenate([cos * re - sin * im, sin * re + cos * im], axis=0)
        flat = jnp.concatenate([re, im], axis=0)
        both = jnp.dot(
            matrix,
            jnp.concatenate([flat, turned], axis=1),
            precision=lax.Precision.HIGHEST,
            preferred_element_type=F32,
        )
        plain, w = both[:, :256], both[:, 256:]
        out_re = share * re + plain[:F] - cos * w[:F] - sin * w[F:]
        out_im = share * im + plain[F:] - cos * w[F:] + sin * w[:F]
        return out_re, out_im

    def take(ref, first):
        rows = pl.ds(first, F, stride=32)
        return jnp.concatenate([ref[0, rows, :], ref[1, rows, :]], axis=1)

    def put(ref, first, value):
        rows = pl.ds(first, F, stride=32)
        ref[0, rows, :] = value[:, :128]
        ref[1, rows, :] = value[:, 128:]

    def one(c, carry):
        re, im = apply(take(y, c), take(y, c + 16))
        put(g, c, re)
        put(g, c + 16, im)
        re, im = apply(re, im)
        put(s, c, re)
        put(s, c + 16, im)
        return carry

    lax.fori_loop(0, 16, one, 0)
    for half in range(2):
        start = z * 256 + (half + core - 2 * half * core) * 128
        rows = pl.ds(pl.multiple_of(start, 128), 128)
        g_ref[half] = jnp.concatenate([g[0, rows, :], g[1, rows, :]], axis=1)
        s_ref[half] = jnp.concatenate([s[0, rows, :], s[1, rows, :]], axis=1).astype(BF)


def window(place, blocks, matrix, cos, sin, share):
    return pl.pallas_call(
        window_kernel,
        in_specs=[SMEM] + [VMEM] * 8,
        out_specs=[VMEM, VMEM],
        out_shape=[
            jax.ShapeDtypeStruct((2, 128, 256), F32),
            jax.ShapeDtypeStruct((2, 128, 256), BF),
        ],
        scratch_shapes=[pltpu.VMEM((2, 1024, 128), F32)] * 3,
        compiler_params=pltpu.CompilerParams(vmem_limit_bytes=12 << 20),
        cost_estimate=pl.CostEstimate(flops=1 << 29, bytes_accessed=2 << 20, transcendentals=0),
        name="window",
    )(place, *blocks, matrix, cos, sin, share)


def total(values):
    values = values + move(values, other_core)
    for axis in (along_z, along_small, along_big):
        values = values + move(values, axis(1)) + move(values, axis(2)) + move(values, axis(3))
    return values


def body(kernel, data, cutoffs):
    rcv = lax.axis_index("rcv")
    freq = lax.axis_index("freq")
    yy, xx, zz, core = rcv // 4, rcv % 4, freq // 2, freq % 2
    place = jnp.stack([zz, core]).astype(jnp.int32)
    far = jnp.arange(16, dtype=jnp.int32) // 4
    near = jnp.arange(16, dtype=jnp.int32) % 4
    off_y = jnp.where(core == 0, far, near)
    off_x = jnp.where(core == 0, near, far)
    table = (yy + off_y) % 4 * 4 + (xx + off_x) % 4

    kernel = pltpu.with_memory_space_constraint(kernel, pltpu.VMEM)
    matrix = jnp.asarray(window_matrix())
    bins = jnp.arange(1, F + 1, dtype=jnp.int32)
    phase = (bins[:, None] * cutoffs[None, :] % NT).astype(F32) * (2.0 * math.pi / NT)
    cos, sin = jnp.cos(phase), jnp.sin(phase)
    share = (cutoffs.astype(F32) / NT)[None, :]

    def by_half(t):
        t = t.reshape(2, 4, 2, 16, 256).transpose(1, 2, 0, 3, 4)
        return jnp.where(core == 0, t, t[:, ::-1]).reshape(4, 64, 256)

    def from_half(t):
        t = t.reshape(4, 2, 2, 16, 256)
        t = jnp.where(core == 0, t, t[:, ::-1])
        return t.transpose(2, 0, 1, 3, 4).reshape(2, 4, 32, 256)

    def gather_terms(u):
        own, oth = adjoint(table, u, kernel)
        got = move(oth, other_core)
        own = own.reshape(4, 4, 128, 256)
        got = got.reshape(4, 4, 128, 256)
        pair = [jnp.stack([own[kb], got[kb]], axis=1) for kb in range(4)]
        rest = pair[0][1:].astype(F32)
        mine = pair[0][0].astype(F32)
        for kb in (2, 1, 3):
            rest = rest + move(pair[kb][1:], along_big(kb)).astype(F32)
        for kb in (2, 1, 3):
            mine = mine + move(pair[kb][0], along_big(kb)).astype(F32)
        rest = rest.astype(BF)
        for ks in (2, 1, 3):
            mine = mine + move(rest[ks - 1], along_small(ks)).astype(F32)
        mine = mine.astype(BF).reshape(256, 256)
        return [mine] + [move(mine, along_z(-k)) for k in (1, 2, 3)]

    def image_of(shaped):
        near = [shaped] + [move(shaped, along_small(-ks)) for ks in (1, 2, 3)]
        rest = jnp.stack(near[1:])
        blocks = [jnp.stack(near)]
        for kb in (1, 2, 3):
            first = move(shaped, along_big(-kb))
            more = move(rest, along_big(-kb))
            blocks.append(jnp.concatenate([first[None], more], axis=0))
        blocks = jnp.concatenate(blocks, axis=0)
        own = blocks[:, 0]
        oth = move(blocks[:, 1], other_core)
        return forward(
            table, own.reshape(16, 4, 32, 256), oth.reshape(16, 4, 32, 256), kernel
        )

    def windowed(blocks):
        return window(place, blocks, matrix, cos, sin, share)

    start = jnp.swapaxes(data, 2, 3)
    g0, s0 = windowed(gather_terms(by_half(start.astype(BF))))
    i0 = image_of(s0)
    h, s1 = windowed(gather_terms(i0.astype(BF)))
    i1 = image_of(s1)

    sums = [
        jnp.sum(g0 * g0),
        jnp.sum(g0 * h),
        jnp.sum(h * h),
        jnp.sum(i0 * i0),
        jnp.sum(i0 * i1),
        jnp.sum(i1 * i1),
    ]
    sums = total(jnp.stack(sums + [jnp.zeros((), F32)] * 2))
    gg, gh, hh, ii, ij, jj = [sums[k] for k in range(6)]
    alpha0 = gg / ii
    fresh = gg - 2.0 * alpha0 * gh + alpha0 * alpha0 * hh
    stay = 1.0 + fresh / gg
    delta = stay * stay * ii - 2.0 * stay * alpha0 * ij + alpha0 * alpha0 * jj
    alpha1 = fresh / delta
    on_first = alpha0 + alpha1 * stay
    on_second = alpha1 * alpha0

    def whole(t):
        got = move(t[1].astype(BF), other_core).astype(F32)
        joined = jnp.stack([t[0].reshape(4, 32, 256), got.reshape(4, 32, 256)], axis=1)
        return joined.reshape(4, 64, 256)

    model = from_half(on_first * whole(g0) - on_second * whole(h))
    residual = start - from_half(on_first * i0 - on_second * i1)
    return jnp.swapaxes(model, 2, 3), jnp.swapaxes(residual, 2, 3)


def solution(mesh):
    placed = P(None, "freq", "rcv", None)
    return jax.shard_map(
        body,
        mesh=mesh,
        in_specs=(placed, placed, P("rcv")),
        out_specs=(placed, placed),
        check_vma=False,
    )
```

time: 646 us -> 232 us (0.36)
  blocking collectives: 259 us -> 0 us
  waiting for transfers between devices: 235 us -> 83.2 us
  matrix products: 88.8 us -> 0 us
  starting transfers between devices: 7.32 us -> 73.1 us
  Pallas kernels: 0 us -> 42.1 us
  between operations: 18.4 us -> 7.06 us
    psum x3 -> x0, blocking collectives: 195 us -> none  [the longest x2 130 us: model_norm(): return lax.psum(jnp.sum(values * values), ('rcv', 'freq'))]
    reduce_scatter x2 -> x0, waiting for transfers between devices: 144 us -> none  [adjoint(): lax.psum_scatter(term.astype(jnp.bfloat16), 'rcv', scatter_dimension=2, t...]
    dot_general x16 -> x0, matrix products: 88.8 us -> none  [the longest x4 41.6 us: window(): jnp.dot(table.T, times, precision=lax.Precision.HIGHEST)]
    all_gather x2 -> x0, waiting for transfers between devices: 86.1 us -> none  [body(): piece = lax.all_gather(shaped, 'rcv', axis=2, tiled=True)]
    ppermute x0 -> x58, waiting for transfers between devices: none -> 83.2 us  [move(): return lax.ppermute(value, AXES, pairs)]
    ppermute x0 -> x58, starting transfers between devices: none -> 73.1 us  [move(): return lax.ppermute(value, AXES, pairs)]
    all_to_all x7 -> x0, blocking collectives: 64.2 us -> none  [the longest x4 34.2 us: window(): lax.all_to_all(for_sending(back), 'freq', split_axis=1, concat_axis=2, ti...]
    pallas_call x0 -> x6, Pallas kernels: none -> 42.1 us  [the longest x2 22.6 us: window(): pl.pallas_call(window_kernel, in_specs=[SMEM] + [VMEM] * 8, out_specs=[VM...]
  transfers between devices with their start and end apart: 5 -> 58, of which waited for: 5 -> 40; matrix products, arithmetic and copies ran while one was open for 0% -> 1% of each run, Pallas kernels for 0% -> 0%
where the time goes in v1:
time: 232 us; the launch traced here: 228 us
  waiting for transfers between devices  83.2 us (36%)
  starting transfers between devices  73.1 us (32%)
  Pallas kernels  42.1 us (18%)
  local copies, waits for them, and re-layouts  17.9 us (8%)
  between operations  7.06 us (3%)
  other arithmetic  4.72 us (2%)
    ppermute x58, waiting for transfers between devices, move(): return lax.ppermute(value, AXES, pairs)  83.2 us
    ppermute x58, starting transfers between devices, move(): return lax.ppermute(value, AXES, pairs)  73.1 us
    pallas_call x2, Pallas kernels, window(): pl.pallas_call(window_kernel, in_specs=[SMEM] + [VMEM] * 8, out_specs=[VM...  22.6 us
    unnamed x36, local copies, waits for them, and re-layouts  11.8 us
    pallas_call x2, Pallas kernels, forward(): pl.pallas_call(forward_kernel, in_specs=[SMEM, VMEM, VMEM, VMEM], out_spe...  11.4 us
    pallas_call x2, Pallas kernels, adjoint(): pl.pallas_call(adjoint_kernel, in_specs=[SMEM, VMEM, VMEM], out_specs=[VM...  8.13 us
  transfers between devices with their start and end apart: 58, of which 40 were waited for; matrix products, arithmetic and copies ran while one was open for 1% of the time, Pallas kernels for 0%

profile of v1, /device:TPU:1, one launch (start us, length us, event | category | flops | bytes accessed | tf_op | source)
XLA Modules:
  0.0 228.1 jit_solution(17999888533021458956)
XLA Ops:
  1.7 5.8 %copy-done = bf16[2,4,256,4096]{3,2,1,0:T(8,128)(2,1)S(1)} copy-done((bf16[2,4,256,4096]{3,2,1,0:T(8,128)(2,1)S(1)}, bf16[2,4,256,4096]{3,2,1,0:T(8,128)(2,1)}, u32[]{:S(2)}) %copy-start) | copy-done | bytes 16777240
  7.5 4.0 %adjoint.2 = (bf16[16,4,32,256]{3,2,1,0:T(8,128)(2,1)S(1)}, bf16[16,4,32,256]{3,2,1,0:T(8,128)(2,1)S(1)}) custom-call(s32[16]{0:T(128)S(1)} %fusion.22.j_ref, bf16[4,64,256]{2,1,0:T(8,128)(2,1)S(1)} %bitcast.180, bf16[2,4,256,4096]{3,2,1,0:T(8,128)(2,1)S(1)} %copy-done), custom_call_target="tpu_custom_call" | custom-call | flops 2147483648 | bytes 4194304 | tf_op jit(solution)/shard_map/adjoint/pallas_call | solution.py:91
  13.1 2.2 collective-permute-done
  15.5 2.6 %collective-permute-start.6 = (bf16[3,2,128,256]{3,2,1,0:T(8,128)(2,1)S(1)}, bf16[3,2,128,256]{3,2,1,0:T(8,128)(2,1)S(1)}, u32[]{:S(2)}, u32[]{:S(2)}) collective-permute-start(bf16[3,2,128,256]{3,2,1,0:T(8,128)(2,1)S(1)} %pad_maximum_fusion.4), channel_id=1, source_target_pairs={{0,96},{1,25},{2,98},{3,27},{4,100},{5,29},{6,102},{7,31},{8,104},... | collective-permute-start | bytes 1179656 | tf_op jit(solution)/shard_map/ppermute | solution.py:30
  18.3 1.8 collective-permute-start.4
  21.8 5.2 %collective-permute-done.6 = bf16[3,2,128,256]{3,2,1,0:T(8,128)(2,1)S(1)} collective-permute-done((bf16[3,2,128,256]{3,2,1,0:T(8,128)(2,1)S(1)}, bf16[3,2,128,256]{3,2,1,0:T(8,128)(2,1)S(1)}, u32[]{:S(2)}, u32[]{:S(2)}) %collective-permute-start.6) | collective-permute-done | bytes 393248 | tf_op jit(solution)/shard_map/ppermute | solution.py:30
  27.0 3.5 %collective-permute-done.5 = bf16[3,2,128,256]{3,2,1,0:T(8,128)(2,1)S(1)} collective-permute-done((bf16[3,2,128,256]{3,2,1,0:T(8,128)(2,1)S(1)}, bf16[3,2,128,256]{3,2,1,0:T(8,128)(2,1)S(1)}, u32[]{:S(2)}, u32[]{:S(2)}) %collective-permute-start.5) | collective-permute-done | bytes 393248 | tf_op jit(solution)/shard_map/ppermute | solution.py:30
  30.8 2.5 %collective-permute-start.9 = (bf16[2,128,256]{2,1,0:T(8,128)(2,1)S(1)}, bf16[2,128,256]{2,1,0:T(8,128)(2,1)S(1)}, u32[]{:S(2)}, u32[]{:S(2)}) collective-permute-start(bf16[2,128,256]{2,1,0:T(8,128)(2,1)S(1)} %get-tuple-element.48), channel_id=1, source_target_pairs={{0,24},{1,97},{2,26},{3,99},{4,28},{5,101},{6,30},{7,103},{8,0},{9... | collective-permute-start | bytes 393224 | tf_op jit(solution)/shard_map/ppermute | solution.py:30
  33.3 1.6 collective-permute-start.7
  36.3 3.7 %collective-permute-done.8 = bf16[2,128,256]{2,1,0:T(8,128)(2,1)S(1)} collective-permute-done((bf16[2,128,256]{2,1,0:T(8,128)(2,1)S(1)}, bf16[2,128,256]{2,1,0:T(8,128)(2,1)S(1)}, u32[]{:S(2)}, u32[]{:S(2)}) %collective-permute-start.8) | collective-permute-done | bytes 131104 | tf_op jit(solution)/shard_map/ppermute | solution.py:30
  40.2 3.8 %collective-permute-start.10 = (bf16[256,256]{1,0:T(8,128)(2,1)S(1)}, bf16[256,256]{1,0:T(8,128)(2,1)S(1)}, u32[]{:S(2)}, u32[]{:S(2)}) collective-permute-start(bf16[256,256]{1,0:T(8,128)(2,1)S(1)} %bitcast.181), channel_id=1, source_target_pairs={{0,6},{1,7},{2,0},{3,1},{4,2},{5,3},{6,4},{7,5},{8,14},{9,15},{10,... | collective-permute-start | bytes 393224 | tf_op jit(solution)/shard_map/ppermute | solution.py:30
  44.8 2.3 %collective-permute-done.10.a1 = bf16[256,256]{1,0:T(8,128)(2,1)S(1)} collective-permute-done((bf16[256,256]{1,0:T(8,128)(2,1)S(1)}, bf16[256,256]{1,0:T(8,128)(2,1)S(1)}, u32[]{:S(2)}, u32[]{:S(2)}) %collective-permute-start.10) | collective-permute-done | bytes 131104 | tf_op jit(solution)/shard_map/ppermute | solution.py:30
  47.1 2.4 %collective-permute-done.11.a2 = bf16[256,256]{1,0:T(8,128)(2,1)S(1)} collective-permute-done((bf16[256,256]{1,0:T(8,128)(2,1)S(1)}, bf16[256,256]{1,0:T(8,128)(2,1)S(1)}, u32[]{:S(2)}, u32[]{:S(2)}) %collective-permute-start.11) | collective-permute-done | bytes 131104 | tf_op jit(solution)/shard_map/ppermute | solution.py:30
  50.4 11.3 %window.2 = (f32[2,128,256]{2,1,0:T(8,128)S(1)}, bf16[2,128,256]{2,1,0:T(8,128)(2,1)S(1)}) custom-call(s32[2]{0:T(128)S(1)} %pad_add_fusion.place_ref, bf16[256,256]{1,0:T(8,128)(2,1)S(1)} %bitcast.184, bf16[256,256]{1,0:T(8,128)(2,1)S(1)} %collective-permute-done.10.a1, bf16[256,256]{1,0:T(8,128)(2,1)S(1)} %collective-permute-done.11.a2, ...), custom_call_target="tpu_custom_call" | custom-call | flops 536870912 | bytes 2097152 | tf_op jit(solution)/shard_map/window/pallas_call | solution.py:195
  61.7 3.7 %collective-permute-start.13 = (bf16[2,128,256]{2,1,0:T(8,128)(2,1)S(1)}, bf16[2,128,256]{2,1,0:T(8,128)(2,1)S(1)}, u32[]{:S(2)}, u32[]{:S(2)}) collective-permute-start(bf16[2,128,256]{2,1,0:T(8,128)(2,1)S(1)} %get-tuple-element.13), channel_id=1, source_target_pairs={{0,24},{1,97},{2,26},{3,99},{4,28},{5,101},{6,30},{7,103},{8,0},{9... | collective-permute-start | bytes 393224 | tf_op jit(solution)/shard_map/ppermute | solution.py:30
  66.2 2.9 %collective-permute-start.18 = (bf16[2,128,256]{2,1,0:T(8,128)(2,1)S(1)}, bf16[2,128,256]{2,1,0:T(8,128)(2,1)S(1)}, u32[]{:S(2)}, u32[]{:S(2)}) collective-permute-start(bf16[2,128,256]{2,1,0:T(8,128)(2,1)S(1)} %get-tuple-element.13), channel_id=1, source_target_pairs={{0,64},{1,17},{2,66},{3,19},{4,68},{5,21},{6,70},{7,23},{8,72},{9,... | collective-permute-start | bytes 393224 | tf_op jit(solution)/shard_map/ppermute | solution.py:30
  72.1 3.0 %collective-permute-start.19 = (bf16[3,2,128,256]{3,2,1,0:T(8,128)(2,1)S(1)}, bf16[3,2,128,256]{3,2,1,0:T(8,128)(2,1)S(1)}, u32[]{:S(2)}, u32[]{:S(2)}) collective-permute-start(bf16[3,2,128,256]{3,2,1,0:T(8,128)(2,1)S(1)} %pad_maximum_fusion.8), channel_id=1, source_target_pairs={{0,64},{1,17},{2,66},{3,19},{4,68},{5,21},{6,70},{7,23},{8,72},{9,... | collective-permute-start | bytes 1179656 | tf_op jit(solution)/shard_map/ppermute | solution.py:30
  75.3 3.4 %collective-permute-done.17 = bf16[3,2,128,256]{3,2,1,0:T(8,128)(2,1)S(1)} collective-permute-done((bf16[3,2,128,256]{3,2,1,0:T(8,128)(2,1)S(1)}, bf16[3,2,128,256]{3,2,1,0:T(8,128)(2,1)S(1)}, u32[]{:S(2)}, u32[]{:S(2)}) %collective-permute-start.17) | collective-permute-done | bytes 393248 | tf_op jit(solution)/shard_map/ppermute | solution.py:30
  78.7 2.0 collective-permute-done.19
  80.8 4.5 %collective-permute-done.21 = bf16[3,2,128,256]{3,2,1,0:T(8,128)(2,1)S(1)} collective-permute-done((bf16[3,2,128,256]{3,2,1,0:T(8,128)(2,1)S(1)}, bf16[3,2,128,256]{3,2,1,0:T(8,128)(2,1)S(1)}, u32[]{:S(2)}, u32[]{:S(2)}) %collective-permute-start.21) | collective-permute-done | bytes 393248 | tf_op jit(solution)/shard_map/ppermute | solution.py:30
  85.5 6.5 %collective-permute-start.22 = (bf16[16,128,256]{2,1,0:T(8,128)(2,1)S(1)}, bf16[16,128,256]{2,1,0:T(8,128)(2,1)S(1)}, u32[]{:S(2)}, u32[]{:S(2)}) collective-permute-start(bf16[16,128,256]{2,1,0:T(8,128)(2,1)S(1)} %get-tuple-element.26), channel_id=1, source_target_pairs={{0,1},{1,0},{2,3},{3,2},{4,5},{5,4},{6,7},{7,6},{8,9},{9,8},{10,11... | collective-permute-start | bytes 3145736 | tf_op jit(solution)/shard_map/ppermute | solution.py:30
  92.0 2.3 %collective-permute-done.22 = bf16[16,128,256]{2,1,0:T(8,128)(2,1)S(1)} collective-permute-done((bf16[16,128,256]{2,1,0:T(8,128)(2,1)S(1)}, bf16[16,128,256]{2,1,0:T(8,128)(2,1)S(1)}, u32[]{:S(2)}, u32[]{:S(2)}) %collective-permute-start.22) | collective-permute-done | bytes 1048608 | tf_op jit(solution)/shard_map/ppermute | solution.py:30
  94.3 5.8 %copy-done.1 = bf16[2,4,256,4096]{3,2,1,0:T(8,128)(2,1)S(1)} copy-done((bf16[2,4,256,4096]{3,2,1,0:T(8,128)(2,1)S(1)}, bf16[2,4,256,4096]{3,2,1,0:T(8,128)(2,1)}, u32[]{:S(2)}) %copy-start.1) | copy-done | bytes 16777240
  100.1 5.7 %forward.2 = f32[4,64,256]{2,1,0:T(8,128)S(1)} custom-call(s32[16]{0:T(128)S(1)} %fusion.22.j_ref, bf16[16,4,32,256]{3,2,1,0:T(8,128)(2,1)S(1)} %bitcast.177, bf16[16,4,32,256]{3,2,1,0:T(8,128)(2,1)S(1)} %bitcast.179, bf16[2,4,256,4096]{3,2,1,0:T(8,128)(2,1)S(1)} %copy-done.1), custom_call_target="tpu_custom_call" | custom-call | flops 2147483648 | bytes 4194304 | tf_op jit(solution)/shard_map/forward/pallas_call | solution.py:126
  105.8 4.1 %adjoint.3 = (bf16[16,4,32,256]{3,2,1,0:T(8,128)(2,1)S(1)}, bf16[16,4,32,256]{3,2,1,0:T(8,128)(2,1)S(1)}) custom-call(s32[16]{0:T(128)S(1)} %fusion.22.j_ref, bf16[4,64,256]{2,1,0:T(8,128)(2,1)S(1)} %convert_element_type.123.u_ref, bf16[2,4,256,4096]{3,2,1,0:T(8,128)(2,1)S(1)} %copy-done.1), custom_call_target="tpu_custom_call" | custom-call | flops 2147483648 | bytes 4194304 | tf_op jit(solution)/shard_map/adjoint/pallas_call | solution.py:91
  110.4 2.2 collective-permute-done.23
  114.5 2.2 collective-permute-start.27
  119.8 2.1 collective-permute-start.24
  122.1 4.2 %collective-permute-done.27 = bf16[3,2,128,256]{3,2,1,0:T(8,128)(2,1)S(1)} collective-permute-done((bf16[3,2,128,256]{3,2,1,0:T(8,128)(2,1)S(1)}, bf16[3,2,128,256]{3,2,1,0:T(8,128)(2,1)S(1)}, u32[]{:S(2)}, u32[]{:S(2)}) %collective-permute-start.27) | collective-permute-done | bytes 393248 | tf_op jit(solution)/shard_map/ppermute | solution.py:30
  128.0 1.6 collective-permute-start.30
  133.6 5.4 %collective-permute-start.33 = (bf16[256,256]{1,0:T(8,128)(2,1)S(1)}, bf16[256,256]{1,0:T(8,128)(2,1)S(1)}, u32[]{:S(2)}, u32[]{:S(2)}) collective-permute-start(bf16[256,256]{1,0:T(8,128)(2,1)S(1)} %bitcast.185), channel_id=1, source_target_pairs={{0,6},{1,7},{2,0},{3,1},{4,2},{5,3},{6,4},{7,5},{8,14},{9,15},{10,... | collective-permute-start | bytes 393224 | tf_op jit(solution)/shard_map/ppermute | solution.py:30
  139.7 2.6 %collective-permute-done.33.a1 = bf16[256,256]{1,0:T(8,128)(2,1)S(1)} collective-permute-done((bf16[256,256]{1,0:T(8,128)(2,1)S(1)}, bf16[256,256]{1,0:T(8,128)(2,1)S(1)}, u32[]{:S(2)}, u32[]{:S(2)}) %collective-permute-start.33) | collective-permute-done | bytes 131104 | tf_op jit(solution)/shard_map/ppermute | solution.py:30
  142.3 2.1 collective-permute-done.34.a2
  145.4 11.3 %window.3 = (f32[2,128,256]{2,1,0:T(8,128)S(1)}, bf16[2,128,256]{2,1,0:T(8,128)(2,1)S(1)}) custom-call(s32[2]{0:T(128)S(1)} %pad_add_fusion.place_ref, bf16[256,256]{1,0:T(8,128)(2,1)S(1)} %bitcast.188, bf16[256,256]{1,0:T(8,128)(2,1)S(1)} %collective-permute-done.33.a1, bf16[256,256]{1,0:T(8,128)(2,1)S(1)} %collective-permute-done.34.a2, ...), custom_call_target="tpu_custom_call" | custom-call | flops 536870912 | bytes 2097152 | tf_op jit(solution)/shard_map/window/pallas_call | solution.py:195
  156.7 4.2 %collective-permute-start.36 = (bf16[2,128,256]{2,1,0:T(8,128)(2,1)S(1)}, bf16[2,128,256]{2,1,0:T(8,128)(2,1)S(1)}, u32[]{:S(2)}, u32[]{:S(2)}) collective-permute-start(bf16[2,128,256]{2,1,0:T(8,128)(2,1)S(1)} %get-tuple-element.17), channel_id=1, source_target_pairs={{0,24},{1,97},{2,26},{3,99},{4,28},{5,101},{6,30},{7,103},{8,0},{9... | collective-permute-start | bytes 393224 | tf_op jit(solution)/shard_map/ppermute | solution.py:30
  161.6 2.6 %collective-permute-done.36 = bf16[2,128,256]{2,1,0:T(8,128)(2,1)S(1)} collective-permute-done((bf16[2,128,256]{2,1,0:T(8,128)(2,1)S(1)}, bf16[2,128,256]{2,1,0:T(8,128)(2,1)S(1)}, u32[]{:S(2)}, u32[]{:S(2)}) %collective-permute-start.36) | collective-permute-done | bytes 131104 | tf_op jit(solution)/shard_map/ppermute | solution.py:30
  164.2 2.1 collective-permute-done.37
  169.4 5.0 %collective-permute-done.40 = bf16[3,2,128,256]{3,2,1,0:T(8,128)(2,1)S(1)} collective-permute-done((bf16[3,2,128,256]{3,2,1,0:T(8,128)(2,1)S(1)}, bf16[3,2,128,256]{3,2,1,0:T(8,128)(2,1)S(1)}, u32[]{:S(2)}, u32[]{:S(2)}) %collective-permute-start.40) | collective-permute-done | bytes 393248 | tf_op jit(solution)/shard_map/ppermute | solution.py:30
  174.5 1.6 collective-permute-done.42
  176.2 4.3 %collective-permute-done.44 = bf16[3,2,128,256]{3,2,1,0:T(8,128)(2,1)S(1)} collective-permute-done((bf16[3,2,128,256]{3,2,1,0:T(8,128)(2,1)S(1)}, bf16[3,2,128,256]{3,2,1,0:T(8,128)(2,1)S(1)}, u32[]{:S(2)}, u32[]{:S(2)}) %collective-permute-start.44) | collective-permute-done | bytes 393248 | tf_op jit(solution)/shard_map/ppermute | solution.py:30
  180.8 5.3 %collective-permute-start.45 = (bf16[16,128,256]{2,1,0:T(8,128)(2,1)S(1)}, bf16[16,128,256]{2,1,0:T(8,128)(2,1)S(1)}, u32[]{:S(2)}, u32[]{:S(2)}) collective-permute-start(bf16[16,128,256]{2,1,0:T(8,128)(2,1)S(1)} %get-tuple-element.24), channel_id=1, source_target_pairs={{0,1},{1,0},{2,3},{3,2},{4,5},{5,4},{6,7},{7,6},{8,9},{9,8},{10,11... | collective-permute-start | bytes 3145736 | tf_op jit(solution)/shard_map/ppermute | solution.py:30
  186.2 2.3 collective-permute-done.56
  190.1 5.7 %forward.3 = f32[4,64,256]{2,1,0:T(8,128)S(1)} custom-call(s32[16]{0:T(128)S(1)} %fusion.22.j_ref, bf16[16,4,32,256]{3,2,1,0:T(8,128)(2,1)S(1)} %bitcast.176, bf16[16,4,32,256]{3,2,1,0:T(8,128)(2,1)S(1)} %bitcast.178, bf16[2,4,256,4096]{3,2,1,0:T(8,128)(2,1)S(1)} %bitcast.175), custom_call_target="tpu_custom_call" | custom-call | flops 2147483648 | bytes 4194304 | tf_op jit(solution)/shard_map/forward/pallas_call | solution.py:126
  196.6 3.8 %stack.135 = f32[8]{0:T(128)S(1)} concatenate(f32[1]{0:T(128)} %bitcast.31, f32[1]{0:T(128)} %bitcast.66, f32[1]{0:T(128)} %bitcast.67, f32[1]{0:T(128)} %bitcast.68, f32[1]{0:T(128)} %bitcast.79, f32[1]{0:T(128)} %bitcast.80, f32[2]{0:T(128)S(1)} %broadcast.48), dimensions={0} | concatenate | bytes 64 | tf_op jit(solution)/shard_map/stack | solution.py:294
  201.6 4.9 %collective-permute-start.49 = (f32[8]{0:T(128)S(1)}, f32[8]{0:T(128)S(1)}, u32[]{:S(2)}, u32[]{:S(2)}) collective-permute-start(f32[8]{0:T(128)S(1)} %add.181), channel_id=1, source_target_pairs={{0,6},{1,7},{2,0},{3,1},{4,2},{5,3},{6,4},{7,5},{8,14},{9,15},{10,... | collective-permute-start | bytes 104 | tf_op jit(solution)/shard_map/ppermute | solution.py:30
  207.1 3.2 %collective-permute-done.48 = f32[8]{0:T(128)S(1)} collective-permute-done((f32[8]{0:T(128)S(1)}, f32[8]{0:T(128)S(1)}, u32[]{:S(2)}, u32[]{:S(2)}) %collective-permute-start.48) | collective-permute-done | bytes 64 | tf_op jit(solution)/shard_map/ppermute | solution.py:30
  212.8 2.4 %collective-permute-done.51 = f32[8]{0:T(128)S(1)} collective-permute-done((f32[8]{0:T(128)S(1)}, f32[8]{0:T(128)S(1)}, u32[]{:S(2)}, u32[]{:S(2)}) %collective-permute-start.51) | collective-permute-done | bytes 64 | tf_op jit(solution)/shard_map/ppermute | solution.py:30
  217.6 1.6 collective-permute-done.54
  (169 shorter events, 41.5 us)
Async XLA Ops:
  15.5 11.6 %collective-permute-start.6 = (bf16[3,2,128,256]{3,2,1,0:T(8,128)(2,1)S(1)}, bf16[3,2,128,256]{3,2,1,0:T(8,128)(2,1)S(1)}, u32[]{:S(2)}, u32[]{:S(2)}) collective-permute-start(bf16[3,2,128,256]{3,2,1,0:T(8,128)(2,1)S(1)} %pad_maximum_fusion.4), channel_id=1, source_target_pairs={{0,96},{1,25},{2,98},{3,27},{4,100},{5,29},{6,102},{7,31},{8,104},... | collective-permute-start | bytes 1179656 | tf_op jit(solution)/shard_map/ppermute | solution.py:30
  18.1 12.4 %collective-permute-start.5 = (bf16[3,2,128,256]{3,2,1,0:T(8,128)(2,1)S(1)}, bf16[3,2,128,256]{3,2,1,0:T(8,128)(2,1)S(1)}, u32[]{:S(2)}, u32[]{:S(2)}) collective-permute-start(bf16[3,2,128,256]{3,2,1,0:T(8,128)(2,1)S(1)} %pad_maximum_fusion.5), channel_id=1, source_target_pairs={{0,32},{1,9},{2,34},{3,11},{4,36},{5,13},{6,38},{7,15},{8,40},{9,1... | collective-permute-start | bytes 1179656 | tf_op jit(solution)/shard_map/ppermute | solution.py:30
  18.3 12.3 %collective-permute-start.4 = (bf16[3,2,128,256]{3,2,1,0:T(8,128)(2,1)S(1)}, bf16[3,2,128,256]{3,2,1,0:T(8,128)(2,1)S(1)}, u32[]{:S(2)}, u32[]{:S(2)}) collective-permute-start(bf16[3,2,128,256]{3,2,1,0:T(8,128)(2,1)S(1)} %pad_maximum_fusion.6), channel_id=1, source_target_pairs={{0,64},{1,17},{2,66},{3,19},{4,68},{5,21},{6,70},{7,23},{8,72},{9,... | collective-permute-start | bytes 1179656 | tf_op jit(solution)/shard_map/ppermute | solution.py:30
  20.1 13.2 %collective-permute-start.3 = (bf16[2,128,256]{2,1,0:T(8,128)(2,1)S(1)}, bf16[2,128,256]{2,1,0:T(8,128)(2,1)S(1)}, u32[]{:S(2)}, u32[]{:S(2)}) collective-permute-start(bf16[2,128,256]{2,1,0:T(8,128)(2,1)S(1)} %maximum_bitcast_fusion.4), channel_id=1, source_target_pairs={{0,96},{1,25},{2,98},{3,27},{4,100},{5,29},{6,102},{7,31},{8,104},... | collective-permute-start | bytes 393224 | tf_op jit(solution)/shard_map/ppermute | solution.py:30
  21.2 14.0 %collective-permute-start.2 = (bf16[2,128,256]{2,1,0:T(8,128)(2,1)S(1)}, bf16[2,128,256]{2,1,0:T(8,128)(2,1)S(1)}, u32[]{:S(2)}, u32[]{:S(2)}) collective-permute-start(bf16[2,128,256]{2,1,0:T(8,128)(2,1)S(1)} %maximum_bitcast_fusion.5), channel_id=1, source_target_pairs={{0,32},{1,9},{2,34},{3,11},{4,36},{5,13},{6,38},{7,15},{8,40},{9,1... | collective-permute-start | bytes 393224 | tf_op jit(solution)/shard_map/ppermute | solution.py:30
  27.0 8.1 %collective-permute-start.1 = (bf16[2,128,256]{2,1,0:T(8,128)(2,1)S(1)}, bf16[2,128,256]{2,1,0:T(8,128)(2,1)S(1)}, u32[]{:S(2)}, u32[]{:S(2)}) collective-permute-start(bf16[2,128,256]{2,1,0:T(8,128)(2,1)S(1)} %maximum_bitcast_fusion.6), channel_id=1, source_target_pairs={{0,64},{1,17},{2,66},{3,19},{4,68},{5,21},{6,70},{7,23},{8,72},{9,... | collective-permute-start | bytes 393224 | tf_op jit(solution)/shard_map/ppermute | solution.py:30
  30.8 5.5 %collective-permute-start.9 = (bf16[2,128,256]{2,1,0:T(8,128)(2,1)S(1)}, bf16[2,128,256]{2,1,0:T(8,128)(2,1)S(1)}, u32[]{:S(2)}, u32[]{:S(2)}) collective-permute-start(bf16[2,128,256]{2,1,0:T(8,128)(2,1)S(1)} %get-tuple-element.48), channel_id=1, source_target_pairs={{0,24},{1,97},{2,26},{3,99},{4,28},{5,101},{6,30},{7,103},{8,0},{9... | collective-permute-start | bytes 393224 | tf_op jit(solution)/shard_map/ppermute | solution.py:30
  33.3 6.7 %collective-permute-start.8 = (bf16[2,128,256]{2,1,0:T(8,128)(2,1)S(1)}, bf16[2,128,256]{2,1,0:T(8,128)(2,1)S(1)}, u32[]{:S(2)}, u32[]{:S(2)}) collective-permute-start(bf16[2,128,256]{2,1,0:T(8,128)(2,1)S(1)} %get-tuple-element.49), channel_id=1, source_target_pairs={{0,8},{1,33},{2,10},{3,35},{4,12},{5,37},{6,14},{7,39},{8,16},{9,4... | collective-permute-start | bytes 393224 | tf_op jit(solution)/shard_map/ppermute | solution.py:30
  33.3 6.7 %collective-permute-start.7 = (bf16[2,128,256]{2,1,0:T(8,128)(2,1)S(1)}, bf16[2,128,256]{2,1,0:T(8,128)(2,1)S(1)}, u32[]{:S(2)}, u32[]{:S(2)}) collective-permute-start(bf16[2,128,256]{2,1,0:T(8,128)(2,1)S(1)} %get-tuple-element.47), channel_id=1, source_target_pairs={{0,16},{1,65},{2,18},{3,67},{4,20},{5,69},{6,22},{7,71},{8,24},{9,... | collective-permute-start | bytes 393224 | tf_op jit(solution)/shard_map/ppermute | solution.py:30
  40.2 6.9 %collective-permute-start.10 = (bf16[256,256]{1,0:T(8,128)(2,1)S(1)}, bf16[256,256]{1,0:T(8,128)(2,1)S(1)}, u32[]{:S(2)}, u32[]{:S(2)}) collective-permute-start(bf16[256,256]{1,0:T(8,128)(2,1)S(1)} %bitcast.181), channel_id=1, source_target_pairs={{0,6},{1,7},{2,0},{3,1},{4,2},{5,3},{6,4},{7,5},{8,14},{9,15},{10,... | collective-permute-start | bytes 393224 | tf_op jit(solution)/shard_map/ppermute | solution.py:30
  44.0 5.4 %collective-permute-start.11 = (bf16[256,256]{1,0:T(8,128)(2,1)S(1)}, bf16[256,256]{1,0:T(8,128)(2,1)S(1)}, u32[]{:S(2)}, u32[]{:S(2)}) collective-permute-start(bf16[256,256]{1,0:T(8,128)(2,1)S(1)} %bitcast.182), channel_id=1, source_target_pairs={{0,4},{1,5},{2,6},{3,7},{4,0},{5,1},{6,2},{7,3},{8,12},{9,13},{10,... | collective-permute-start | bytes 393224 | tf_op jit(solution)/shard_map/ppermute | solution.py:30
  44.0 6.4 %collective-permute-start.12 = (bf16[256,256]{1,0:T(8,128)(2,1)S(1)}, bf16[256,256]{1,0:T(8,128)(2,1)S(1)}, u32[]{:S(2)}, u32[]{:S(2)}) collective-permute-start(bf16[256,256]{1,0:T(8,128)(2,1)S(1)} %bitcast.183), channel_id=1, source_target_pairs={{0,2},{1,3},{2,4},{3,5},{4,6},{5,7},{6,0},{7,1},{8,10},{9,11},{10,... | collective-permute-start | bytes 393224 | tf_op jit(solution)/shard_map/ppermute | solution.py:30
  61.7 7.3 %collective-permute-start.13 = (bf16[2,128,256]{2,1,0:T(8,128)(2,1)S(1)}, bf16[2,128,256]{2,1,0:T(8,128)(2,1)S(1)}, u32[]{:S(2)}, u32[]{:S(2)}) collective-permute-start(bf16[2,128,256]{2,1,0:T(8,128)(2,1)S(1)} %get-tuple-element.13), channel_id=1, source_target_pairs={{0,24},{1,97},{2,26},{3,99},{4,28},{5,101},{6,30},{7,103},{8,0},{9... | collective-permute-start | bytes 393224 | tf_op jit(solution)/shard_map/ppermute | solution.py:30
  65.5 5.4 %collective-permute-start.14 = (bf16[2,128,256]{2,1,0:T(8,128)(2,1)S(1)}, bf16[2,128,256]{2,1,0:T(8,128)(2,1)S(1)}, u32[]{:S(2)}, u32[]{:S(2)}) collective-permute-start(bf16[2,128,256]{2,1,0:T(8,128)(2,1)S(1)} %get-tuple-element.13), channel_id=1, source_target_pairs={{0,16},{1,65},{2,18},{3,67},{4,20},{5,69},{6,22},{7,71},{8,24},{9,... | collective-permute-start | bytes 393224 | tf_op jit(solution)/shard_map/ppermute | solution.py:30
  65.5 6.4 %collective-permute-start.15 = (bf16[2,128,256]{2,1,0:T(8,128)(2,1)S(1)}, bf16[2,128,256]{2,1,0:T(8,128)(2,1)S(1)}, u32[]{:S(2)}, u32[]{:S(2)}) collective-permute-start(bf16[2,128,256]{2,1,0:T(8,128)(2,1)S(1)} %get-tuple-element.13), channel_id=1, source_target_pairs={{0,8},{1,33},{2,10},{3,35},{4,12},{5,37},{6,14},{7,39},{8,16},{9,4... | collective-permute-start | bytes 393224 | tf_op jit(solution)/shard_map/ppermute | solution.py:30
  66.2 9.0 %collective-permute-start.16 = (bf16[2,128,256]{2,1,0:T(8,128)(2,1)S(1)}, bf16[2,128,256]{2,1,0:T(8,128)(2,1)S(1)}, u32[]{:S(2)}, u32[]{:S(2)}) collective-permute-start(bf16[2,128,256]{2,1,0:T(8,128)(2,1)S(1)} %get-tuple-element.13), channel_id=1, source_target_pairs={{0,96},{1,25},{2,98},{3,27},{4,100},{5,29},{6,102},{7,31},{8,104},... | collective-permute-start | bytes 393224 | tf_op jit(solution)/shard_map/ppermute | solution.py:30
  66.2 12.5 %collective-permute-start.18 = (bf16[2,128,256]{2,1,0:T(8,128)(2,1)S(1)}, bf16[2,128,256]{2,1,0:T(8,128)(2,1)S(1)}, u32[]{:S(2)}, u32[]{:S(2)}) collective-permute-start(bf16[2,128,256]{2,1,0:T(8,128)(2,1)S(1)} %get-tuple-element.13), channel_id=1, source_target_pairs={{0,64},{1,17},{2,66},{3,19},{4,68},{5,21},{6,70},{7,23},{8,72},{9,... | collective-permute-start | bytes 393224 | tf_op jit(solution)/shard_map/ppermute | solution.py:30
  69.1 11.7 %collective-permute-start.20 = (bf16[2,128,256]{2,1,0:T(8,128)(2,1)S(1)}, bf16[2,128,256]{2,1,0:T(8,128)(2,1)S(1)}, u32[]{:S(2)}, u32[]{:S(2)}) collective-permute-start(bf16[2,128,256]{2,1,0:T(8,128)(2,1)S(1)} %get-tuple-element.13), channel_id=1, source_target_pairs={{0,32},{1,9},{2,34},{3,11},{4,36},{5,13},{6,38},{7,15},{8,40},{9,1... | collective-permute-start | bytes 393224 | tf_op jit(solution)/shard_map/ppermute | solution.py:30
  72.0 6.7 %collective-permute-start.17 = (bf16[3,2,128,256]{3,2,1,0:T(8,128)(2,1)S(1)}, bf16[3,2,128,256]{3,2,1,0:T(8,128)(2,1)S(1)}, u32[]{:S(2)}, u32[]{:S(2)}) collective-permute-start(bf16[3,2,128,256]{3,2,1,0:T(8,128)(2,1)S(1)} %pad_maximum_fusion.8), channel_id=1, source_target_pairs={{0,96},{1,25},{2,98},{3,27},{4,100},{5,29},{6,102},{7,31},{8,104},... | collective-permute-start | bytes 1179656 | tf_op jit(solution)/shard_map/ppermute | solution.py:30
  72.1 8.7 %collective-permute-start.19 = (bf16[3,2,128,256]{3,2,1,0:T(8,128)(2,1)S(1)}, bf16[3,2,128,256]{3,2,1,0:T(8,128)(2,1)S(1)}, u32[]{:S(2)}, u32[]{:S(2)}) collective-permute-start(bf16[3,2,128,256]{3,2,1,0:T(8,128)(2,1)S(1)} %pad_maximum_fusion.8), channel_id=1, source_target_pairs={{0,64},{1,17},{2,66},{3,19},{4,68},{5,21},{6,70},{7,23},{8,72},{9,... | collective-permute-start | bytes 1179656 | tf_op jit(solution)/shard_map/ppermute | solution.py:30
  75.2 10.2 %collective-permute-start.21 = (bf16[3,2,128,256]{3,2,1,0:T(8,128)(2,1)S(1)}, bf16[3,2,128,256]{3,2,1,0:T(8,128)(2,1)S(1)}, u32[]{:S(2)}, u32[]{:S(2)}) collective-permute-start(bf16[3,2,128,256]{3,2,1,0:T(8,128)(2,1)S(1)} %pad_maximum_fusion.8), channel_id=1, source_target_pairs={{0,32},{1,9},{2,34},{3,11},{4,36},{5,13},{6,38},{7,15},{8,40},{9,1... | collective-permute-start | bytes 1179656 | tf_op jit(solution)/shard_map/ppermute | solution.py:30
  85.5 8.8 %collective-permute-start.22 = (bf16[16,128,256]{2,1,0:T(8,128)(2,1)S(1)}, bf16[16,128,256]{2,1,0:T(8,128)(2,1)S(1)}, u32[]{:S(2)}, u32[]{:S(2)}) collective-permute-start(bf16[16,128,256]{2,1,0:T(8,128)(2,1)S(1)} %get-tuple-element.26), channel_id=1, source_target_pairs={{0,1},{1,0},{2,3},{3,2},{4,5},{5,4},{6,7},{7,6},{8,9},{9,8},{10,11... | collective-permute-start | bytes 3145736 | tf_op jit(solution)/shard_map/ppermute | solution.py:30
  112.8 7.0 %collective-permute-start.29 = (bf16[3,2,128,256]{3,2,1,0:T(8,128)(2,1)S(1)}, bf16[3,2,128,256]{3,2,1,0:T(8,128)(2,1)S(1)}, u32[]{:S(2)}, u32[]{:S(2)}) collective-permute-start(bf16[3,2,128,256]{3,2,1,0:T(8,128)(2,1)S(1)} %pad_maximum_fusion), channel_id=1, source_target_pairs={{0,96},{1,25},{2,98},{3,27},{4,100},{5,29},{6,102},{7,31},{8,104},... | collective-permute-start | bytes 1179656 | tf_op jit(solution)/shard_map/ppermute | solution.py:30
  113.9 8.2 %collective-permute-start.28 = (bf16[3,2,128,256]{3,2,1,0:T(8,128)(2,1)S(1)}, bf16[3,2,128,256]{3,2,1,0:T(8,128)(2,1)S(1)}, u32[]{:S(2)}, u32[]{:S(2)}) collective-permute-start(bf16[3,2,128,256]{3,2,1,0:T(8,128)(2,1)S(1)} %pad_maximum_fusion.1), channel_id=1, source_target_pairs={{0,32},{1,9},{2,34},{3,11},{4,36},{5,13},{6,38},{7,15},{8,40},{9,1... | collective-permute-start | bytes 1179656 | tf_op jit(solution)/shard_map/ppermute | solution.py:30
  114.5 11.8 %collective-permute-start.27 = (bf16[3,2,128,256]{3,2,1,0:T(8,128)(2,1)S(1)}, bf16[3,2,128,256]{3,2,1,0:T(8,128)(2,1)S(1)}, u32[]{:S(2)}, u32[]{:S(2)}) collective-permute-start(bf16[3,2,128,256]{3,2,1,0:T(8,128)(2,1)S(1)} %pad_maximum_fusion.2), channel_id=1, source_target_pairs={{0,64},{1,17},{2,66},{3,19},{4,68},{5,21},{6,70},{7,23},{8,72},{9,... | collective-permute-start | bytes 1179656 | tf_op jit(solution)/shard_map/ppermute | solution.py:30
  116.7 11.4 %collective-permute-start.26 = (bf16[2,128,256]{2,1,0:T(8,128)(2,1)S(1)}, bf16[2,128,256]{2,1,0:T(8,128)(2,1)S(1)}, u32[]{:S(2)}, u32[]{:S(2)}) collective-permute-start(bf16[2,128,256]{2,1,0:T(8,128)(2,1)S(1)} %maximum_bitcast_fusion), channel_id=1, source_target_pairs={{0,96},{1,25},{2,98},{3,27},{4,100},{5,29},{6,102},{7,31},{8,104},... | collective-permute-start | bytes 393224 | tf_op jit(solution)/shard_map/ppermute | solution.py:30
  117.4 12.3 %collective-permute-start.25 = (bf16[2,128,256]{2,1,0:T(8,128)(2,1)S(1)}, bf16[2,128,256]{2,1,0:T(8,128)(2,1)S(1)}, u32[]{:S(2)}, u32[]{:S(2)}) collective-permute-start(bf16[2,128,256]{2,1,0:T(8,128)(2,1)S(1)} %maximum_bitcast_fusion.1), channel_id=1, source_target_pairs={{0,32},{1,9},{2,34},{3,11},{4,36},{5,13},{6,38},{7,15},{8,40},{9,1... | collective-permute-start | bytes 393224 | tf_op jit(solution)/shard_map/ppermute | solution.py:30
  119.8 9.9 %collective-permute-start.24 = (bf16[2,128,256]{2,1,0:T(8,128)(2,1)S(1)}, bf16[2,128,256]{2,1,0:T(8,128)(2,1)S(1)}, u32[]{:S(2)}, u32[]{:S(2)}) collective-permute-start(bf16[2,128,256]{2,1,0:T(8,128)(2,1)S(1)} %maximum_bitcast_fusion.2), channel_id=1, source_target_pairs={{0,64},{1,17},{2,66},{3,19},{4,68},{5,21},{6,70},{7,23},{8,72},{9,... | collective-permute-start | bytes 393224 | tf_op jit(solution)/shard_map/ppermute | solution.py:30
  126.9 5.0 %collective-permute-start.31 = (bf16[2,128,256]{2,1,0:T(8,128)(2,1)S(1)}, bf16[2,128,256]{2,1,0:T(8,128)(2,1)S(1)}, u32[]{:S(2)}, u32[]{:S(2)}) collective-permute-start(bf16[2,128,256]{2,1,0:T(8,128)(2,1)S(1)} %get-tuple-element.46), channel_id=1, source_target_pairs={{0,8},{1,33},{2,10},{3,35},{4,12},{5,37},{6,14},{7,39},{8,16},{9,4... | collective-permute-start | bytes 393224 | tf_op jit(solution)/shard_map/ppermute | solution.py:30
  128.0 5.4 %collective-permute-start.30 = (bf16[2,128,256]{2,1,0:T(8,128)(2,1)S(1)}, bf16[2,128,256]{2,1,0:T(8,128)(2,1)S(1)}, u32[]{:S(2)}, u32[]{:S(2)}) collective-permute-start(bf16[2,128,256]{2,1,0:T(8,128)(2,1)S(1)} %get-tuple-element.44), channel_id=1, source_target_pairs={{0,16},{1,65},{2,18},{3,67},{4,20},{5,69},{6,22},{7,71},{8,24},{9,... | collective-permute-start | bytes 393224 | tf_op jit(solution)/shard_map/ppermute | solution.py:30
  133.6 8.7 %collective-permute-start.33 = (bf16[256,256]{1,0:T(8,128)(2,1)S(1)}, bf16[256,256]{1,0:T(8,128)(2,1)S(1)}, u32[]{:S(2)}, u32[]{:S(2)}) collective-permute-start(bf16[256,256]{1,0:T(8,128)(2,1)S(1)} %bitcast.185), channel_id=1, source_target_pairs={{0,6},{1,7},{2,0},{3,1},{4,2},{5,3},{6,4},{7,5},{8,14},{9,15},{10,... | collective-permute-start | bytes 393224 | tf_op jit(solution)/shard_map/ppermute | solution.py:30
  138.9 5.4 %collective-permute-start.34 = (bf16[256,256]{1,0:T(8,128)(2,1)S(1)}, bf16[256,256]{1,0:T(8,128)(2,1)S(1)}, u32[]{:S(2)}, u32[]{:S(2)}) collective-permute-start(bf16[256,256]{1,0:T(8,128)(2,1)S(1)} %bitcast.186), channel_id=1, source_target_pairs={{0,4},{1,5},{2,6},{3,7},{4,0},{5,1},{6,2},{7,3},{8,12},{9,13},{10,... | collective-permute-start | bytes 393224 | tf_op jit(solution)/shard_map/ppermute | solution.py:30
  138.9 6.4 %collective-permute-start.35 = (bf16[256,256]{1,0:T(8,128)(2,1)S(1)}, bf16[256,256]{1,0:T(8,128)(2,1)S(1)}, u32[]{:S(2)}, u32[]{:S(2)}) collective-permute-start(bf16[256,256]{1,0:T(8,128)(2,1)S(1)} %bitcast.187), channel_id=1, source_target_pairs={{0,2},{1,3},{2,4},{3,5},{4,6},{5,7},{6,0},{7,1},{8,10},{9,11},{10,... | collective-permute-start | bytes 393224 | tf_op jit(solution)/shard_map/ppermute | solution.py:30
  156.7 7.6 %collective-permute-start.36 = (bf16[2,128,256]{2,1,0:T(8,128)(2,1)S(1)}, bf16[2,128,256]{2,1,0:T(8,128)(2,1)S(1)}, u32[]{:S(2)}, u32[]{:S(2)}) collective-permute-start(bf16[2,128,256]{2,1,0:T(8,128)(2,1)S(1)} %get-tuple-element.17), channel_id=1, source_target_pairs={{0,24},{1,97},{2,26},{3,99},{4,28},{5,101},{6,30},{7,103},{8,0},{9... | collective-permute-start | bytes 393224 | tf_op jit(solution)/shard_map/ppermute | solution.py:30
  160.9 5.4 %collective-permute-start.37 = (bf16[2,128,256]{2,1,0:T(8,128)(2,1)S(1)}, bf16[2,128,256]{2,1,0:T(8,128)(2,1)S(1)}, u32[]{:S(2)}, u32[]{:S(2)}) collective-permute-start(bf16[2,128,256]{2,1,0:T(8,128)(2,1)S(1)} %get-tuple-element.17), channel_id=1, source_target_pairs={{0,16},{1,65},{2,18},{3,67},{4,20},{5,69},{6,22},{7,71},{8,24},{9,... | collective-permute-start | bytes 393224 | tf_op jit(solution)/shard_map/ppermute | solution.py:30
  160.9 6.7 %collective-permute-start.38 = (bf16[2,128,256]{2,1,0:T(8,128)(2,1)S(1)}, bf16[2,128,256]{2,1,0:T(8,128)(2,1)S(1)}, u32[]{:S(2)}, u32[]{:S(2)}) collective-permute-start(bf16[2,128,256]{2,1,0:T(8,128)(2,1)S(1)} %get-tuple-element.17), channel_id=1, source_target_pairs={{0,8},{1,33},{2,10},{3,35},{4,12},{5,37},{6,14},{7,39},{8,16},{9,4... | collective-permute-start | bytes 393224 | tf_op jit(solution)/shard_map/ppermute | solution.py:30
  161.6 6.3 %collective-permute-start.39 = (bf16[2,128,256]{2,1,0:T(8,128)(2,1)S(1)}, bf16[2,128,256]{2,1,0:T(8,128)(2,1)S(1)}, u32[]{:S(2)}, u32[]{:S(2)}) collective-permute-start(bf16[2,128,256]{2,1,0:T(8,128)(2,1)S(1)} %get-tuple-element.17), channel_id=1, source_target_pairs={{0,96},{1,25},{2,98},{3,27},{4,100},{5,29},{6,102},{7,31},{8,104},... | collective-permute-start | bytes 393224 | tf_op jit(solution)/shard_map/ppermute | solution.py:30
  161.6 12.8 %collective-permute-start.41 = (bf16[2,128,256]{2,1,0:T(8,128)(2,1)S(1)}, bf16[2,128,256]{2,1,0:T(8,128)(2,1)S(1)}, u32[]{:S(2)}, u32[]{:S(2)}) collective-permute-start(bf16[2,128,256]{2,1,0:T(8,128)(2,1)S(1)} %get-tuple-element.17), channel_id=1, source_target_pairs={{0,64},{1,17},{2,66},{3,19},{4,68},{5,21},{6,70},{7,23},{8,72},{9,... | collective-permute-start | bytes 393224 | tf_op jit(solution)/shard_map/ppermute | solution.py:30
  164.2 11.9 %collective-permute-start.43 = (bf16[2,128,256]{2,1,0:T(8,128)(2,1)S(1)}, bf16[2,128,256]{2,1,0:T(8,128)(2,1)S(1)}, u32[]{:S(2)}, u32[]{:S(2)}) collective-permute-start(bf16[2,128,256]{2,1,0:T(8,128)(2,1)S(1)} %get-tuple-element.17), channel_id=1, source_target_pairs={{0,32},{1,9},{2,34},{3,11},{4,36},{5,13},{6,38},{7,15},{8,40},{9,1... | collective-permute-start | bytes 393224 | tf_op jit(solution)/shard_map/ppermute | solution.py:30
  167.7 6.7 %collective-permute-start.40 = (bf16[3,2,128,256]{3,2,1,0:T(8,128)(2,1)S(1)}, bf16[3,2,128,256]{3,2,1,0:T(8,128)(2,1)S(1)}, u32[]{:S(2)}, u32[]{:S(2)}) collective-permute-start(bf16[3,2,128,256]{3,2,1,0:T(8,128)(2,1)S(1)} %pad_maximum_fusion.9), channel_id=1, source_target_pairs={{0,96},{1,25},{2,98},{3,27},{4,100},{5,29},{6,102},{7,31},{8,104},... | collective-permute-start | bytes 1179656 | tf_op jit(solution)/shard_map/ppermute | solution.py:30
  167.8 8.3 %collective-permute-start.42 = (bf16[3,2,128,256]{3,2,1,0:T(8,128)(2,1)S(1)}, bf16[3,2,128,256]{3,2,1,0:T(8,128)(2,1)S(1)}, u32[]{:S(2)}, u32[]{:S(2)}) collective-permute-start(bf16[3,2,128,256]{3,2,1,0:T(8,128)(2,1)S(1)} %pad_maximum_fusion.9), channel_id=1, source_target_pairs={{0,64},{1,17},{2,66},{3,19},{4,68},{5,21},{6,70},{7,23},{8,72},{9,... | collective-permute-start | bytes 1179656 | tf_op jit(solution)/shard_map/ppermute | solution.py:30
  168.0 12.6 %collective-permute-start.44 = (bf16[3,2,128,256]{3,2,1,0:T(8,128)(2,1)S(1)}, bf16[3,2,128,256]{3,2,1,0:T(8,128)(2,1)S(1)}, u32[]{:S(2)}, u32[]{:S(2)}) collective-permute-start(bf16[3,2,128,256]{3,2,1,0:T(8,128)(2,1)S(1)} %pad_maximum_fusion.9), channel_id=1, source_target_pairs={{0,32},{1,9},{2,34},{3,11},{4,36},{5,13},{6,38},{7,15},{8,40},{9,1... | collective-permute-start | bytes 1179656 | tf_op jit(solution)/shard_map/ppermute | solution.py:30
  180.8 9.3 %collective-permute-start.45 = (bf16[16,128,256]{2,1,0:T(8,128)(2,1)S(1)}, bf16[16,128,256]{2,1,0:T(8,128)(2,1)S(1)}, u32[]{:S(2)}, u32[]{:S(2)}) collective-permute-start(bf16[16,128,256]{2,1,0:T(8,128)(2,1)S(1)} %get-tuple-element.24), channel_id=1, source_target_pairs={{0,1},{1,0},{2,3},{3,2},{4,5},{5,4},{6,7},{7,6},{8,9},{9,8},{10,11... | collective-permute-start | bytes 3145736 | tf_op jit(solution)/shard_map/ppermute | solution.py:30
  201.6 5.6 %collective-permute-start.49 = (f32[8]{0:T(128)S(1)}, f32[8]{0:T(128)S(1)}, u32[]{:S(2)}, u32[]{:S(2)}) collective-permute-start(f32[8]{0:T(128)S(1)} %add.181), channel_id=1, source_target_pairs={{0,6},{1,7},{2,0},{3,1},{4,2},{5,3},{6,4},{7,5},{8,14},{9,15},{10,... | collective-permute-start | bytes 104 | tf_op jit(solution)/shard_map/ppermute | solution.py:30
  206.4 3.9 %collective-permute-start.48 = (f32[8]{0:T(128)S(1)}, f32[8]{0:T(128)S(1)}, u32[]{:S(2)}, u32[]{:S(2)}) collective-permute-start(f32[8]{0:T(128)S(1)} %add.181), channel_id=1, source_target_pairs={{0,4},{1,5},{2,6},{3,7},{4,0},{5,1},{6,2},{7,3},{8,12},{9,13},{10,... | collective-permute-start | bytes 104 | tf_op jit(solution)/shard_map/ppermute | solution.py:30
  211.3 3.9 %collective-permute-start.50 = (f32[8]{0:T(128)S(1)}, f32[8]{0:T(128)S(1)}, u32[]{:S(2)}, u32[]{:S(2)}) collective-permute-start(f32[8]{0:T(128)S(1)} %add_add_fusion.2), channel_id=1, source_target_pairs={{0,8},{1,33},{2,10},{3,35},{4,12},{5,37},{6,14},{7,39},{8,16},{9,4... | collective-permute-start | bytes 104 | tf_op jit(solution)/shard_map/ppermute | solution.py:30
  215.3 4.0 %collective-permute-start.54 = (f32[8]{0:T(128)S(1)}, f32[8]{0:T(128)S(1)}, u32[]{:S(2)}, u32[]{:S(2)}) collective-permute-start(f32[8]{0:T(128)S(1)} %add_add_fusion.1), channel_id=1, source_target_pairs={{0,64},{1,17},{2,66},{3,19},{4,68},{5,21},{6,70},{7,23},{8,72},{9,... | collective-permute-start | bytes 104 | tf_op jit(solution)/shard_map/ppermute | solution.py:30
  215.4 4.7 %collective-permute-start.53 = (f32[8]{0:T(128)S(1)}, f32[8]{0:T(128)S(1)}, u32[]{:S(2)}, u32[]{:S(2)}) collective-permute-start(f32[8]{0:T(128)S(1)} %add_add_fusion.1), channel_id=1, source_target_pairs={{0,32},{1,9},{2,34},{3,11},{4,36},{5,13},{6,38},{7,15},{8,40},{9,1... | collective-permute-start | bytes 104 | tf_op jit(solution)/shard_map/ppermute | solution.py:30
  (19 other events, 385.5 us)

commit v2 on v1

v2 whole, which is shorter than its diff:
```python
import math

import jax
import jax.numpy as jnp
import numpy as np
from jax import lax
from jax.experimental import pallas as pl
from jax.experimental.pallas import tpu as pltpu
from jax.sharding import PartitionSpec as P

NT = 1024
F = 32
AXES = ("rcv", "freq")
BF = jnp.bfloat16
F32 = jnp.float32
VMEM = pl.BlockSpec(memory_space=pltpu.VMEM)
HBM = pl.BlockSpec(memory_space=pltpu.HBM)
CC = 16
SMEM = pl.BlockSpec(memory_space=pltpu.SMEM)
NT_DIMS = (((1,), (1,)), ((), ()))


def index(y, x, z, c):
    return (y * 4 + x) * 8 + z * 2 + c


DEVICES = [(y, x, z, c) for y in range(4) for x in range(4) for z in range(4) for c in range(2)]


def move(value, target):
    pairs = [(index(*d), index(*target(*d))) for d in DEVICES]
    return lax.ppermute(value, AXES, pairs)


def along_big(step):
    def target(y, x, z, c):
        return ((y + step) % 4, x, z, c) if c == 0 else (y, (x + step) % 4, z, c)

    return target


def along_small(step):
    def target(y, x, z, c):
        return (y, (x + step) % 4, z, c) if c == 0 else ((y + step) % 4, x, z, c)

    return target


def along_z(step):
    return lambda y, x, z, c: (y, x, (z + step) % 4, c)


def other_core(y, x, z, c):
    return (y, x, z, 1 - c)


def window_matrix():
    bins = np.arange(1, F + 1)
    theta = 2.0 * np.pi / NT

    def ratio(k):
        half = theta * k / 2.0
        safe = np.where(k == 0, 1.0, half)
        return np.where(k == 0, 0.0, 0.5 - 0.5j / np.tan(safe))

    direct = ratio(bins[:, None] - bins[None, :]) / NT
    mirror = ratio(bins[:, None] + bins[None, :]) / NT
    top = np.concatenate([direct.real + mirror.real, -direct.imag + mirror.imag], axis=1)
    low = np.concatenate([direct.imag + mirror.imag, direct.real - mirror.real], axis=1)
    return np.concatenate([top, low], axis=0).astype(np.float32)


def cost(flops):
    return pl.CostEstimate(flops=flops, bytes_accessed=4 << 20, transcendentals=0)


def params(mib):
    return pltpu.CompilerParams(vmem_limit_bytes=mib << 20)


def swapped(v, sign):
    rows = []
    for k in range(0, 64, 32):
        rows += [sign * v[k + 16 : k + 32], -sign * v[k : k + 16]]
    return jnp.concatenate(rows, axis=0)


def terms(kb, f, u, j_ref, k_ref, out_ref):
    v = swapped(u, 1)
    for ks in range(4):
        cols = pl.ds(pl.multiple_of(j_ref[kb * 4 + ks] * 256, 256), 256)
        r = jnp.dot(u, k_ref[0, f, :, cols], preferred_element_type=F32)
        r = r + jnp.dot(v, k_ref[1, f, :, cols], preferred_element_type=F32)
        out_ref[ks, f] = r.astype(BF)


def first_kernel(place_ref, j_ref, data_hbm, k_hbm, k_ref, *refs):
    out_refs, (data_ref, sem, sems) = refs[:4], refs[4:]
    core = place_ref[1]
    fetch = pltpu.make_async_copy(data_hbm, data_ref, sem)
    fetch.start()
    copies = [
        [pltpu.make_async_copy(k_hbm.at[p, f], k_ref.at[p, f], sems.at[p, f]) for p in range(2)]
        for f in range(4)
    ]
    for f in range(2):
        for p in range(2):
            copies[f][p].start()
    fetch.wait()
    for f in range(4):
        rows = []
        for half in range(2):
            at = pl.ds(pl.multiple_of((half + core - 2 * half * core) * 16, 16), 16)
            rows += [data_ref[0, f, at, :], data_ref[1, f, at, :]]
        u = jnp.concatenate(rows, axis=0).astype(BF)
        for p in range(2):
            copies[f][p].wait()
            if f < 2:
                copies[f + 2][p].start()
        for kb in range(4):
            terms(kb, f, u, j_ref, k_ref, out_refs[kb])


TERMS = jax.ShapeDtypeStruct((4, 4, 64, 256), BF)


def first_adjoint(place, table, data, kernel):
    return pl.pallas_call(
        first_kernel,
        in_specs=[SMEM, SMEM, HBM, HBM],
        out_specs=[VMEM] * 5,
        out_shape=[pltpu.VMEM(kernel.shape, BF)] + [TERMS] * 4,
        scratch_shapes=[
            pltpu.VMEM(data.shape, F32),
            pltpu.SemaphoreType.DMA,
            pltpu.SemaphoreType.DMA((2, 4)),
        ],
        compiler_params=params(8),
        cost_estimate=cost(4 << 30),
        name="first_adjoint",
    )(
        place,
        table,
        pltpu.with_memory_space_constraint(data, pltpu.HBM),
        pltpu.with_memory_space_constraint(kernel, pltpu.HBM),
    )


def adjoint_kernel(kbs, j_ref, u_ref, k_ref, *out_refs):
    for f in range(4):
        u = u_ref[f].astype(BF)
        for kb, out_ref in zip(kbs, out_refs):
            terms(kb, f, u, j_ref, k_ref, out_ref)


def adjoint(table, u, kernel, kbs):
    return pl.pallas_call(
        lambda *refs: adjoint_kernel(kbs, *refs),
        in_specs=[SMEM, VMEM, VMEM],
        out_specs=[VMEM] * len(kbs),
        out_shape=[TERMS] * len(kbs),
        compiler_params=params(8),
        cost_estimate=cost(len(kbs) << 33),
        name="adjoint",
    )(table, u, kernel)


def fold(v):
    v = jnp.sum(v, axis=0, keepdims=True)
    return v[:, :128] + v[:, 128:]


def forward_kernel(kb, last, second, j_ref, x_ref, k_ref, *refs):
    if kb > 0:
        before_ref, *refs = refs
    if second:
        i0_ref, gg_ref, hh_ref, ii_ref, *refs = refs
    out_ref = refs[0]

    zero = jnp.zeros((1, 128), F32)
    sums = [zero, zero]
    for f in range(4):
        acc = jnp.zeros((256, 64), F32)
        for ks in range(4):
            cols = pl.ds(pl.multiple_of(j_ref[kb * 4 + ks] * 256, 256), 256)
            x = x_ref[ks, f]
            acc = acc + lax.dot_general(
                k_ref[0, f, :, cols], x, NT_DIMS, preferred_element_type=F32
            )
            acc = acc + lax.dot_general(
                k_ref[1, f, :, cols], swapped(x, -1), NT_DIMS, preferred_element_type=F32
            )
        out = acc.T
        if kb > 0:
            out = out + before_ref[f]
        out_ref[f] = out
        if second:
            sums[0] = sums[0] + fold(i0_ref[f] * out)
        if last:
            sums[1] = sums[1] + fold(out * out)
    if second:
        rows = [gg_ref[0:1], hh_ref[0:2], ii_ref[0:1], *sums, zero, zero]
        refs[1][...] = jnp.concatenate(rows, axis=0)
    elif last:
        refs[1][...] = jnp.broadcast_to(sums[1], (8, 128))


def forward(kb, table, blocks, kernel, before=None, last=False, more=()):
    inputs = (blocks, kernel) + (() if before is None else (before,)) + tuple(more)
    out = [jax.ShapeDtypeStruct((4, 64, 256), F32)]
    if last:
        out.append(jax.ShapeDtypeStruct((8, 128), F32))
    return pl.pallas_call(
        lambda *refs: forward_kernel(kb, last, len(more) > 0, *refs),
        in_specs=[SMEM] + [VMEM] * len(inputs),
        out_specs=[VMEM] * len(out),
        out_shape=out,
        compiler_params=params(8),
        cost_estimate=cost(1 << 33),
        name="forward",
    )(table, *inputs)


def parts_of(x):
    high = x.astype(BF)
    low = (x - high.astype(F32)).astype(BF)
    return jnp.concatenate([high, high, low], axis=0)


def window_kernel(second, place_ref, a0, a1, a2, a3, m_ref, mo_ref, cos_ref, sin_ref, n_ref, *refs):
    if second:
        g0_ref, g_ref, s_ref, sum_ref, y, g, s = refs
    else:
        g_ref, s_ref, sum_ref, y, g, s = refs
    z = place_ref[0]
    core = place_ref[1]

    size = 8 * CC

    def swap(half):
        return half + core - 2 * half * core

    for k, a in enumerate((a0, a1, a2, a3)):
        for half in range(2):
            at = (lax.rem(z + k, 4) * 2 + swap(half)) * size
            rows = pl.ds(pl.multiple_of(at, size), size)
            part = a[pl.ds(half * size, size), :].astype(F32)
            y[0, rows, :] = part[:, :128]
            y[1, rows, :] = part[:, 128:]

    cos = cos_ref[...]
    sin = sin_ref[...]
    share = n_ref[...]
    eight = pl.ds(pl.multiple_of(z * 8, 8), 8)
    cos_own = cos_ref[eight, :]
    sin_own = sin_ref[eight, :]

    def take(ref, first, count):
        rows = pl.ds(first, count, stride=2 * CC)
        return jnp.concatenate([ref[0, rows, :], ref[1, rows, :]], axis=1)

    def put(ref, first, value):
        rows = pl.ds(first, value.shape[0], stride=2 * CC)
        ref[0, rows, :] = value[:, :128]
        ref[1, rows, :] = value[:, 128:]

    def products(matrix, pairs):
        columns = []
        for re, im in pairs:
            columns.append(parts_of(jnp.concatenate([re, im], axis=0)))
            turned = jnp.concatenate([cos * re - sin * im, sin * re + cos * im], axis=0)
            columns.append(parts_of(turned))
        return jnp.dot(matrix, jnp.concatenate(columns, axis=1), preferred_element_type=F32)

    def combine(re, im, both, at, c, d):
        n = re.shape[0]
        plain = both[:, at * 512 : at * 512 + 256]
        w = both[:, at * 512 + 256 : at * 512 + 512]
        out_re = share * re + plain[:n] - c * w[:n] - d * w[n:]
        out_im = share * im + plain[n:] - c * w[n:] + d * w[:n]
        return out_re, out_im

    def four(step, carry):
        first = step * 4
        pairs = [(take(y, first + i, F), take(y, first + i + CC, F)) for i in range(4)]
        both = products(m_ref[...], pairs)
        grads = []
        for i, (re, im) in enumerate(pairs):
            re, im = combine(re, im, both, i, cos, sin)
            put(g, first + i, re)
            put(g, first + i + CC, im)
            grads.append((re, im))
        both = products(mo_ref[z], grads)
        for i in range(4):
            re = take(g, z * 2 * size + first + i, 8)
            im = take(g, z * 2 * size + first + i + CC, 8)
            re, im = combine(re, im, both, i, cos_own, sin_own)
            put(s, first + i, re)
            put(s, first + i + CC, im)
        return carry

    lax.fori_loop(0, CC // 4, four, 0)
    sums = [jnp.zeros((1, 128), F32)] * 2
    for half in range(2):
        rows = pl.ds(pl.multiple_of((z * 2 + swap(half)) * size, size), size)
        value = jnp.concatenate([g[0, rows, :], g[1, rows, :]], axis=1)
        g_ref[half] = value
        if second:
            sums = [sums[0] + fold(g0_ref[half] * value), sums[1] + fold(value * value)]
        else:
            sums = [sums[0] + fold(value * value), sums[1]]
        rows = pl.ds(pl.multiple_of(swap(half) * size, size), size)
        s_ref[half] = jnp.concatenate([s[0, rows, :], s[1, rows, :]], axis=1).astype(BF)
    sum_ref[...] = jnp.concatenate(sums + [jnp.zeros((6, 128), F32)], axis=0)


def window(place, blocks, constants, *more):
    return pl.pallas_call(
        lambda *refs: window_kernel(len(more) > 0, *refs),
        in_specs=[SMEM] + [VMEM] * (9 + len(more)),
        out_specs=[VMEM, VMEM, VMEM],
        out_shape=[
            jax.ShapeDtypeStruct((2, 8 * CC, 256), F32),
            jax.ShapeDtypeStruct((2, 8 * CC, 256), BF),
            jax.ShapeDtypeStruct((8, 128), F32),
        ],
        scratch_shapes=[pltpu.VMEM((2, 64 * CC, 128), F32)] * 2
        + [pltpu.VMEM((2, 16 * CC, 128), F32)],
        compiler_params=params(12),
        cost_estimate=cost(1 << 30),
        name="window",
    )(place, *blocks, *constants, *more)


def last_kernel(place_ref, sum_ref, i0, i1, data_ref, g0, g0_got, h, h_got, model_ref, res_ref):
    core = place_ref[1]
    sums = jnp.sum(sum_ref[...], axis=1, keepdims=True)
    gg, gh, hh, ii, ij, jj = [sums[k : k + 1] for k in range(6)]
    alpha0 = gg / ii
    fresh = gg - 2.0 * alpha0 * gh + alpha0 * alpha0 * hh
    stay = 1.0 + fresh / gg
    delta = stay * stay * ii - 2.0 * stay * alpha0 * ij + alpha0 * alpha0 * jj
    alpha1 = fresh / delta
    on_first = alpha0 + alpha1 * stay
    on_second = alpha1 * alpha0
    for half in range(2):
        at = pl.ds(pl.multiple_of((half + core - 2 * half * core) * 16, 16), 16)
        for f in range(4):
            for p in range(2):
                rows = slice(f * 32 + p * 16, f * 32 + p * 16 + 16)
                left = g0[0, rows, :] if half == 0 else g0_got[rows, :]
                right = h[0, rows, :] if half == 0 else h_got[rows, :]
                model_ref[p, f, at, :] = on_first * left - on_second * right
                rows = slice(half * 32 + p * 16, half * 32 + p * 16 + 16)
                change = on_first * i0[f, rows, :] - on_second * i1[f, rows, :]
                res_ref[p, f, at, :] = data_ref[p, f, at, :] - change


def last(place, *arrays):
    shape = jax.ShapeDtypeStruct((2, 4, 32, 256), F32)
    return pl.pallas_call(
        last_kernel,
        in_specs=[SMEM] + [VMEM] * len(arrays),
        out_specs=[VMEM, VMEM],
        out_shape=[shape, shape],
        compiler_params=params(8),
        cost_estimate=cost(1 << 20),
        name="last",
    )(place, *arrays)


def total(values):
    values = values + move(values, other_core)
    for axis in (along_z, along_small, along_big):
        values = values + move(values, axis(1)) + move(values, axis(2)) + move(values, axis(3))
    return values


def body(kernel, data, cutoffs):
    rcv = lax.axis_index("rcv")
    freq = lax.axis_index("freq")
    yy, xx, zz, core = rcv // 4, rcv % 4, freq // 2, freq % 2
    place = jnp.stack([zz, core]).astype(jnp.int32)
    far = jnp.arange(16, dtype=jnp.int32) // 4
    near = jnp.arange(16, dtype=jnp.int32) % 4
    off_y = jnp.where(core == 0, far, near)
    off_x = jnp.where(core == 0, near, far)
    table = (yy + off_y) % 4 * 4 + (xx + off_x) % 4

    matrix = window_matrix()
    high = matrix.astype(jnp.bfloat16)
    low = (matrix - high.astype(np.float32)).astype(jnp.bfloat16)
    stacked = jnp.asarray(np.concatenate([high, low, high], axis=1))
    own_rows = stacked.reshape(2, 4, 8, 192).swapaxes(0, 1).reshape(4, 16, 192)
    bins = jnp.arange(1, F + 1, dtype=jnp.int32)
    phase = (bins[:, None] * cutoffs[None, :] % NT).astype(F32) * (2.0 * math.pi / NT)
    share = (cutoffs.astype(F32) / NT)[None, :]
    constants = (stacked, own_rows, jnp.cos(phase), jnp.sin(phase), share)

    def summed(parts):
        out = parts[0].astype(F32)
        for part in parts[1:]:
            out = out + part.astype(F32)
        return out.astype(BF)

    def gather_terms(own):
        got = [move(own[kb], along_big(kb)) for kb in (2, 1, 3)]
        row = [summed([own[0][ks]] + [part[ks] for part in got]) for ks in range(4)]
        mine = summed([row[0]] + [move(row[ks], along_small(ks)) for ks in (2, 1, 3)])
        mine = mine.reshape(4, 2, 32, 256)
        mine = jnp.stack([mine[:, 0], move(mine[:, 1], other_core)]).reshape(256, 256)
        return [mine] + [move(mine, along_z(-k)) for k in (1, 2, 3)]

    def image_of(shaped, *more):
        shaped = shaped.reshape(2, 4, 32, 256)
        shaped = jnp.stack([shaped[0], move(shaped[1], other_core)], axis=1).reshape(4, 64, 256)
        row = jnp.stack([shaped] + [move(shaped, along_small(-ks)) for ks in (1, 2, 3)])
        near = {kb: move(row, along_big(-kb)) for kb in (1, 3)}
        (out,) = forward(0, table, row, held)
        row, out = lax.optimization_barrier((row, out))
        far = move(row, along_big(-2))
        for kb in (1, 3):
            (out,) = forward(kb, table, near[kb], held, out)
        return forward(2, table, far, held, out, True, more)

    start = jnp.swapaxes(data, 2, 3)
    held, *own = first_adjoint(place, table, start, kernel)
    held = pltpu.with_memory_space_constraint(held, pltpu.VMEM)
    g0, s0, gg = window(place, gather_terms(own), constants)
    i0, ii = image_of(s0)
    far = adjoint(table, i0, held, (2,))
    rest = adjoint(table, i0, held, (0, 1, 3))
    h, s1, hh = window(place, gather_terms([*rest[:2], far[0], rest[2]]), constants, g0)
    i1, sums = image_of(s1, i0, gg, hh, ii)
    g0_got = move(g0[1], other_core)
    h_got = move(h[1], other_core)
    model, residual = last(place, total(sums), i0, i1, start, g0, g0_got, h, h_got)
    return jnp.swapaxes(model, 2, 3), jnp.swapaxes(residual, 2, 3)


def solution(mesh):
    placed = P(None, "freq", "rcv", None)
    return jax.shard_map(
        body,
        mesh=mesh,
        in_specs=(placed, placed, P("rcv")),
        out_specs=(placed, placed),
        check_vma=False,
    )
```

time: 232 us -> 186 us (0.80); the launches traced: 228 us -> 185 us
  local copies, waits for them, and re-layouts: 17.9 us -> 0.09 us
  starting transfers between devices: 73.1 us -> 61.8 us
  Pallas kernels: 42.1 us -> 35.2 us
  between operations: 7.06 us -> 0.95 us
  other arithmetic: 4.72 us -> 1.27 us
    unnamed x36 -> x8, local copies, waits for them, and re-layouts: 11.8 us -> 0.02 us
    ppermute x58 -> x46, starting transfers between devices: 73.1 us -> 61.8 us  [move(): return lax.ppermute(value, AXES, pairs)]
    pallas_call x6 -> x14, Pallas kernels: 42.1 us -> 35.2 us  [the longest x8 14.8 us: forward(): pl.pallas_call(lambda *refs: forward_kernel(kb, last, len(more) > 0, *ref...]
    another operation x2, local copies, waits for them, and re-layouts: 3.85 us -> 0.02 us  [gather_terms(): jnp.stack([mine[:, 0], move(mine[:, 1], other_core)]).reshape(256, 256)]
    ppermute x58 -> x46, waiting for transfers between devices: 83.2 us -> 85.3 us  [move(): return lax.ppermute(value, AXES, pairs)]
  transfers between devices with their start and end apart: 58 -> 46, of which waited for: 40 -> 33; matrix products, arithmetic and copies ran while one was open for 1% -> 0% of each run, Pallas kernels for 0% -> 6%
where the time goes in v2:
time: 186 us; the launch traced here: 185 us
  waiting for transfers between devices  85.3 us (46%)
  starting transfers between devices  61.8 us (33%)
  Pallas kernels  35.2 us (19%)
    ppermute x46, waiting for transfers between devices, move(): return lax.ppermute(value, AXES, pairs)  85.3 us
    ppermute x46, starting transfers between devices, move(): return lax.ppermute(value, AXES, pairs)  61.8 us
    pallas_call x8, Pallas kernels, forward(): pl.pallas_call(lambda *refs: forward_kernel(kb, last, len(more) > 0, *ref...  14.8 us
    pallas_call x1, Pallas kernels, first_adjoint(): pl.pallas_call(first_kernel, in_specs=[SMEM, SMEM, HBM, HBM], out_specs=[...  7.86 us
    pallas_call x2, Pallas kernels, window(): pl.pallas_call(lambda *refs: window_kernel(len(more) > 0, *refs), in_spec...  6.75 us
    pallas_call x2, Pallas kernels, adjoint(): pl.pallas_call(lambda *refs: adjoint_kernel(kbs, *refs), in_specs=[SMEM,...  4.25 us
  transfers between devices with their start and end apart: 46, of which 33 were waited for; matrix products, arithmetic and copies ran while one was open for 0% of the time, Pallas kernels for 6%

profile of v2, /device:TPU:1, one launch (start us, length us, event | category | flops | bytes accessed | tf_op | source)
XLA Modules:
  0.0 184.7 jit_solution(923036934832234486)
XLA Ops:
  0.8 7.9 %first_adjoint.1 = (bf16[2,4,256,4096]{3,2,1,0:T(8,128)(2,1)S(1)}, bf16[4,4,64,256]{3,2,1,0:T(8,128)(2,1)S(1)}, bf16[4,4,64,256]{3,2,1,0:T(8,128)(2,1)S(1)}, bf1...) custom-call(s32[2]{0:T(128)S(1)} %pad_add_fusion.place_ref.refs_0_, s32[16]{0:T(128)S(1)} %fusion.19.j_ref.refs_0_, ...), custom_call_target="tpu_custom_call" | custom-call | flops 4294967296 | bytes 4194304 | tf_op jit(solution)/shard_map/first_adjoint/pallas_call | solution.py:128
  8.7 3.7 %collective-permute-start = (bf16[4,4,64,256]{3,2,1,0:T(8,128)(2,1)S(1)}, bf16[4,4,64,256]{3,2,1,0:T(8,128)(2,1)S(1)}, u32[]{:S(2)}, u32[]{:S(2)}) collective-permute-start(bf16[4,4,64,256]{3,2,1,0:T(8,128)(2,1)S(1)} %get-tuple-element.27), channel_id=1, source_target_pairs={{0,64},{1,17},{2,66},{3,19},{4,68},{5,21},{6,70},{7,23},{8,72},{9,... | collective-permute-start | bytes 1572872 | tf_op jit(solution)/shard_map/ppermute | solution.py:32
  12.6 2.4 %collective-permute-start.2 = (bf16[4,4,64,256]{3,2,1,0:T(8,128)(2,1)S(1)}, bf16[4,4,64,256]{3,2,1,0:T(8,128)(2,1)S(1)}, u32[]{:S(2)}, u32[]{:S(2)}) collective-permute-start(bf16[4,4,64,256]{3,2,1,0:T(8,128)(2,1)S(1)} %get-tuple-element.29), channel_id=1, source_target_pairs={{0,96},{1,25},{2,98},{3,27},{4,100},{5,29},{6,102},{7,31},{8,104},... | collective-permute-start | bytes 1572872 | tf_op jit(solution)/shard_map/ppermute | solution.py:32
  15.0 4.2 %collective-permute-done = bf16[4,4,64,256]{3,2,1,0:T(8,128)(2,1)S(1)} collective-permute-done((bf16[4,4,64,256]{3,2,1,0:T(8,128)(2,1)S(1)}, bf16[4,4,64,256]{3,2,1,0:T(8,128)(2,1)S(1)}, u32[]{:S(2)}, u32[]{:S(2)}) %collective-permute-start) | collective-permute-done | bytes 524320 | tf_op jit(solution)/shard_map/ppermute | solution.py:32
  19.2 5.6 %collective-permute-done.1 = bf16[4,4,64,256]{3,2,1,0:T(8,128)(2,1)S(1)} collective-permute-done((bf16[4,4,64,256]{3,2,1,0:T(8,128)(2,1)S(1)}, bf16[4,4,64,256]{3,2,1,0:T(8,128)(2,1)S(1)}, u32[]{:S(2)}, u32[]{:S(2)}) %collective-permute-start.1) | collective-permute-done | bytes 524320 | tf_op jit(solution)/shard_map/ppermute | solution.py:32
  25.4 3.0 %collective-permute-start.3 = (bf16[4,64,256]{2,1,0:T(8,128)(2,1)S(1)}, bf16[4,64,256]{2,1,0:T(8,128)(2,1)S(1)}, u32[]{:S(2)}, u32[]{:S(2)}) collective-permute-start(bf16[4,64,256]{2,1,0:T(8,128)(2,1)S(1)} %get-tuple-element.53), channel_id=1, source_target_pairs={{0,16},{1,65},{2,18},{3,67},{4,20},{5,69},{6,22},{7,71},{8,24},{9,... | collective-permute-start | bytes 393224 | tf_op jit(solution)/shard_map/ppermute | solution.py:32
  28.8 2.3 %collective-permute-start.5 = (bf16[4,64,256]{2,1,0:T(8,128)(2,1)S(1)}, bf16[4,64,256]{2,1,0:T(8,128)(2,1)S(1)}, u32[]{:S(2)}, u32[]{:S(2)}) collective-permute-start(bf16[4,64,256]{2,1,0:T(8,128)(2,1)S(1)} %get-tuple-element.54), channel_id=1, source_target_pairs={{0,24},{1,97},{2,26},{3,99},{4,28},{5,101},{6,30},{7,103},{8,0},{9... | collective-permute-start | bytes 393224 | tf_op jit(solution)/shard_map/ppermute | solution.py:32
  31.1 2.3 %collective-permute-done.4 = bf16[4,64,256]{2,1,0:T(8,128)(2,1)S(1)} collective-permute-done((bf16[4,64,256]{2,1,0:T(8,128)(2,1)S(1)}, bf16[4,64,256]{2,1,0:T(8,128)(2,1)S(1)}, u32[]{:S(2)}, u32[]{:S(2)}) %collective-permute-start.4) | collective-permute-done | bytes 131104 | tf_op jit(solution)/shard_map/ppermute | solution.py:32
  33.6 3.1 %collective-permute-start.6 = (bf16[4,32,256]{2,1,0:T(8,128)(2,1)S(1)}, bf16[4,32,256]{2,1,0:T(8,128)(2,1)S(1)}, u32[]{:S(2)}, u32[]{:S(2)}) collective-permute-start(bf16[4,32,256]{2,1,0:T(8,128)(2,1)S(1)} %get-tuple-element.63), channel_id=1, source_target_pairs={{0,1},{1,0},{2,3},{3,2},{4,5},{5,4},{6,7},{7,6},{8,9},{9,8},{10,11... | collective-permute-start | bytes 196616 | tf_op jit(solution)/shard_map/ppermute | solution.py:32
  37.6 3.8 %collective-permute-start.7 = (bf16[256,256]{1,0:T(8,128)(2,1)S(1)}, bf16[256,256]{1,0:T(8,128)(2,1)S(1)}, u32[]{:S(2)}, u32[]{:S(2)}) collective-permute-start(bf16[256,256]{1,0:T(8,128)(2,1)S(1)} %bitcast.80), channel_id=1, source_target_pairs={{0,6},{1,7},{2,0},{3,1},{4,2},{5,3},{6,4},{7,5},{8,14},{9,15},{10,... | collective-permute-start | bytes 393224 | tf_op jit(solution)/shard_map/ppermute | solution.py:32
  42.1 4.9 %collective-permute-done.7.refs_2_ = bf16[256,256]{1,0:T(8,128)(2,1)S(1)} collective-permute-done((bf16[256,256]{1,0:T(8,128)(2,1)S(1)}, bf16[256,256]{1,0:T(8,128)(2,1)S(1)}, u32[]{:S(2)}, u32[]{:S(2)}) %collective-permute-start.7) | collective-permute-done | bytes 131104 | tf_op jit(solution)/shard_map/ppermute | solution.py:32
  47.4 3.1 %collective-permute-done.9.refs_4_ = bf16[256,256]{1,0:T(8,128)(2,1)S(1)} collective-permute-done((bf16[256,256]{1,0:T(8,128)(2,1)S(1)}, bf16[256,256]{1,0:T(8,128)(2,1)S(1)}, u32[]{:S(2)}, u32[]{:S(2)}) %collective-permute-start.9) | collective-permute-done | bytes 131104 | tf_op jit(solution)/shard_map/ppermute | solution.py:32
  50.6 3.4 %window.2 = (f32[2,128,256]{2,1,0:T(8,128)S(1)}, bf16[2,128,256]{2,1,0:T(8,128)(2,1)S(1)}, f32[8,128]{1,0:T(8,128)S(1)}) custom-call(s32[2]{0:T(128)S(1)} %pad_add_fusion.place_ref.refs_0_, bf16[256,256]{1,0:T(8,128)(2,1)S(1)} %bitcast.83, bf16[256,256]{1,0:T(8,128)(2,1)S(1)} %collective-permute-done.7.refs_2_, ...), custom_call_target="tpu_custom_call" | custom-call | flops 1073741824 | bytes 4194304 | tf_op jit(solution)/shard_map/window/pallas_call | solution.py:318
  55.8 2.4 %collective-permute-start.11 = (bf16[4,64,256]{2,1,0:T(8,128)(2,1)S(1)}, bf16[4,64,256]{2,1,0:T(8,128)(2,1)S(1)}, u32[]{:S(2)}, u32[]{:S(2)}) collective-permute-start(bf16[4,64,256]{2,1,0:T(8,128)(2,1)S(1)} %bitcast.86), channel_id=1, source_target_pairs={{0,24},{1,97},{2,26},{3,99},{4,28},{5,101},{6,30},{7,103},{8,0},{9... | collective-permute-start | bytes 393224 | tf_op jit(solution)/shard_map/ppermute | solution.py:32
  58.9 2.6 %collective-permute-done.11 = bf16[4,64,256]{2,1,0:T(8,128)(2,1)S(1)} collective-permute-done((bf16[4,64,256]{2,1,0:T(8,128)(2,1)S(1)}, bf16[4,64,256]{2,1,0:T(8,128)(2,1)S(1)}, u32[]{:S(2)}, u32[]{:S(2)}) %collective-permute-start.11) | collective-permute-done | bytes 131104 | tf_op jit(solution)/shard_map/ppermute | solution.py:32
  61.5 2.1 %collective-permute-done.12 = bf16[4,64,256]{2,1,0:T(8,128)(2,1)S(1)} collective-permute-done((bf16[4,64,256]{2,1,0:T(8,128)(2,1)S(1)}, bf16[4,64,256]{2,1,0:T(8,128)(2,1)S(1)}, u32[]{:S(2)}, u32[]{:S(2)}) %collective-permute-start.12) | collective-permute-done | bytes 131104 | tf_op jit(solution)/shard_map/ppermute | solution.py:32
  63.6 1.6 collective-permute-done.13
  65.3 2.7 %collective-permute-start.16 = (bf16[4,4,64,256]{3,2,1,0:T(8,128)(2,1)S(1)}, bf16[4,4,64,256]{3,2,1,0:T(8,128)(2,1)S(1)}, u32[]{:S(2)}, u32[]{:S(2)}) collective-permute-start(bf16[4,4,64,256]{3,2,1,0:T(8,128)(2,1)S(1)} %pad_maximum_fusion.refs_1_), channel_id=1, source_target_pairs={{0,96},{1,25},{2,98},{3,27},{4,100},{5,29},{6,102},{7,31},{8,104},... | collective-permute-start | bytes 1572872 | tf_op jit(solution)/shard_map/ppermute | solution.py:32
  68.0 1.8 forward.8.refs_3_
  71.4 8.4 %collective-permute-done.16.refs_1_ = bf16[4,4,64,256]{3,2,1,0:T(8,128)(2,1)S(1)} collective-permute-done((bf16[4,4,64,256]{3,2,1,0:T(8,128)(2,1)S(1)}, bf16[4,4,64,256]{3,2,1,0:T(8,128)(2,1)S(1)}, u32[]{:S(2)}, u32[]{:S(2)}) %collective-permute-start.16) | collective-permute-done | bytes 524320 | tf_op jit(solution)/shard_map/ppermute | solution.py:32
  79.8 1.8 %forward.9.refs_3_ = f32[4,64,256]{2,1,0:T(8,128)S(1)} custom-call(s32[16]{0:T(128)S(1)} %fusion.19.j_ref.refs_0_, bf16[4,4,64,256]{3,2,1,0:T(8,128)(2,1)S(1)} %collective-permute-done.16.refs_1_, bf16[2,4,256,4096]{3,2,1,0:T(8,128)(2,1)S(1)} %get-tuple-element.31.refs_2_, f32[4,64,256]{2,1,0:T(8,128)S(1)} %forward.8.refs_3_), custom_call_target="tpu_custom_call" | custom-call | flops 8589934592 | bytes 4194304 | tf_op jit(solution)/shard_map/forward/pallas_call | solution.py:213
  83.2 1.8 %forward.10.refs_3_ = f32[4,64,256]{2,1,0:T(8,128)S(1)} custom-call(s32[16]{0:T(128)S(1)} %fusion.19.j_ref.refs_0_, bf16[4,4,64,256]{3,2,1,0:T(8,128)(2,1)S(1)} %collective-permute-done.15.refs_1_, bf16[2,4,256,4096]{3,2,1,0:T(8,128)(2,1)S(1)} %get-tuple-element.31.refs_2_, f32[4,64,256]{2,1,0:T(8,128)S(1)} %forward.9.refs_3_), custom_call_target="tpu_custom_call" | custom-call | flops 8589934592 | bytes 4194304 | tf_op jit(solution)/shard_map/forward/pallas_call | solution.py:213
  85.0 1.9 %forward.11 = (f32[4,64,256]{2,1,0:T(8,128)S(1)}, f32[8,128]{1,0:T(8,128)S(1)}) custom-call(s32[16]{0:T(128)S(1)} %fusion.19.j_ref.refs_0_, bf16[4,4,64,256]{3,2,1,0:T(8,128)(2,1)S(1)} %collective-permute-done.14.refs_1_, bf16[2,4,256,4096]{3,2,1,0:T(8,128)(2,1)S(1)} %get-tuple-element.31.refs_2_, f32[4,64,256]{2,1,0:T(8,128)S(1)} %forward.10.refs_3_), custom_call_target="tpu_custom_call" | custom-call | flops 8589934592 | bytes 4194304 | tf_op jit(solution)/shard_map/forward/pallas_call | solution.py:213
  88.3 2.9 %adjoint.2 = (bf16[4,4,64,256]{3,2,1,0:T(8,128)(2,1)S(1)}, bf16[4,4,64,256]{3,2,1,0:T(8,128)(2,1)S(1)}, bf16[4,4,64,256]{3,2,1,0:T(8,128)(2,1)S(1)}) custom-call(s32[16]{0:T(128)S(1)} %fusion.19.j_ref.refs_0_, f32[4,64,256]{2,1,0:T(8,128)S(1)} %get-tuple-element.34.refs_1_.refs_4_.i0, bf16[2,4,256,4096]{3,2,1,0:T(8,128)(2,1)S(1)} %get-tuple-element.31.refs_2_), custom_call_target="tpu_custom_call" | custom-call | flops 25769803776 | bytes 4194304 | tf_op jit(solution)/shard_map/adjoint/pallas_call | solution.py:157
  91.3 2.5 %collective-permute-start.18 = (bf16[4,4,64,256]{3,2,1,0:T(8,128)(2,1)S(1)}, bf16[4,4,64,256]{3,2,1,0:T(8,128)(2,1)S(1)}, u32[]{:S(2)}, u32[]{:S(2)}) collective-permute-start(bf16[4,4,64,256]{3,2,1,0:T(8,128)(2,1)S(1)} %get-tuple-element.36), channel_id=1, source_target_pairs={{0,32},{1,9},{2,34},{3,11},{4,36},{5,13},{6,38},{7,15},{8,40},{9,1... | collective-permute-start | bytes 1572872 | tf_op jit(solution)/shard_map/ppermute | solution.py:32
  94.0 7.1 %collective-permute-done.17 = bf16[4,4,64,256]{3,2,1,0:T(8,128)(2,1)S(1)} collective-permute-done((bf16[4,4,64,256]{3,2,1,0:T(8,128)(2,1)S(1)}, bf16[4,4,64,256]{3,2,1,0:T(8,128)(2,1)S(1)}, u32[]{:S(2)}, u32[]{:S(2)}) %collective-permute-start.17) | collective-permute-done | bytes 524320 | tf_op jit(solution)/shard_map/ppermute | solution.py:32
  101.1 5.4 %collective-permute-done.18 = bf16[4,4,64,256]{3,2,1,0:T(8,128)(2,1)S(1)} collective-permute-done((bf16[4,4,64,256]{3,2,1,0:T(8,128)(2,1)S(1)}, bf16[4,4,64,256]{3,2,1,0:T(8,128)(2,1)S(1)}, u32[]{:S(2)}, u32[]{:S(2)}) %collective-permute-start.18) | collective-permute-done | bytes 524320 | tf_op jit(solution)/shard_map/ppermute | solution.py:32
  108.0 1.9 %collective-permute-start.22 = (bf16[4,64,256]{2,1,0:T(8,128)(2,1)S(1)}, bf16[4,64,256]{2,1,0:T(8,128)(2,1)S(1)}, u32[]{:S(2)}, u32[]{:S(2)}) collective-permute-start(bf16[4,64,256]{2,1,0:T(8,128)(2,1)S(1)} %get-tuple-element.51), channel_id=1, source_target_pairs={{0,24},{1,97},{2,26},{3,99},{4,28},{5,101},{6,30},{7,103},{8,0},{9... | collective-permute-start | bytes 393224 | tf_op jit(solution)/shard_map/ppermute | solution.py:32
  109.9 2.4 %collective-permute-done.20 = bf16[4,64,256]{2,1,0:T(8,128)(2,1)S(1)} collective-permute-done((bf16[4,64,256]{2,1,0:T(8,128)(2,1)S(1)}, bf16[4,64,256]{2,1,0:T(8,128)(2,1)S(1)}, u32[]{:S(2)}, u32[]{:S(2)}) %collective-permute-start.20) | collective-permute-done | bytes 131104 | tf_op jit(solution)/shard_map/ppermute | solution.py:32
  113.7 4.7 %collective-permute-start.23 = (bf16[4,32,256]{2,1,0:T(8,128)(2,1)S(1)}, bf16[4,32,256]{2,1,0:T(8,128)(2,1)S(1)}, u32[]{:S(2)}, u32[]{:S(2)}) collective-permute-start(bf16[4,32,256]{2,1,0:T(8,128)(2,1)S(1)} %get-tuple-element.59), channel_id=1, source_target_pairs={{0,1},{1,0},{2,3},{3,2},{4,5},{5,4},{6,7},{7,6},{8,9},{9,8},{10,11... | collective-permute-start | bytes 196616 | tf_op jit(solution)/shard_map/ppermute | solution.py:32
  120.9 3.3 %collective-permute-done.24.refs_2_ = bf16[256,256]{1,0:T(8,128)(2,1)S(1)} collective-permute-done((bf16[256,256]{1,0:T(8,128)(2,1)S(1)}, bf16[256,256]{1,0:T(8,128)(2,1)S(1)}, u32[]{:S(2)}, u32[]{:S(2)}) %collective-permute-start.24) | collective-permute-done | bytes 131104 | tf_op jit(solution)/shard_map/ppermute | solution.py:32
  124.2 1.8 collective-permute-done.25.refs_3_
  126.0 3.8 %collective-permute-done.26.refs_4_ = bf16[256,256]{1,0:T(8,128)(2,1)S(1)} collective-permute-done((bf16[256,256]{1,0:T(8,128)(2,1)S(1)}, bf16[256,256]{1,0:T(8,128)(2,1)S(1)}, u32[]{:S(2)}, u32[]{:S(2)}) %collective-permute-start.26) | collective-permute-done | bytes 131104 | tf_op jit(solution)/shard_map/ppermute | solution.py:32
  129.8 3.4 %window.3 = (f32[2,128,256]{2,1,0:T(8,128)S(1)}, bf16[2,128,256]{2,1,0:T(8,128)(2,1)S(1)}, f32[8,128]{1,0:T(8,128)S(1)}) custom-call(s32[2]{0:T(128)S(1)} %pad_add_fusion.place_ref.refs_0_, bf16[256,256]{1,0:T(8,128)(2,1)S(1)} %bitcast.79, bf16[256,256]{1,0:T(8,128)(2,1)S(1)} %collective-permute-done.24.refs_2_, ...), custom_call_target="tpu_custom_call" | custom-call | flops 1073741824 | bytes 4194304 | tf_op jit(solution)/shard_map/window/pallas_call | solution.py:318
  136.2 2.6 %collective-permute-done.28 = bf16[4,64,256]{2,1,0:T(8,128)(2,1)S(1)} collective-permute-done((bf16[4,64,256]{2,1,0:T(8,128)(2,1)S(1)}, bf16[4,64,256]{2,1,0:T(8,128)(2,1)S(1)}, u32[]{:S(2)}, u32[]{:S(2)}) %collective-permute-start.28) | collective-permute-done | bytes 131104 | tf_op jit(solution)/shard_map/ppermute | solution.py:32
  138.9 1.9 %collective-permute-done.29 = bf16[4,64,256]{2,1,0:T(8,128)(2,1)S(1)} collective-permute-done((bf16[4,64,256]{2,1,0:T(8,128)(2,1)S(1)}, bf16[4,64,256]{2,1,0:T(8,128)(2,1)S(1)}, u32[]{:S(2)}, u32[]{:S(2)}) %collective-permute-start.29) | collective-permute-done | bytes 131104 | tf_op jit(solution)/shard_map/ppermute | solution.py:32
  140.7 1.6 collective-permute-done.30
  142.4 2.2 %collective-permute-start.33 = (bf16[4,4,64,256]{3,2,1,0:T(8,128)(2,1)S(1)}, bf16[4,4,64,256]{3,2,1,0:T(8,128)(2,1)S(1)}, u32[]{:S(2)}, u32[]{:S(2)}) collective-permute-start(bf16[4,4,64,256]{3,2,1,0:T(8,128)(2,1)S(1)} %pad_maximum_fusion.1.refs_1_), channel_id=1, source_target_pairs={{0,96},{1,25},{2,98},{3,27},{4,100},{5,29},{6,102},{7,31},{8,104},... | collective-permute-start | bytes 1572872 | tf_op jit(solution)/shard_map/ppermute | solution.py:32
  144.6 1.8 forward.12.refs_3_
  148.0 8.3 %collective-permute-done.33.refs_1_ = bf16[4,4,64,256]{3,2,1,0:T(8,128)(2,1)S(1)} collective-permute-done((bf16[4,4,64,256]{3,2,1,0:T(8,128)(2,1)S(1)}, bf16[4,4,64,256]{3,2,1,0:T(8,128)(2,1)S(1)}, u32[]{:S(2)}, u32[]{:S(2)}) %collective-permute-start.33) | collective-permute-done | bytes 524320 | tf_op jit(solution)/shard_map/ppermute | solution.py:32
  156.3 1.8 %forward.13.refs_3_ = f32[4,64,256]{2,1,0:T(8,128)S(1)} custom-call(s32[16]{0:T(128)S(1)} %fusion.19.j_ref.refs_0_, bf16[4,4,64,256]{3,2,1,0:T(8,128)(2,1)S(1)} %collective-permute-done.33.refs_1_, bf16[2,4,256,4096]{3,2,1,0:T(8,128)(2,1)S(1)} %get-tuple-element.31.refs_2_, f32[4,64,256]{2,1,0:T(8,128)S(1)} %forward.12.refs_3_), custom_call_target="tpu_custom_call" | custom-call | flops 8589934592 | bytes 4194304 | tf_op jit(solution)/shard_map/forward/pallas_call | solution.py:213
  159.7 1.8 %forward.14.refs_3_ = f32[4,64,256]{2,1,0:T(8,128)S(1)} custom-call(s32[16]{0:T(128)S(1)} %fusion.19.j_ref.refs_0_, bf16[4,4,64,256]{3,2,1,0:T(8,128)(2,1)S(1)} %collective-permute-done.32.refs_1_, bf16[2,4,256,4096]{3,2,1,0:T(8,128)(2,1)S(1)} %get-tuple-element.31.refs_2_, f32[4,64,256]{2,1,0:T(8,128)S(1)} %forward.13.refs_3_), custom_call_target="tpu_custom_call" | custom-call | flops 8589934592 | bytes 4194304 | tf_op jit(solution)/shard_map/forward/pallas_call | solution.py:213
  161.6 1.9 %forward.15 = (f32[4,64,256]{2,1,0:T(8,128)S(1)}, f32[8,128]{1,0:T(8,128)S(1)}) custom-call(s32[16]{0:T(128)S(1)} %fusion.19.j_ref.refs_0_, bf16[4,4,64,256]{3,2,1,0:T(8,128)(2,1)S(1)} %collective-permute-done.31.refs_1_, bf16[2,4,256,4096]{3,2,1,0:T(8,128)(2,1)S(1)} %get-tuple-element.31.refs_2_, f32[4,64,256]{2,1,0:T(8,128)S(1)} %forward.14.refs_3_, ...), custom_call_target="tpu_custom_call" | custom-call | flops 8589934592 | bytes 4194304 | tf_op jit(solution)/shard_map/forward/pallas_call | solution.py:213
  163.5 2.6 %collective-permute-start.34 = (f32[8,128]{1,0:T(8,128)S(1)}, f32[8,128]{1,0:T(8,128)S(1)}, u32[]{:S(2)}, u32[]{:S(2)}) collective-permute-start(f32[8,128]{1,0:T(8,128)S(1)} %get-tuple-element.45), channel_id=1, source_target_pairs={{0,1},{1,0},{2,3},{3,2},{4,5},{5,4},{6,7},{7,6},{8,9},{9,8},{10,11... | collective-permute-start | bytes 12296 | tf_op jit(solution)/shard_map/ppermute | solution.py:32
  172.0 2.2 %collective-permute-start.40 = (f32[8,128]{1,0:T(8,128)S(1)}, f32[8,128]{1,0:T(8,128)S(1)}, u32[]{:S(2)}, u32[]{:S(2)}) collective-permute-start(f32[8,128]{1,0:T(8,128)S(1)} %add_add_fusion.2), channel_id=1, source_target_pairs={{0,24},{1,97},{2,26},{3,99},{4,28},{5,101},{6,30},{7,103},{8,0},{9... | collective-permute-start | bytes 12296 | tf_op jit(solution)/shard_map/ppermute | solution.py:32
  174.2 2.2 %collective-permute-start.44 = (f32[128,256]{1,0:T(8,128)S(1)}, f32[128,256]{1,0:T(8,128)S(1)}, u32[]{:S(2)}, u32[]{:S(2)}) collective-permute-start(f32[128,256]{1,0:T(8,128)S(1)} %slice_bitcast_fusion.1), channel_id=1, source_target_pairs={{0,1},{1,0},{2,3},{3,2},{4,5},{5,4},{6,7},{7,6},{8,9},{9,8},{10,11... | collective-permute-start | bytes 393224 | tf_op jit(solution)/shard_map/ppermute | solution.py:32
  177.1 2.1 %collective-permute-start.42 = (f32[8,128]{1,0:T(8,128)S(1)}, f32[8,128]{1,0:T(8,128)S(1)}, u32[]{:S(2)}, u32[]{:S(2)}) collective-permute-start(f32[8,128]{1,0:T(8,128)S(1)} %add_add_fusion.1), channel_id=1, source_target_pairs={{0,64},{1,17},{2,66},{3,19},{4,68},{5,21},{6,70},{7,23},{8,72},{9,... | collective-permute-start | bytes 12296 | tf_op jit(solution)/shard_map/ppermute | solution.py:32
  179.2 2.0 %collective-permute-start.43 = (f32[8,128]{1,0:T(8,128)S(1)}, f32[8,128]{1,0:T(8,128)S(1)}, u32[]{:S(2)}, u32[]{:S(2)}) collective-permute-start(f32[8,128]{1,0:T(8,128)S(1)} %add_add_fusion.1), channel_id=1, source_target_pairs={{0,96},{1,25},{2,98},{3,27},{4,100},{5,29},{6,102},{7,31},{8,104},... | collective-permute-start | bytes 12296 | tf_op jit(solution)/shard_map/ppermute | solution.py:32
  (91 shorter events, 32.5 us)
Async XLA Ops:
  0.6 50.0 %copy-start.1 = (bf16[64,192]{1,0:T(8,128)(2,1)S(1)}, bf16[64,192]{1,0:T(8,128)(2,1)}, u32[]{:S(2)}) copy-start(bf16[64,192]{1,0:T(8,128)(2,1)} %constant.105.clone.refs_5_) | copy-start | bytes 73732
  0.6 49.9 %copy-start.2 = (bf16[4,16,192]{2,1,0:T(8,128)(2,1)S(1)}, bf16[4,16,192]{2,1,0:T(8,128)(2,1)}, u32[]{:S(2)}) copy-start(bf16[4,16,192]{2,1,0:T(8,128)(2,1)} %constant.110.refs_6_) | copy-start | bytes 73732
  8.7 10.6 %collective-permute-start = (bf16[4,4,64,256]{3,2,1,0:T(8,128)(2,1)S(1)}, bf16[4,4,64,256]{3,2,1,0:T(8,128)(2,1)S(1)}, u32[]{:S(2)}, u32[]{:S(2)}) collective-permute-start(bf16[4,4,64,256]{3,2,1,0:T(8,128)(2,1)S(1)} %get-tuple-element.27), channel_id=1, source_target_pairs={{0,64},{1,17},{2,66},{3,19},{4,68},{5,21},{6,70},{7,23},{8,72},{9,... | collective-permute-start | bytes 1572872 | tf_op jit(solution)/shard_map/ppermute | solution.py:32
  12.3 12.5 %collective-permute-start.1 = (bf16[4,4,64,256]{3,2,1,0:T(8,128)(2,1)S(1)}, bf16[4,4,64,256]{3,2,1,0:T(8,128)(2,1)S(1)}, u32[]{:S(2)}, u32[]{:S(2)}) collective-permute-start(bf16[4,4,64,256]{3,2,1,0:T(8,128)(2,1)S(1)} %get-tuple-element.28), channel_id=1, source_target_pairs={{0,32},{1,9},{2,34},{3,11},{4,36},{5,13},{6,38},{7,15},{8,40},{9,1... | collective-permute-start | bytes 1572872 | tf_op jit(solution)/shard_map/ppermute | solution.py:32
  12.6 12.5 %collective-permute-start.2 = (bf16[4,4,64,256]{3,2,1,0:T(8,128)(2,1)S(1)}, bf16[4,4,64,256]{3,2,1,0:T(8,128)(2,1)S(1)}, u32[]{:S(2)}, u32[]{:S(2)}) collective-permute-start(bf16[4,4,64,256]{3,2,1,0:T(8,128)(2,1)S(1)} %get-tuple-element.29), channel_id=1, source_target_pairs={{0,96},{1,25},{2,98},{3,27},{4,100},{5,29},{6,102},{7,31},{8,104},... | collective-permute-start | bytes 1572872 | tf_op jit(solution)/shard_map/ppermute | solution.py:32
  25.4 5.7 %collective-permute-start.3 = (bf16[4,64,256]{2,1,0:T(8,128)(2,1)S(1)}, bf16[4,64,256]{2,1,0:T(8,128)(2,1)S(1)}, u32[]{:S(2)}, u32[]{:S(2)}) collective-permute-start(bf16[4,64,256]{2,1,0:T(8,128)(2,1)S(1)} %get-tuple-element.53), channel_id=1, source_target_pairs={{0,16},{1,65},{2,18},{3,67},{4,20},{5,69},{6,22},{7,71},{8,24},{9,... | collective-permute-start | bytes 393224 | tf_op jit(solution)/shard_map/ppermute | solution.py:32
  28.4 5.0 %collective-permute-start.4 = (bf16[4,64,256]{2,1,0:T(8,128)(2,1)S(1)}, bf16[4,64,256]{2,1,0:T(8,128)(2,1)S(1)}, u32[]{:S(2)}, u32[]{:S(2)}) collective-permute-start(bf16[4,64,256]{2,1,0:T(8,128)(2,1)S(1)} %get-tuple-element.55), channel_id=1, source_target_pairs={{0,8},{1,33},{2,10},{3,35},{4,12},{5,37},{6,14},{7,39},{8,16},{9,4... | collective-permute-start | bytes 393224 | tf_op jit(solution)/shard_map/ppermute | solution.py:32
  28.8 4.6 %collective-permute-start.5 = (bf16[4,64,256]{2,1,0:T(8,128)(2,1)S(1)}, bf16[4,64,256]{2,1,0:T(8,128)(2,1)S(1)}, u32[]{:S(2)}, u32[]{:S(2)}) collective-permute-start(bf16[4,64,256]{2,1,0:T(8,128)(2,1)S(1)} %get-tuple-element.54), channel_id=1, source_target_pairs={{0,24},{1,97},{2,26},{3,99},{4,28},{5,101},{6,30},{7,103},{8,0},{9... | collective-permute-start | bytes 393224 | tf_op jit(solution)/shard_map/ppermute | solution.py:32
  33.6 4.0 %collective-permute-start.6 = (bf16[4,32,256]{2,1,0:T(8,128)(2,1)S(1)}, bf16[4,32,256]{2,1,0:T(8,128)(2,1)S(1)}, u32[]{:S(2)}, u32[]{:S(2)}) collective-permute-start(bf16[4,32,256]{2,1,0:T(8,128)(2,1)S(1)} %get-tuple-element.63), channel_id=1, source_target_pairs={{0,1},{1,0},{2,3},{3,2},{4,5},{5,4},{6,7},{7,6},{8,9},{9,8},{10,11... | collective-permute-start | bytes 196616 | tf_op jit(solution)/shard_map/ppermute | solution.py:32
  37.6 9.5 %collective-permute-start.7 = (bf16[256,256]{1,0:T(8,128)(2,1)S(1)}, bf16[256,256]{1,0:T(8,128)(2,1)S(1)}, u32[]{:S(2)}, u32[]{:S(2)}) collective-permute-start(bf16[256,256]{1,0:T(8,128)(2,1)S(1)} %bitcast.80), channel_id=1, source_target_pairs={{0,6},{1,7},{2,0},{3,1},{4,2},{5,3},{6,4},{7,5},{8,14},{9,15},{10,... | collective-permute-start | bytes 393224 | tf_op jit(solution)/shard_map/ppermute | solution.py:32
  41.4 6.0 %collective-permute-start.8 = (bf16[256,256]{1,0:T(8,128)(2,1)S(1)}, bf16[256,256]{1,0:T(8,128)(2,1)S(1)}, u32[]{:S(2)}, u32[]{:S(2)}) collective-permute-start(bf16[256,256]{1,0:T(8,128)(2,1)S(1)} %bitcast.81), channel_id=1, source_target_pairs={{0,4},{1,5},{2,6},{3,7},{4,0},{5,1},{6,2},{7,3},{8,12},{9,13},{10,... | collective-permute-start | bytes 393224 | tf_op jit(solution)/shard_map/ppermute | solution.py:32
  41.4 9.1 %collective-permute-start.9 = (bf16[256,256]{1,0:T(8,128)(2,1)S(1)}, bf16[256,256]{1,0:T(8,128)(2,1)S(1)}, u32[]{:S(2)}, u32[]{:S(2)}) collective-permute-start(bf16[256,256]{1,0:T(8,128)(2,1)S(1)} %bitcast.82), channel_id=1, source_target_pairs={{0,2},{1,3},{2,4},{3,5},{4,6},{5,7},{6,0},{7,1},{8,10},{9,11},{10,... | collective-permute-start | bytes 393224 | tf_op jit(solution)/shard_map/ppermute | solution.py:32
  54.0 1.8 collective-permute-start.10
  55.8 5.7 %collective-permute-start.11 = (bf16[4,64,256]{2,1,0:T(8,128)(2,1)S(1)}, bf16[4,64,256]{2,1,0:T(8,128)(2,1)S(1)}, u32[]{:S(2)}, u32[]{:S(2)}) collective-permute-start(bf16[4,64,256]{2,1,0:T(8,128)(2,1)S(1)} %bitcast.86), channel_id=1, source_target_pairs={{0,24},{1,97},{2,26},{3,99},{4,28},{5,101},{6,30},{7,103},{8,0},{9... | collective-permute-start | bytes 393224 | tf_op jit(solution)/shard_map/ppermute | solution.py:32
  58.2 5.4 %collective-permute-start.12 = (bf16[4,64,256]{2,1,0:T(8,128)(2,1)S(1)}, bf16[4,64,256]{2,1,0:T(8,128)(2,1)S(1)}, u32[]{:S(2)}, u32[]{:S(2)}) collective-permute-start(bf16[4,64,256]{2,1,0:T(8,128)(2,1)S(1)} %bitcast.87), channel_id=1, source_target_pairs={{0,16},{1,65},{2,18},{3,67},{4,20},{5,69},{6,22},{7,71},{8,24},{9,... | collective-permute-start | bytes 393224 | tf_op jit(solution)/shard_map/ppermute | solution.py:32
  58.7 6.5 %collective-permute-start.13 = (bf16[4,64,256]{2,1,0:T(8,128)(2,1)S(1)}, bf16[4,64,256]{2,1,0:T(8,128)(2,1)S(1)}, u32[]{:S(2)}, u32[]{:S(2)}) collective-permute-start(bf16[4,64,256]{2,1,0:T(8,128)(2,1)S(1)} %bitcast.88), channel_id=1, source_target_pairs={{0,8},{1,33},{2,10},{3,35},{4,12},{5,37},{6,14},{7,39},{8,16},{9,4... | collective-permute-start | bytes 393224 | tf_op jit(solution)/shard_map/ppermute | solution.py:32
  65.3 14.5 %collective-permute-start.16 = (bf16[4,4,64,256]{3,2,1,0:T(8,128)(2,1)S(1)}, bf16[4,4,64,256]{3,2,1,0:T(8,128)(2,1)S(1)}, u32[]{:S(2)}, u32[]{:S(2)}) collective-permute-start(bf16[4,4,64,256]{3,2,1,0:T(8,128)(2,1)S(1)} %pad_maximum_fusion.refs_1_), channel_id=1, source_target_pairs={{0,96},{1,25},{2,98},{3,27},{4,100},{5,29},{6,102},{7,31},{8,104},... | collective-permute-start | bytes 1572872 | tf_op jit(solution)/shard_map/ppermute | solution.py:32
  68.0 15.2 %collective-permute-start.15 = (bf16[4,4,64,256]{3,2,1,0:T(8,128)(2,1)S(1)}, bf16[4,4,64,256]{3,2,1,0:T(8,128)(2,1)S(1)}, u32[]{:S(2)}, u32[]{:S(2)}) collective-permute-start(bf16[4,4,64,256]{3,2,1,0:T(8,128)(2,1)S(1)} %pad_maximum_fusion.refs_1_), channel_id=1, source_target_pairs={{0,32},{1,9},{2,34},{3,11},{4,36},{5,13},{6,38},{7,15},{8,40},{9,1... | collective-permute-start | bytes 1572872 | tf_op jit(solution)/shard_map/ppermute | solution.py:32
  69.9 15.2 %collective-permute-start.14 = (bf16[4,4,64,256]{3,2,1,0:T(8,128)(2,1)S(1)}, bf16[4,4,64,256]{3,2,1,0:T(8,128)(2,1)S(1)}, u32[]{:S(2)}, u32[]{:S(2)}) collective-permute-start(bf16[4,4,64,256]{3,2,1,0:T(8,128)(2,1)S(1)} %pad_maximum_fusion.refs_1_), channel_id=1, source_target_pairs={{0,64},{1,17},{2,66},{3,19},{4,68},{5,21},{6,70},{7,23},{8,72},{9,... | collective-permute-start | bytes 1572872 | tf_op jit(solution)/shard_map/ppermute | solution.py:32
  91.2 10.0 %collective-permute-start.17 = (bf16[4,4,64,256]{3,2,1,0:T(8,128)(2,1)S(1)}, bf16[4,4,64,256]{3,2,1,0:T(8,128)(2,1)S(1)}, u32[]{:S(2)}, u32[]{:S(2)}) collective-permute-start(bf16[4,4,64,256]{3,2,1,0:T(8,128)(2,1)S(1)} %adjoint.3), channel_id=1, source_target_pairs={{0,64},{1,17},{2,66},{3,19},{4,68},{5,21},{6,70},{7,23},{8,72},{9,... | collective-permute-start | bytes 1572872 | tf_op jit(solution)/shard_map/ppermute | solution.py:32
  91.3 15.2 %collective-permute-start.18 = (bf16[4,4,64,256]{3,2,1,0:T(8,128)(2,1)S(1)}, bf16[4,4,64,256]{3,2,1,0:T(8,128)(2,1)S(1)}, u32[]{:S(2)}, u32[]{:S(2)}) collective-permute-start(bf16[4,4,64,256]{3,2,1,0:T(8,128)(2,1)S(1)} %get-tuple-element.36), channel_id=1, source_target_pairs={{0,32},{1,9},{2,34},{3,11},{4,36},{5,13},{6,38},{7,15},{8,40},{9,1... | collective-permute-start | bytes 1572872 | tf_op jit(solution)/shard_map/ppermute | solution.py:32
  93.7 12.8 %collective-permute-start.19 = (bf16[4,4,64,256]{3,2,1,0:T(8,128)(2,1)S(1)}, bf16[4,4,64,256]{3,2,1,0:T(8,128)(2,1)S(1)}, u32[]{:S(2)}, u32[]{:S(2)}) collective-permute-start(bf16[4,4,64,256]{3,2,1,0:T(8,128)(2,1)S(1)} %get-tuple-element.37), channel_id=1, source_target_pairs={{0,96},{1,25},{2,98},{3,27},{4,100},{5,29},{6,102},{7,31},{8,104},... | collective-permute-start | bytes 1572872 | tf_op jit(solution)/shard_map/ppermute | solution.py:32
  106.7 5.5 %collective-permute-start.20 = (bf16[4,64,256]{2,1,0:T(8,128)(2,1)S(1)}, bf16[4,64,256]{2,1,0:T(8,128)(2,1)S(1)}, u32[]{:S(2)}, u32[]{:S(2)}) collective-permute-start(bf16[4,64,256]{2,1,0:T(8,128)(2,1)S(1)} %get-tuple-element.50), channel_id=1, source_target_pairs={{0,16},{1,65},{2,18},{3,67},{4,20},{5,69},{6,22},{7,71},{8,24},{9,... | collective-permute-start | bytes 393224 | tf_op jit(solution)/shard_map/ppermute | solution.py:32
  107.2 6.3 %collective-permute-start.21 = (bf16[4,64,256]{2,1,0:T(8,128)(2,1)S(1)}, bf16[4,64,256]{2,1,0:T(8,128)(2,1)S(1)}, u32[]{:S(2)}, u32[]{:S(2)}) collective-permute-start(bf16[4,64,256]{2,1,0:T(8,128)(2,1)S(1)} %get-tuple-element.52), channel_id=1, source_target_pairs={{0,8},{1,33},{2,10},{3,35},{4,12},{5,37},{6,14},{7,39},{8,16},{9,4... | collective-permute-start | bytes 393224 | tf_op jit(solution)/shard_map/ppermute | solution.py:32
  108.0 5.6 %collective-permute-start.22 = (bf16[4,64,256]{2,1,0:T(8,128)(2,1)S(1)}, bf16[4,64,256]{2,1,0:T(8,128)(2,1)S(1)}, u32[]{:S(2)}, u32[]{:S(2)}) collective-permute-start(bf16[4,64,256]{2,1,0:T(8,128)(2,1)S(1)} %get-tuple-element.51), channel_id=1, source_target_pairs={{0,24},{1,97},{2,26},{3,99},{4,28},{5,101},{6,30},{7,103},{8,0},{9... | collective-permute-start | bytes 393224 | tf_op jit(solution)/shard_map/ppermute | solution.py:32
  113.7 5.6 %collective-permute-start.23 = (bf16[4,32,256]{2,1,0:T(8,128)(2,1)S(1)}, bf16[4,32,256]{2,1,0:T(8,128)(2,1)S(1)}, u32[]{:S(2)}, u32[]{:S(2)}) collective-permute-start(bf16[4,32,256]{2,1,0:T(8,128)(2,1)S(1)} %get-tuple-element.59), channel_id=1, source_target_pairs={{0,1},{1,0},{2,3},{3,2},{4,5},{5,4},{6,7},{7,6},{8,9},{9,8},{10,11... | collective-permute-start | bytes 196616 | tf_op jit(solution)/shard_map/ppermute | solution.py:32
  119.4 4.8 %collective-permute-start.24 = (bf16[256,256]{1,0:T(8,128)(2,1)S(1)}, bf16[256,256]{1,0:T(8,128)(2,1)S(1)}, u32[]{:S(2)}, u32[]{:S(2)}) collective-permute-start(bf16[256,256]{1,0:T(8,128)(2,1)S(1)} %bitcast.76), channel_id=1, source_target_pairs={{0,6},{1,7},{2,0},{3,1},{4,2},{5,3},{6,4},{7,5},{8,14},{9,15},{10,... | collective-permute-start | bytes 393224 | tf_op jit(solution)/shard_map/ppermute | solution.py:32
  120.0 5.9 %collective-permute-start.25 = (bf16[256,256]{1,0:T(8,128)(2,1)S(1)}, bf16[256,256]{1,0:T(8,128)(2,1)S(1)}, u32[]{:S(2)}, u32[]{:S(2)}) collective-permute-start(bf16[256,256]{1,0:T(8,128)(2,1)S(1)} %bitcast.77), channel_id=1, source_target_pairs={{0,4},{1,5},{2,6},{3,7},{4,0},{5,1},{6,2},{7,3},{8,12},{9,13},{10,... | collective-permute-start | bytes 393224 | tf_op jit(solution)/shard_map/ppermute | solution.py:32
  120.0 9.7 %collective-permute-start.26 = (bf16[256,256]{1,0:T(8,128)(2,1)S(1)}, bf16[256,256]{1,0:T(8,128)(2,1)S(1)}, u32[]{:S(2)}, u32[]{:S(2)}) collective-permute-start(bf16[256,256]{1,0:T(8,128)(2,1)S(1)} %bitcast.78), channel_id=1, source_target_pairs={{0,2},{1,3},{2,4},{3,5},{4,6},{5,7},{6,0},{7,1},{8,10},{9,11},{10,... | collective-permute-start | bytes 393224 | tf_op jit(solution)/shard_map/ppermute | solution.py:32
  133.2 1.5 collective-permute-start.27
  134.7 4.2 %collective-permute-start.28 = (bf16[4,64,256]{2,1,0:T(8,128)(2,1)S(1)}, bf16[4,64,256]{2,1,0:T(8,128)(2,1)S(1)}, u32[]{:S(2)}, u32[]{:S(2)}) collective-permute-start(bf16[4,64,256]{2,1,0:T(8,128)(2,1)S(1)} %bitcast.90), channel_id=1, source_target_pairs={{0,24},{1,97},{2,26},{3,99},{4,28},{5,101},{6,30},{7,103},{8,0},{9... | collective-permute-start | bytes 393224 | tf_op jit(solution)/shard_map/ppermute | solution.py:32
  135.3 5.4 %collective-permute-start.29 = (bf16[4,64,256]{2,1,0:T(8,128)(2,1)S(1)}, bf16[4,64,256]{2,1,0:T(8,128)(2,1)S(1)}, u32[]{:S(2)}, u32[]{:S(2)}) collective-permute-start(bf16[4,64,256]{2,1,0:T(8,128)(2,1)S(1)} %bitcast.91), channel_id=1, source_target_pairs={{0,16},{1,65},{2,18},{3,67},{4,20},{5,69},{6,22},{7,71},{8,24},{9,... | collective-permute-start | bytes 393224 | tf_op jit(solution)/shard_map/ppermute | solution.py:32
  135.3 7.0 %collective-permute-start.30 = (bf16[4,64,256]{2,1,0:T(8,128)(2,1)S(1)}, bf16[4,64,256]{2,1,0:T(8,128)(2,1)S(1)}, u32[]{:S(2)}, u32[]{:S(2)}) collective-permute-start(bf16[4,64,256]{2,1,0:T(8,128)(2,1)S(1)} %bitcast.92), channel_id=1, source_target_pairs={{0,8},{1,33},{2,10},{3,35},{4,12},{5,37},{6,14},{7,39},{8,16},{9,4... | collective-permute-start | bytes 393224 | tf_op jit(solution)/shard_map/ppermute | solution.py:32
  142.4 14.0 %collective-permute-start.33 = (bf16[4,4,64,256]{3,2,1,0:T(8,128)(2,1)S(1)}, bf16[4,4,64,256]{3,2,1,0:T(8,128)(2,1)S(1)}, u32[]{:S(2)}, u32[]{:S(2)}) collective-permute-start(bf16[4,4,64,256]{3,2,1,0:T(8,128)(2,1)S(1)} %pad_maximum_fusion.1.refs_1_), channel_id=1, source_target_pairs={{0,96},{1,25},{2,98},{3,27},{4,100},{5,29},{6,102},{7,31},{8,104},... | collective-permute-start | bytes 1572872 | tf_op jit(solution)/shard_map/ppermute | solution.py:32
  144.6 15.2 %collective-permute-start.32 = (bf16[4,4,64,256]{3,2,1,0:T(8,128)(2,1)S(1)}, bf16[4,4,64,256]{3,2,1,0:T(8,128)(2,1)S(1)}, u32[]{:S(2)}, u32[]{:S(2)}) collective-permute-start(bf16[4,4,64,256]{3,2,1,0:T(8,128)(2,1)S(1)} %pad_maximum_fusion.1.refs_1_), channel_id=1, source_target_pairs={{0,32},{1,9},{2,34},{3,11},{4,36},{5,13},{6,38},{7,15},{8,40},{9,1... | collective-permute-start | bytes 1572872 | tf_op jit(solution)/shard_map/ppermute | solution.py:32
  146.4 15.2 %collective-permute-start.31 = (bf16[4,4,64,256]{3,2,1,0:T(8,128)(2,1)S(1)}, bf16[4,4,64,256]{3,2,1,0:T(8,128)(2,1)S(1)}, u32[]{:S(2)}, u32[]{:S(2)}) collective-permute-start(bf16[4,4,64,256]{3,2,1,0:T(8,128)(2,1)S(1)} %pad_maximum_fusion.1.refs_1_), channel_id=1, source_target_pairs={{0,64},{1,17},{2,66},{3,19},{4,68},{5,21},{6,70},{7,23},{8,72},{9,... | collective-permute-start | bytes 1572872 | tf_op jit(solution)/shard_map/ppermute | solution.py:32
  163.5 3.5 %collective-permute-start.34 = (f32[8,128]{1,0:T(8,128)S(1)}, f32[8,128]{1,0:T(8,128)S(1)}, u32[]{:S(2)}, u32[]{:S(2)}) collective-permute-start(f32[8,128]{1,0:T(8,128)S(1)} %get-tuple-element.45), channel_id=1, source_target_pairs={{0,1},{1,0},{2,3},{3,2},{4,5},{5,4},{6,7},{7,6},{8,9},{9,8},{10,11... | collective-permute-start | bytes 12296 | tf_op jit(solution)/shard_map/ppermute | solution.py:32
  167.0 3.7 %collective-permute-start.35 = (f32[8,128]{1,0:T(8,128)S(1)}, f32[8,128]{1,0:T(8,128)S(1)}, u32[]{:S(2)}, u32[]{:S(2)}) collective-permute-start(f32[8,128]{1,0:T(8,128)S(1)} %add.268), channel_id=1, source_target_pairs={{0,2},{1,3},{2,4},{3,5},{4,6},{5,7},{6,0},{7,1},{8,10},{9,11},{10,... | collective-permute-start | bytes 12296 | tf_op jit(solution)/shard_map/ppermute | solution.py:32
  167.0 4.0 %collective-permute-start.36 = (f32[8,128]{1,0:T(8,128)S(1)}, f32[8,128]{1,0:T(8,128)S(1)}, u32[]{:S(2)}, u32[]{:S(2)}) collective-permute-start(f32[8,128]{1,0:T(8,128)S(1)} %add.268), channel_id=1, source_target_pairs={{0,4},{1,5},{2,6},{3,7},{4,0},{5,1},{6,2},{7,3},{8,12},{9,13},{10,... | collective-permute-start | bytes 12296 | tf_op jit(solution)/shard_map/ppermute | solution.py:32
  168.4 3.1 %collective-permute-start.37 = (f32[8,128]{1,0:T(8,128)S(1)}, f32[8,128]{1,0:T(8,128)S(1)}, u32[]{:S(2)}, u32[]{:S(2)}) collective-permute-start(f32[8,128]{1,0:T(8,128)S(1)} %add.268), channel_id=1, source_target_pairs={{0,6},{1,7},{2,0},{3,1},{4,2},{5,3},{6,4},{7,5},{8,14},{9,15},{10,... | collective-permute-start | bytes 12296 | tf_op jit(solution)/shard_map/ppermute | solution.py:32
  171.5 4.9 %collective-permute-start.38 = (f32[8,128]{1,0:T(8,128)S(1)}, f32[8,128]{1,0:T(8,128)S(1)}, u32[]{:S(2)}, u32[]{:S(2)}) collective-permute-start(f32[8,128]{1,0:T(8,128)S(1)} %add_add_fusion.2), channel_id=1, source_target_pairs={{0,8},{1,33},{2,10},{3,35},{4,12},{5,37},{6,14},{7,39},{8,16},{9,4... | collective-permute-start | bytes 12296 | tf_op jit(solution)/shard_map/ppermute | solution.py:32
  171.5 4.9 %collective-permute-start.39 = (f32[8,128]{1,0:T(8,128)S(1)}, f32[8,128]{1,0:T(8,128)S(1)}, u32[]{:S(2)}, u32[]{:S(2)}) collective-permute-start(f32[8,128]{1,0:T(8,128)S(1)} %add_add_fusion.2), channel_id=1, source_target_pairs={{0,16},{1,65},{2,18},{3,67},{4,20},{5,69},{6,22},{7,71},{8,24},{9,... | collective-permute-start | bytes 12296 | tf_op jit(solution)/shard_map/ppermute | solution.py:32
  172.0 4.5 %collective-permute-start.40 = (f32[8,128]{1,0:T(8,128)S(1)}, f32[8,128]{1,0:T(8,128)S(1)}, u32[]{:S(2)}, u32[]{:S(2)}) collective-permute-start(f32[8,128]{1,0:T(8,128)S(1)} %add_add_fusion.2), channel_id=1, source_target_pairs={{0,24},{1,97},{2,26},{3,99},{4,28},{5,101},{6,30},{7,103},{8,0},{9... | collective-permute-start | bytes 12296 | tf_op jit(solution)/shard_map/ppermute | solution.py:32
  174.2 7.9 %collective-permute-start.44 = (f32[128,256]{1,0:T(8,128)S(1)}, f32[128,256]{1,0:T(8,128)S(1)}, u32[]{:S(2)}, u32[]{:S(2)}) collective-permute-start(f32[128,256]{1,0:T(8,128)S(1)} %slice_bitcast_fusion.1), channel_id=1, source_target_pairs={{0,1},{1,0},{2,3},{3,2},{4,5},{5,4},{6,7},{7,6},{8,9},{9,8},{10,11... | collective-permute-start | bytes 393224 | tf_op jit(solution)/shard_map/ppermute | solution.py:32
  176.5 5.6 %collective-permute-start.41 = (f32[8,128]{1,0:T(8,128)S(1)}, f32[8,128]{1,0:T(8,128)S(1)}, u32[]{:S(2)}, u32[]{:S(2)}) collective-permute-start(f32[8,128]{1,0:T(8,128)S(1)} %add_add_fusion.1), channel_id=1, source_target_pairs={{0,32},{1,9},{2,34},{3,11},{4,36},{5,13},{6,38},{7,15},{8,40},{9,1... | collective-permute-start | bytes 12296 | tf_op jit(solution)/shard_map/ppermute | solution.py:32
  177.1 5.0 %collective-permute-start.42 = (f32[8,128]{1,0:T(8,128)S(1)}, f32[8,128]{1,0:T(8,128)S(1)}, u32[]{:S(2)}, u32[]{:S(2)}) collective-permute-start(f32[8,128]{1,0:T(8,128)S(1)} %add_add_fusion.1), channel_id=1, source_target_pairs={{0,64},{1,17},{2,66},{3,19},{4,68},{5,21},{6,70},{7,23},{8,72},{9,... | collective-permute-start | bytes 12296 | tf_op jit(solution)/shard_map/ppermute | solution.py:32
  179.2 3.0 %collective-permute-start.43 = (f32[8,128]{1,0:T(8,128)S(1)}, f32[8,128]{1,0:T(8,128)S(1)}, u32[]{:S(2)}, u32[]{:S(2)}) collective-permute-start(f32[8,128]{1,0:T(8,128)S(1)} %add_add_fusion.1), channel_id=1, source_target_pairs={{0,96},{1,25},{2,98},{3,27},{4,100},{5,29},{6,102},{7,31},{8,104},... | collective-permute-start | bytes 12296 | tf_op jit(solution)/shard_map/ppermute | solution.py:32
  181.2 1.9 %collective-permute-start.45 = (f32[128,256]{1,0:T(8,128)S(1)}, f32[128,256]{1,0:T(8,128)S(1)}, u32[]{:S(2)}, u32[]{:S(2)}) collective-permute-start(f32[128,256]{1,0:T(8,128)S(1)} %slice_bitcast_fusion), channel_id=1, source_target_pairs={{0,1},{1,0},{2,3},{3,2},{4,5},{5,4},{6,7},{7,6},{8,9},{9,8},{10,11... | collective-permute-start | bytes 393224 | tf_op jit(solution)/shard_map/ppermute | solution.py:32
  (2 other events, 57.6 us)

commit v3 on v2

--- a/solution.py
+++ b/solution.py
@@ -85,22 +85,26 @@
     return jnp.concatenate(rows, axis=0)
 
 
-def terms(kb, f, u, j_ref, k_ref, out_ref):
+def terms(kb, f, u, at, j_ref, k_ref, out_ref):
     v = swapped(u, 1)
     for ks in range(4):
         cols = pl.ds(pl.multiple_of(j_ref[kb * 4 + ks] * 256, 256), 256)
         r = jnp.dot(u, k_ref[0, f, :, cols], preferred_element_type=F32)
         r = r + jnp.dot(v, k_ref[1, f, :, cols], preferred_element_type=F32)
-        out_ref[ks, f] = r.astype(BF)
-
-
-def first_kernel(place_ref, j_ref, data_hbm, k_hbm, k_ref, *refs):
-    out_refs, (data_ref, sem, sems) = refs[:4], refs[4:]
+        out_ref[ks, at] = r.astype(BF)
+
+
+def first_kernel(place_ref, j_ref, data_hbm, k_hbm, *refs):
+    held_refs, turned_refs, out_refs = refs[:2], refs[2:4], refs[4:8]
+    data_ref, sem, sems = refs[8:]
     core = place_ref[1]
     fetch = pltpu.make_async_copy(data_hbm, data_ref, sem)
     fetch.start()
     copies = [
-        [pltpu.make_async_copy(k_hbm.at[p, f], k_ref.at[p, f], sems.at[p, f]) for p in range(2)]
+        [
+            pltpu.make_async_copy(k_hbm.at[p, f], held_refs[f // 2].at[p, f % 2], sems.at[p, f])
+            for p in range(2)
+        ]
         for f in range(4)
     ]
     for f in range(2):
@@ -118,25 +122,29 @@
             if f < 2:
                 copies[f + 2][p].start()
         for kb in range(4):
-            terms(kb, f, u, j_ref, k_ref, out_refs[kb])
-
-
-TERMS = jax.ShapeDtypeStruct((4, 4, 64, 256), BF)
+            k_ref = held_refs[f // 2]
+            terms(kb, f % 2, u, f, j_ref, k_ref, out_refs[kb])
+            for p in range(2):
+                for j in range(kb * 4, kb * 4 + 4):
+                    at = slice(j * 256, j * 256 + 256)
+                    turned_refs[f // 2][p, f % 2, at, :] = k_ref[p, f % 2, :, at].T
 
 
 def first_adjoint(place, table, data, kernel):
     return pl.pallas_call(
         first_kernel,
         in_specs=[SMEM, SMEM, HBM, HBM],
-        out_specs=[VMEM] * 5,
-        out_shape=[pltpu.VMEM(kernel.shape, BF)] + [TERMS] * 4,
+        out_specs=[VMEM] * 8,
+        out_shape=[pltpu.VMEM((2, 2, 256, 4096), BF)] * 2
+        + [pltpu.VMEM((2, 2, 4096, 256), BF)] * 2
+        + [jax.ShapeDtypeStruct((4, 4, 64, 256), BF)] * 4,
         scratch_shapes=[
             pltpu.VMEM(data.shape, F32),
             pltpu.SemaphoreType.DMA,
             pltpu.SemaphoreType.DMA((2, 4)),
         ],
         compiler_params=params(8),
-        cost_estimate=cost(4 << 30),
+        cost_estimate=cost(1 << 33),
         name="first_adjoint",
     )(
         place,
@@ -146,21 +154,24 @@
     )
 
 
-def adjoint_kernel(kbs, j_ref, u_ref, k_ref, *out_refs):
-    for f in range(4):
+TERMS = jax.ShapeDtypeStruct((4, 2, 64, 256), BF)
+
+
+def adjoint_kernel(j_ref, u_ref, k_ref, *out_refs):
+    for f in range(2):
         u = u_ref[f].astype(BF)
-        for kb, out_ref in zip(kbs, out_refs):
-            terms(kb, f, u, j_ref, k_ref, out_ref)
-
-
-def adjoint(table, u, kernel, kbs):
+        for kb in (2, 1, 3, 0):
+            terms(kb, f, u, f, j_ref, k_ref, out_refs[kb])
+
+
+def adjoint(table, u, kernel):
     return pl.pallas_call(
-        lambda *refs: adjoint_kernel(kbs, *refs),
+        adjoint_kernel,
         in_specs=[SMEM, VMEM, VMEM],
-        out_specs=[VMEM] * len(kbs),
-        out_shape=[TERMS] * len(kbs),
+        out_specs=[VMEM] * 4,
+        out_shape=[TERMS] * 4,
         compiler_params=params(8),
-        cost_estimate=cost(len(kbs) << 33),
+        cost_estimate=cost(1 << 31),
         name="adjoint",
     )(table, u, kernel)
 
@@ -170,53 +181,55 @@
     return v[:, :128] + v[:, 128:]
 
 
-def forward_kernel(kb, last, second, j_ref, x_ref, k_ref, *refs):
-    if kb > 0:
+def forward_kernel(kbs, first, last, second, early, j_ref, k_ref, *refs):
+    x_refs, refs = refs[: len(kbs)], refs[len(kbs) :]
+    if not first:
         before_ref, *refs = refs
     if second:
-        i0_ref, gg_ref, hh_ref, ii_ref, *refs = refs
+        i0_ref, *refs = refs
+    early_refs, refs = refs[:early], refs[early:]
     out_ref = refs[0]
 
     zero = jnp.zeros((1, 128), F32)
     sums = [zero, zero]
-    for f in range(4):
-        acc = jnp.zeros((256, 64), F32)
-        for ks in range(4):
-            cols = pl.ds(pl.multiple_of(j_ref[kb * 4 + ks] * 256, 256), 256)
-            x = x_ref[ks, f]
-            acc = acc + lax.dot_general(
-                k_ref[0, f, :, cols], x, NT_DIMS, preferred_element_type=F32
-            )
-            acc = acc + lax.dot_general(
-                k_ref[1, f, :, cols], swapped(x, -1), NT_DIMS, preferred_element_type=F32
-            )
-        out = acc.T
-        if kb > 0:
-            out = out + before_ref[f]
+    for f in range(2):
+        out = jnp.zeros((64, 256), F32) if first else before_ref[f]
+        for kb, x_ref in zip(kbs, x_refs):
+            for ks in range(4):
+                rows = pl.ds(pl.multiple_of(j_ref[kb * 4 + ks] * 256, 256), 256)
+                x = x_ref[ks, f]
+                out = out + jnp.dot(x, k_ref[0, f, rows, :], preferred_element_type=F32)
+                out = out + jnp.dot(
+                    swapped(x, -1), k_ref[1, f, rows, :], preferred_element_type=F32
+                )
         out_ref[f] = out
         if second:
             sums[0] = sums[0] + fold(i0_ref[f] * out)
         if last:
             sums[1] = sums[1] + fold(out * out)
-    if second:
-        rows = [gg_ref[0:1], hh_ref[0:2], ii_ref[0:1], *sums, zero, zero]
+    if early:
+        gg, hh, ii0, ii1, other = [ref[...] for ref in early_refs]
+        rows = [gg[0:1], hh[0:2], ii0[1:2] + ii1[1:2]]
+        rows += [other[0:1] + sums[0], other[1:2] + sums[1], zero, zero]
         refs[1][...] = jnp.concatenate(rows, axis=0)
     elif last:
-        refs[1][...] = jnp.broadcast_to(sums[1], (8, 128))
-
-
-def forward(kb, table, blocks, kernel, before=None, last=False, more=()):
-    inputs = (blocks, kernel) + (() if before is None else (before,)) + tuple(more)
-    out = [jax.ShapeDtypeStruct((4, 64, 256), F32)]
+        refs[1][...] = jnp.concatenate(sums + [jnp.zeros((6, 128), F32)], axis=0)
+
+
+def forward(kbs, table, kernel, blocks, before=None, last=False, i0=None, early=()):
+    inputs = [kernel, *blocks]
+    inputs += [a for a in (before, i0) if a is not None] + list(early)
+    out = [jax.ShapeDtypeStruct((2, 64, 256), F32)]
     if last:
         out.append(jax.ShapeDtypeStruct((8, 128), F32))
+    flags = (kbs, before is None, last, i0 is not None, len(early))
     return pl.pallas_call(
-        lambda *refs: forward_kernel(kb, last, len(more) > 0, *refs),
+        lambda *refs: forward_kernel(*flags, *refs),
         in_specs=[SMEM] + [VMEM] * len(inputs),
         out_specs=[VMEM] * len(out),
         out_shape=out,
         compiler_params=params(8),
-        cost_estimate=cost(1 << 33),
+        cost_estimate=cost(1 << 31),
         name="forward",
     )(table, *inputs)
 
@@ -332,7 +345,9 @@
     )(place, *blocks, *constants, *more)
 
 
-def last_kernel(place_ref, sum_ref, i0, i1, data_ref, g0, g0_got, h, h_got, model_ref, res_ref):
+def last_kernel(
+    place_ref, sum_ref, i0a, i0b, i1a, i1b, data_ref, g0, g0_got, h, h_got, model_ref, res_ref
+):
     core = place_ref[1]
     sums = jnp.sum(sum_ref[...], axis=1, keepdims=True)
     gg, gh, hh, ii, ij, jj = [sums[k : k + 1] for k in range(6)]
@@ -352,7 +367,8 @@
                 right = h[0, rows, :] if half == 0 else h_got[rows, :]
                 model_ref[p, f, at, :] = on_first * left - on_second * right
                 rows = slice(half * 32 + p * 16, half * 32 + p * 16 + 16)
-                change = on_first * i0[f, rows, :] - on_second * i1[f, rows, :]
+                i0, i1 = ((i0a, i1a), (i0b, i1b))[f // 2]
+                change = on_first * i0[f % 2, rows, :] - on_second * i1[f % 2, rows, :]
                 res_ref[p, f, at, :] = data_ref[p, f, at, :] - change
 
 
@@ -403,38 +419,53 @@
             out = out + part.astype(F32)
         return out.astype(BF)
 
-    def gather_terms(own):
+    def sum_big(own):
         got = [move(own[kb], along_big(kb)) for kb in (2, 1, 3)]
-        row = [summed([own[0][ks]] + [part[ks] for part in got]) for ks in range(4)]
+        return [summed([own[0][ks]] + [part[ks] for part in got]) for ks in range(4)]
+
+    def gather_terms(row):
         mine = summed([row[0]] + [move(row[ks], along_small(ks)) for ks in (2, 1, 3)])
         mine = mine.reshape(4, 2, 32, 256)
         mine = jnp.stack([mine[:, 0], move(mine[:, 1], other_core)]).reshape(256, 256)
         return [mine] + [move(mine, along_z(-k)) for k in (1, 2, 3)]
 
-    def image_of(shaped, *more):
+    def image_of(shaped, i0=(None, None), early=()):
         shaped = shaped.reshape(2, 4, 32, 256)
         shaped = jnp.stack([shaped[0], move(shaped[1], other_core)], axis=1).reshape(4, 64, 256)
-        row = jnp.stack([shaped] + [move(shaped, along_small(-ks)) for ks in (1, 2, 3)])
-        near = {kb: move(row, along_big(-kb)) for kb in (1, 3)}
-        (out,) = forward(0, table, row, held)
-        row, out = lax.optimization_barrier((row, out))
-        far = move(row, along_big(-2))
-        for kb in (1, 3):
-            (out,) = forward(kb, table, near[kb], held, out)
-        return forward(2, table, far, held, out, True, more)
+        row = [shaped] + [move(shaped, along_small(-ks)) for ks in (1, 2, 3)]
+        one, two = [jnp.stack([part[k : k + 2] for part in row]) for k in (0, 2)]
+        near = [move(one, along_big(-kb)) for kb in (1, 3)]
+        far = move(one, along_big(-2))
+        (out,) = forward((0,), table, turned[0], [one])
+        two, out = lax.optimization_barrier((two, out))
+        near_two = [move(two, along_big(-kb)) for kb in (1, 3)]
+        far_two = move(two, along_big(-2))
+        (out_two,) = forward((0,), table, turned[1], [two])
+        out, sums = forward((1, 3, 2), table, turned[0], near + [far], out, True, i0[0])
+        out_two, out = lax.optimization_barrier((out_two, out))
+        (out_two,) = forward((1, 3), table, turned[1], near_two, out_two)
+        if early:
+            early = (*early, sums)
+        out_two, sums_two = forward(
+            (2,), table, turned[1], [far_two], out_two, True, i0[1], early
+        )
+        return (out, out_two), (sums, sums_two)
 
     start = jnp.swapaxes(data, 2, 3)
-    held, *own = first_adjoint(place, table, start, kernel)
-    held = pltpu.with_memory_space_constraint(held, pltpu.VMEM)
-    g0, s0, gg = window(place, gather_terms(own), constants)
+    out = first_adjoint(place, table, start, kernel)
+    big = [pltpu.with_memory_space_constraint(t, pltpu.VMEM) for t in out[:4]]
+    held, turned, own = big[:2], big[2:], out[4:]
+    g0, s0, gg = window(place, gather_terms(sum_big(own)), constants)
     i0, ii = image_of(s0)
-    far = adjoint(table, i0, held, (2,))
-    rest = adjoint(table, i0, held, (0, 1, 3))
-    h, s1, hh = window(place, gather_terms([*rest[:2], far[0], rest[2]]), constants, g0)
-    i1, sums = image_of(s1, i0, gg, hh, ii)
+    rows = [lax.optimization_barrier(sum_big(adjoint(table, i0[k], held[k]))) for k in range(2)]
+    rows = [jnp.concatenate(pair) for pair in zip(*rows)]
+    h, s1, hh = window(place, gather_terms(rows), constants, g0)
+    i1, sums = image_of(s1, i0, (gg, hh, *ii))
     g0_got = move(g0[1], other_core)
     h_got = move(h[1], other_core)
-    model, residual = last(place, total(sums), i0, i1, start, g0, g0_got, h, h_got)
+    model, residual = last(
+        place, total(sums[1]), *i0, *i1, start, g0, g0_got, h, h_got
+    )
     return jnp.swapaxes(model, 2, 3), jnp.swapaxes(residual, 2, 3)
 
 

time: 186 us -> 181 us (0.973)
  waiting for transfers between devices: 85.3 us -> 66.1 us
  starting transfers between devices: 61.8 us -> 76.8 us
    ppermute x46 -> x55, waiting for transfers between devices: 85.3 us -> 66.1 us  [move(): return lax.ppermute(value, AXES, pairs)]
    ppermute x46 -> x55, starting transfers between devices: 61.8 us -> 76.8 us  [move(): return lax.ppermute(value, AXES, pairs)]
    pallas_call x10 -> x12, Pallas kernels: 19.1 us -> 16.7 us  [the longest x10 12.4 us: forward(): pl.pallas_call(lambda *refs: forward_kernel(*flags, *refs), in_specs=[SME...]
  transfers between devices with their start and end apart: 46 -> 55, of which waited for: 33 -> 32; matrix products, arithmetic and copies ran while one was open for 0% -> 0% of each run, Pallas kernels for 6% -> 9%
where the time goes in v3:
time: 181 us; the launch traced here: 180 us
  starting transfers between devices  76.8 us (42%)
  waiting for transfers between devices  66.1 us (37%)
  Pallas kernels  34 us (19%)
    ppermute x55, starting transfers between devices, move(): return lax.ppermute(value, AXES, pairs)  76.8 us
    ppermute x55, waiting for transfers between devices, move(): return lax.ppermute(value, AXES, pairs)  66.1 us
    pallas_call x10, Pallas kernels, forward(): pl.pallas_call(lambda *refs: forward_kernel(*flags, *refs), in_specs=[SME...  12.4 us
    pallas_call x1, Pallas kernels, first_adjoint(): pl.pallas_call(first_kernel, in_specs=[SMEM, SMEM, HBM, HBM], out_specs=[...  9.09 us
    pallas_call x2, Pallas kernels, window(): pl.pallas_call(lambda *refs: window_kernel(len(more) > 0, *refs), in_spec...  6.75 us
    pallas_call x2, Pallas kernels, adjoint(): pl.pallas_call(adjoint_kernel, in_specs=[SMEM, VMEM, VMEM], out_specs=[VM...  4.25 us
  transfers between devices with their start and end apart: 55, of which 32 were waited for; matrix products, arithmetic and copies ran while one was open for 0% of the time, Pallas kernels for 9%

profile of v3, /device:TPU:1, one launch (start us, length us, event | category | flops | bytes accessed | tf_op | source)
XLA Modules:
  0.0 179.5 jit_solution(9186536868635742508)
XLA Ops:
  0.8 9.1 %first_adjoint.1 = (bf16[2,2,256,4096]{3,2,1,0:T(8,128)(2,1)S(1)}, bf16[2,2,256,4096]{3,2,1,0:T(8,128)(2,1)S(1)}, bf16[2,2,4096,256]{3,2,1,0:T(8,128)(2,1)S(1)},...) custom-call(s32[2]{0:T(128)S(1)} %pad_add_fusion.place_ref.refs_0_, ...), custom_call_target="tpu_custom_call" | custom-call | flops 8589934592 | bytes 4194304 | tf_op jit(solution)/shard_map/first_adjoint/pallas_call | solution.py:134
  9.9 3.7 %collective-permute-start = (bf16[4,4,64,256]{3,2,1,0:T(8,128)(2,1)S(1)}, bf16[4,4,64,256]{3,2,1,0:T(8,128)(2,1)S(1)}, u32[]{:S(2)}, u32[]{:S(2)}) collective-permute-start(bf16[4,4,64,256]{3,2,1,0:T(8,128)(2,1)S(1)} %get-tuple-element.52), channel_id=1, source_target_pairs={{0,64},{1,17},{2,66},{3,19},{4,68},{5,21},{6,70},{7,23},{8,72},{9,... | collective-permute-start | bytes 1572872 | tf_op jit(solution)/shard_map/ppermute | solution.py:32
  13.8 2.4 %collective-permute-start.2 = (bf16[4,4,64,256]{3,2,1,0:T(8,128)(2,1)S(1)}, bf16[4,4,64,256]{3,2,1,0:T(8,128)(2,1)S(1)}, u32[]{:S(2)}, u32[]{:S(2)}) collective-permute-start(bf16[4,4,64,256]{3,2,1,0:T(8,128)(2,1)S(1)} %get-tuple-element.54), channel_id=1, source_target_pairs={{0,96},{1,25},{2,98},{3,27},{4,100},{5,29},{6,102},{7,31},{8,104},... | collective-permute-start | bytes 1572872 | tf_op jit(solution)/shard_map/ppermute | solution.py:32
  16.2 4.2 %collective-permute-done = bf16[4,4,64,256]{3,2,1,0:T(8,128)(2,1)S(1)} collective-permute-done((bf16[4,4,64,256]{3,2,1,0:T(8,128)(2,1)S(1)}, bf16[4,4,64,256]{3,2,1,0:T(8,128)(2,1)S(1)}, u32[]{:S(2)}, u32[]{:S(2)}) %collective-permute-start) | collective-permute-done | bytes 524320 | tf_op jit(solution)/shard_map/ppermute | solution.py:32
  20.5 5.6 %collective-permute-done.1 = bf16[4,4,64,256]{3,2,1,0:T(8,128)(2,1)S(1)} collective-permute-done((bf16[4,4,64,256]{3,2,1,0:T(8,128)(2,1)S(1)}, bf16[4,4,64,256]{3,2,1,0:T(8,128)(2,1)S(1)}, u32[]{:S(2)}, u32[]{:S(2)}) %collective-permute-start.1) | collective-permute-done | bytes 524320 | tf_op jit(solution)/shard_map/ppermute | solution.py:32
  26.6 3.0 %collective-permute-start.3 = (bf16[4,64,256]{2,1,0:T(8,128)(2,1)S(1)}, bf16[4,64,256]{2,1,0:T(8,128)(2,1)S(1)}, u32[]{:S(2)}, u32[]{:S(2)}) collective-permute-start(bf16[4,64,256]{2,1,0:T(8,128)(2,1)S(1)} %get-tuple-element.98), channel_id=1, source_target_pairs={{0,16},{1,65},{2,18},{3,67},{4,20},{5,69},{6,22},{7,71},{8,24},{9,... | collective-permute-start | bytes 393224 | tf_op jit(solution)/shard_map/ppermute | solution.py:32
  30.0 2.3 %collective-permute-start.5 = (bf16[4,64,256]{2,1,0:T(8,128)(2,1)S(1)}, bf16[4,64,256]{2,1,0:T(8,128)(2,1)S(1)}, u32[]{:S(2)}, u32[]{:S(2)}) collective-permute-start(bf16[4,64,256]{2,1,0:T(8,128)(2,1)S(1)} %get-tuple-element.99), channel_id=1, source_target_pairs={{0,24},{1,97},{2,26},{3,99},{4,28},{5,101},{6,30},{7,103},{8,0},{9... | collective-permute-start | bytes 393224 | tf_op jit(solution)/shard_map/ppermute | solution.py:32
  32.3 2.3 %collective-permute-done.4 = bf16[4,64,256]{2,1,0:T(8,128)(2,1)S(1)} collective-permute-done((bf16[4,64,256]{2,1,0:T(8,128)(2,1)S(1)}, bf16[4,64,256]{2,1,0:T(8,128)(2,1)S(1)}, u32[]{:S(2)}, u32[]{:S(2)}) %collective-permute-start.4) | collective-permute-done | bytes 131104 | tf_op jit(solution)/shard_map/ppermute | solution.py:32
  34.8 3.1 %collective-permute-start.6 = (bf16[4,32,256]{2,1,0:T(8,128)(2,1)S(1)}, bf16[4,32,256]{2,1,0:T(8,128)(2,1)S(1)}, u32[]{:S(2)}, u32[]{:S(2)}) collective-permute-start(bf16[4,32,256]{2,1,0:T(8,128)(2,1)S(1)} %get-tuple-element.132), channel_id=1, source_target_pairs={{0,1},{1,0},{2,3},{3,2},{4,5},{5,4},{6,7},{7,6},{8,9},{9,8},{10,11... | collective-permute-start | bytes 196616 | tf_op jit(solution)/shard_map/ppermute | solution.py:32
  38.8 3.8 %collective-permute-start.7 = (bf16[256,256]{1,0:T(8,128)(2,1)S(1)}, bf16[256,256]{1,0:T(8,128)(2,1)S(1)}, u32[]{:S(2)}, u32[]{:S(2)}) collective-permute-start(bf16[256,256]{1,0:T(8,128)(2,1)S(1)} %bitcast.105), channel_id=1, source_target_pairs={{0,6},{1,7},{2,0},{3,1},{4,2},{5,3},{6,4},{7,5},{8,14},{9,15},{10,... | collective-permute-start | bytes 393224 | tf_op jit(solution)/shard_map/ppermute | solution.py:32
  43.4 4.9 %collective-permute-done.7.refs_2_ = bf16[256,256]{1,0:T(8,128)(2,1)S(1)} collective-permute-done((bf16[256,256]{1,0:T(8,128)(2,1)S(1)}, bf16[256,256]{1,0:T(8,128)(2,1)S(1)}, u32[]{:S(2)}, u32[]{:S(2)}) %collective-permute-start.7) | collective-permute-done | bytes 131104 | tf_op jit(solution)/shard_map/ppermute | solution.py:32
  48.7 3.1 %collective-permute-done.9.refs_4_ = bf16[256,256]{1,0:T(8,128)(2,1)S(1)} collective-permute-done((bf16[256,256]{1,0:T(8,128)(2,1)S(1)}, bf16[256,256]{1,0:T(8,128)(2,1)S(1)}, u32[]{:S(2)}, u32[]{:S(2)}) %collective-permute-start.9) | collective-permute-done | bytes 131104 | tf_op jit(solution)/shard_map/ppermute | solution.py:32
  51.8 3.4 %window.2 = (f32[2,128,256]{2,1,0:T(8,128)S(1)}, bf16[2,128,256]{2,1,0:T(8,128)(2,1)S(1)}, f32[8,128]{1,0:T(8,128)S(1)}) custom-call(s32[2]{0:T(128)S(1)} %pad_add_fusion.place_ref.refs_0_, bf16[256,256]{1,0:T(8,128)(2,1)S(1)} %bitcast.108, bf16[256,256]{1,0:T(8,128)(2,1)S(1)} %collective-permute-done.7.refs_2_, ...), custom_call_target="tpu_custom_call" | custom-call | flops 1073741824 | bytes 4194304 | tf_op jit(solution)/shard_map/window/pallas_call | solution.py:331
  57.0 2.4 %collective-permute-start.11 = (bf16[4,64,256]{2,1,0:T(8,128)(2,1)S(1)}, bf16[4,64,256]{2,1,0:T(8,128)(2,1)S(1)}, u32[]{:S(2)}, u32[]{:S(2)}) collective-permute-start(bf16[4,64,256]{2,1,0:T(8,128)(2,1)S(1)} %bitcast.125), channel_id=1, source_target_pairs={{0,24},{1,97},{2,26},{3,99},{4,28},{5,101},{6,30},{7,103},{8,0},{9... | collective-permute-start | bytes 393224 | tf_op jit(solution)/shard_map/ppermute | solution.py:32
  60.1 2.6 %collective-permute-done.11 = bf16[4,64,256]{2,1,0:T(8,128)(2,1)S(1)} collective-permute-done((bf16[4,64,256]{2,1,0:T(8,128)(2,1)S(1)}, bf16[4,64,256]{2,1,0:T(8,128)(2,1)S(1)}, u32[]{:S(2)}, u32[]{:S(2)}) %collective-permute-start.11) | collective-permute-done | bytes 131104 | tf_op jit(solution)/shard_map/ppermute | solution.py:32
  62.7 2.1 %collective-permute-done.12 = bf16[4,64,256]{2,1,0:T(8,128)(2,1)S(1)} collective-permute-done((bf16[4,64,256]{2,1,0:T(8,128)(2,1)S(1)}, bf16[4,64,256]{2,1,0:T(8,128)(2,1)S(1)}, u32[]{:S(2)}, u32[]{:S(2)}) %collective-permute-start.12) | collective-permute-done | bytes 131104 | tf_op jit(solution)/shard_map/ppermute | solution.py:32
  64.9 1.6 collective-permute-done.13
  66.5 2.7 %collective-permute-start.14 = (bf16[4,2,64,256]{3,2,1,0:T(8,128)(2,1)S(1)}, bf16[4,2,64,256]{3,2,1,0:T(8,128)(2,1)S(1)}, u32[]{:S(2)}, u32[]{:S(2)}) collective-permute-start(bf16[4,2,64,256]{3,2,1,0:T(8,128)(2,1)S(1)} %pad_maximum_fusion.1.refs_2_), channel_id=1, source_target_pairs={{0,96},{1,25},{2,98},{3,27},{4,100},{5,29},{6,102},{7,31},{8,104},... | collective-permute-start | bytes 786440 | tf_op jit(solution)/shard_map/ppermute | solution.py:32
  74.7 1.8 collective-permute-start.20
  76.5 2.2 %collective-permute-done.15.refs_3_ = bf16[4,2,64,256]{3,2,1,0:T(8,128)(2,1)S(1)} collective-permute-done((bf16[4,2,64,256]{3,2,1,0:T(8,128)(2,1)S(1)}, bf16[4,2,64,256]{3,2,1,0:T(8,128)(2,1)S(1)}, u32[]{:S(2)}, u32[]{:S(2)}) %collective-permute-start.15) | collective-permute-done | bytes 262176 | tf_op jit(solution)/shard_map/ppermute | solution.py:32
  78.8 1.8 forward.12
  80.5 2.1 %adjoint.2 = (bf16[4,2,64,256]{3,2,1,0:T(8,128)(2,1)S(1)}, bf16[4,2,64,256]{3,2,1,0:T(8,128)(2,1)S(1)}, bf16[4,2,64,256]{3,2,1,0:T(8,128)(2,1)S(1)}, bf16[4,2,64,256]{3,2,1,0:T(8,128)(2,1)S(1)}) custom-call(s32[16]{0:T(128)S(1)} %fusion.24.j_ref.refs_0_, f32[2,64,256]{2,1,0:T(8,128)S(1)} %get-tuple-element.60.u_ref.refs_6_.i0a, ...), custom_call_target="tpu_custom_call" | custom-call | flops 2147483648 | bytes 4194304 | tf_op jit(solution)/shard_map/adjoint/pallas_call | solution.py:168
  83.5 2.2 %collective-permute-start.19 = (bf16[4,2,64,256]{3,2,1,0:T(8,128)(2,1)S(1)}, bf16[4,2,64,256]{3,2,1,0:T(8,128)(2,1)S(1)}, u32[]{:S(2)}, u32[]{:S(2)}) collective-permute-start(bf16[4,2,64,256]{3,2,1,0:T(8,128)(2,1)S(1)} %get-tuple-element.65), channel_id=1, source_target_pairs={{0,96},{1,25},{2,98},{3,27},{4,100},{5,29},{6,102},{7,31},{8,104},... | collective-permute-start | bytes 786440 | tf_op jit(solution)/shard_map/ppermute | solution.py:32
  88.1 2.1 %adjoint.3 = (bf16[4,2,64,256]{3,2,1,0:T(8,128)(2,1)S(1)}, bf16[4,2,64,256]{3,2,1,0:T(8,128)(2,1)S(1)}, bf16[4,2,64,256]{3,2,1,0:T(8,128)(2,1)S(1)}, bf16[4,2,64,256]{3,2,1,0:T(8,128)(2,1)S(1)}) custom-call(s32[16]{0:T(128)S(1)} %fusion.24.j_ref.refs_0_, f32[2,64,256]{2,1,0:T(8,128)S(1)} %get-tuple-element.68.u_ref.refs_4_.i0b, ...), custom_call_target="tpu_custom_call" | custom-call | flops 2147483648 | bytes 4194304 | tf_op jit(solution)/shard_map/adjoint/pallas_call | solution.py:168
  90.3 1.5 collective-permute-start.23
  91.8 2.7 %collective-permute-start.25 = (bf16[4,2,64,256]{3,2,1,0:T(8,128)(2,1)S(1)}, bf16[4,2,64,256]{3,2,1,0:T(8,128)(2,1)S(1)}, u32[]{:S(2)}, u32[]{:S(2)}) collective-permute-start(bf16[4,2,64,256]{3,2,1,0:T(8,128)(2,1)S(1)} %get-tuple-element.73), channel_id=1, source_target_pairs={{0,96},{1,25},{2,98},{3,27},{4,100},{5,29},{6,102},{7,31},{8,104},... | collective-permute-start | bytes 786440 | tf_op jit(solution)/shard_map/ppermute | solution.py:32
  94.7 2.5 %collective-permute-done.23 = bf16[4,2,64,256]{3,2,1,0:T(8,128)(2,1)S(1)} collective-permute-done((bf16[4,2,64,256]{3,2,1,0:T(8,128)(2,1)S(1)}, bf16[4,2,64,256]{3,2,1,0:T(8,128)(2,1)S(1)}, u32[]{:S(2)}, u32[]{:S(2)}) %collective-permute-start.23) | collective-permute-done | bytes 262176 | tf_op jit(solution)/shard_map/ppermute | solution.py:32
  97.2 3.0 %collective-permute-done.24 = bf16[4,2,64,256]{3,2,1,0:T(8,128)(2,1)S(1)} collective-permute-done((bf16[4,2,64,256]{3,2,1,0:T(8,128)(2,1)S(1)}, bf16[4,2,64,256]{3,2,1,0:T(8,128)(2,1)S(1)}, u32[]{:S(2)}, u32[]{:S(2)}) %collective-permute-start.24) | collective-permute-done | bytes 262176 | tf_op jit(solution)/shard_map/ppermute | solution.py:32
  101.7 2.2 %collective-permute-start.28 = (bf16[4,64,256]{2,1,0:T(8,128)(2,1)S(1)}, bf16[4,64,256]{2,1,0:T(8,128)(2,1)S(1)}, u32[]{:S(2)}, u32[]{:S(2)}) collective-permute-start(bf16[4,64,256]{2,1,0:T(8,128)(2,1)S(1)} %pad_maximum_fusion.9), channel_id=1, source_target_pairs={{0,24},{1,97},{2,26},{3,99},{4,28},{5,101},{6,30},{7,103},{8,0},{9... | collective-permute-start | bytes 393224 | tf_op jit(solution)/shard_map/ppermute | solution.py:32
  103.9 1.9 %collective-permute-done.26 = bf16[4,64,256]{2,1,0:T(8,128)(2,1)S(1)} collective-permute-done((bf16[4,64,256]{2,1,0:T(8,128)(2,1)S(1)}, bf16[4,64,256]{2,1,0:T(8,128)(2,1)S(1)}, u32[]{:S(2)}, u32[]{:S(2)}) %collective-permute-start.26) | collective-permute-done | bytes 131104 | tf_op jit(solution)/shard_map/ppermute | solution.py:32
  107.3 5.3 %collective-permute-start.29 = (bf16[4,32,256]{2,1,0:T(8,128)(2,1)S(1)}, bf16[4,32,256]{2,1,0:T(8,128)(2,1)S(1)}, u32[]{:S(2)}, u32[]{:S(2)}) collective-permute-start(bf16[4,32,256]{2,1,0:T(8,128)(2,1)S(1)} %get-tuple-element.120), channel_id=1, source_target_pairs={{0,1},{1,0},{2,3},{3,2},{4,5},{5,4},{6,7},{7,6},{8,9},{9,8},{10,11... | collective-permute-start | bytes 196616 | tf_op jit(solution)/shard_map/ppermute | solution.py:32
  115.0 3.3 %collective-permute-done.30.refs_2_ = bf16[256,256]{1,0:T(8,128)(2,1)S(1)} collective-permute-done((bf16[256,256]{1,0:T(8,128)(2,1)S(1)}, bf16[256,256]{1,0:T(8,128)(2,1)S(1)}, u32[]{:S(2)}, u32[]{:S(2)}) %collective-permute-start.30) | collective-permute-done | bytes 131104 | tf_op jit(solution)/shard_map/ppermute | solution.py:32
  118.3 1.8 %collective-permute-done.31.refs_3_ = bf16[256,256]{1,0:T(8,128)(2,1)S(1)} collective-permute-done((bf16[256,256]{1,0:T(8,128)(2,1)S(1)}, bf16[256,256]{1,0:T(8,128)(2,1)S(1)}, u32[]{:S(2)}, u32[]{:S(2)}) %collective-permute-start.31) | collective-permute-done | bytes 131104 | tf_op jit(solution)/shard_map/ppermute | solution.py:32
  120.1 3.8 %collective-permute-done.32.refs_4_ = bf16[256,256]{1,0:T(8,128)(2,1)S(1)} collective-permute-done((bf16[256,256]{1,0:T(8,128)(2,1)S(1)}, bf16[256,256]{1,0:T(8,128)(2,1)S(1)}, u32[]{:S(2)}, u32[]{:S(2)}) %collective-permute-start.32) | collective-permute-done | bytes 131104 | tf_op jit(solution)/shard_map/ppermute | solution.py:32
  123.9 3.4 %window.3 = (f32[2,128,256]{2,1,0:T(8,128)S(1)}, bf16[2,128,256]{2,1,0:T(8,128)(2,1)S(1)}, f32[8,128]{1,0:T(8,128)S(1)}) custom-call(s32[2]{0:T(128)S(1)} %pad_add_fusion.place_ref.refs_0_, bf16[256,256]{1,0:T(8,128)(2,1)S(1)} %bitcast.104, bf16[256,256]{1,0:T(8,128)(2,1)S(1)} %collective-permute-done.30.refs_2_, ...), custom_call_target="tpu_custom_call" | custom-call | flops 1073741824 | bytes 4194304 | tf_op jit(solution)/shard_map/window/pallas_call | solution.py:331
  128.8 3.2 %collective-permute-start.34 = (bf16[4,64,256]{2,1,0:T(8,128)(2,1)S(1)}, bf16[4,64,256]{2,1,0:T(8,128)(2,1)S(1)}, u32[]{:S(2)}, u32[]{:S(2)}) collective-permute-start(bf16[4,64,256]{2,1,0:T(8,128)(2,1)S(1)} %bitcast.128), channel_id=1, source_target_pairs={{0,24},{1,97},{2,26},{3,99},{4,28},{5,101},{6,30},{7,103},{8,0},{9... | collective-permute-start | bytes 393224 | tf_op jit(solution)/shard_map/ppermute | solution.py:32
  132.9 2.4 %collective-permute-done.34 = bf16[4,64,256]{2,1,0:T(8,128)(2,1)S(1)} collective-permute-done((bf16[4,64,256]{2,1,0:T(8,128)(2,1)S(1)}, bf16[4,64,256]{2,1,0:T(8,128)(2,1)S(1)}, u32[]{:S(2)}, u32[]{:S(2)}) %collective-permute-start.34) | collective-permute-done | bytes 131104 | tf_op jit(solution)/shard_map/ppermute | solution.py:32
  135.3 2.3 %collective-permute-done.35 = bf16[4,64,256]{2,1,0:T(8,128)(2,1)S(1)} collective-permute-done((bf16[4,64,256]{2,1,0:T(8,128)(2,1)S(1)}, bf16[4,64,256]{2,1,0:T(8,128)(2,1)S(1)}, u32[]{:S(2)}, u32[]{:S(2)}) %collective-permute-start.35) | collective-permute-done | bytes 131104 | tf_op jit(solution)/shard_map/ppermute | solution.py:32
  142.5 1.7 collective-permute-start.38
  145.7 1.8 collective-permute-start.37
  147.5 2.2 %collective-permute-done.41.refs_3_ = bf16[4,2,64,256]{3,2,1,0:T(8,128)(2,1)S(1)} collective-permute-done((bf16[4,2,64,256]{3,2,1,0:T(8,128)(2,1)S(1)}, bf16[4,2,64,256]{3,2,1,0:T(8,128)(2,1)S(1)}, u32[]{:S(2)}, u32[]{:S(2)}) %collective-permute-start.41) | collective-permute-done | bytes 262176 | tf_op jit(solution)/shard_map/ppermute | solution.py:32
  149.7 1.8 forward.17
  151.5 3.8 %collective-permute-done.39.refs_3_ = bf16[4,2,64,256]{3,2,1,0:T(8,128)(2,1)S(1)} collective-permute-done((bf16[4,2,64,256]{3,2,1,0:T(8,128)(2,1)S(1)}, bf16[4,2,64,256]{3,2,1,0:T(8,128)(2,1)S(1)}, u32[]{:S(2)}, u32[]{:S(2)}) %collective-permute-start.39) | collective-permute-done | bytes 262176 | tf_op jit(solution)/shard_map/ppermute | solution.py:32
  157.8 3.3 %collective-permute-start.43 = (f32[8,128]{1,0:T(8,128)S(1)}, f32[8,128]{1,0:T(8,128)S(1)}, u32[]{:S(2)}, u32[]{:S(2)}) collective-permute-start(f32[8,128]{1,0:T(8,128)S(1)} %get-tuple-element.92), channel_id=1, source_target_pairs={{0,1},{1,0},{2,3},{3,2},{4,5},{5,4},{6,7},{7,6},{8,9},{9,8},{10,11... | collective-permute-start | bytes 12296 | tf_op jit(solution)/shard_map/ppermute | solution.py:32
  166.9 2.2 %collective-permute-start.49 = (f32[8,128]{1,0:T(8,128)S(1)}, f32[8,128]{1,0:T(8,128)S(1)}, u32[]{:S(2)}, u32[]{:S(2)}) collective-permute-start(f32[8,128]{1,0:T(8,128)S(1)} %add_add_fusion.2), channel_id=1, source_target_pairs={{0,24},{1,97},{2,26},{3,99},{4,28},{5,101},{6,30},{7,103},{8,0},{9... | collective-permute-start | bytes 12296 | tf_op jit(solution)/shard_map/ppermute | solution.py:32
  169.2 2.6 %collective-permute-start.53 = (f32[128,256]{1,0:T(8,128)S(1)}, f32[128,256]{1,0:T(8,128)S(1)}, u32[]{:S(2)}, u32[]{:S(2)}) collective-permute-start(f32[128,256]{1,0:T(8,128)S(1)} %slice_bitcast_fusion.1), channel_id=1, source_target_pairs={{0,1},{1,0},{2,3},{3,2},{4,5},{5,4},{6,7},{7,6},{8,9},{9,8},{10,11... | collective-permute-start | bytes 393224 | tf_op jit(solution)/shard_map/ppermute | solution.py:32
  171.9 2.2 %collective-permute-start.51 = (f32[8,128]{1,0:T(8,128)S(1)}, f32[8,128]{1,0:T(8,128)S(1)}, u32[]{:S(2)}, u32[]{:S(2)}) collective-permute-start(f32[8,128]{1,0:T(8,128)S(1)} %add_add_fusion.1), channel_id=1, source_target_pairs={{0,64},{1,17},{2,66},{3,19},{4,68},{5,21},{6,70},{7,23},{8,72},{9,... | collective-permute-start | bytes 12296 | tf_op jit(solution)/shard_map/ppermute | solution.py:32
  174.1 2.0 %collective-permute-start.52 = (f32[8,128]{1,0:T(8,128)S(1)}, f32[8,128]{1,0:T(8,128)S(1)}, u32[]{:S(2)}, u32[]{:S(2)}) collective-permute-start(f32[8,128]{1,0:T(8,128)S(1)} %add_add_fusion.1), channel_id=1, source_target_pairs={{0,96},{1,25},{2,98},{3,27},{4,100},{5,29},{6,102},{7,31},{8,104},... | collective-permute-start | bytes 12296 | tf_op jit(solution)/shard_map/ppermute | solution.py:32
  (125 shorter events, 40.9 us)
Async XLA Ops:
  9.9 10.6 %collective-permute-start = (bf16[4,4,64,256]{3,2,1,0:T(8,128)(2,1)S(1)}, bf16[4,4,64,256]{3,2,1,0:T(8,128)(2,1)S(1)}, u32[]{:S(2)}, u32[]{:S(2)}) collective-permute-start(bf16[4,4,64,256]{3,2,1,0:T(8,128)(2,1)S(1)} %get-tuple-element.52), channel_id=1, source_target_pairs={{0,64},{1,17},{2,66},{3,19},{4,68},{5,21},{6,70},{7,23},{8,72},{9,... | collective-permute-start | bytes 1572872 | tf_op jit(solution)/shard_map/ppermute | solution.py:32
  13.6 12.5 %collective-permute-start.1 = (bf16[4,4,64,256]{3,2,1,0:T(8,128)(2,1)S(1)}, bf16[4,4,64,256]{3,2,1,0:T(8,128)(2,1)S(1)}, u32[]{:S(2)}, u32[]{:S(2)}) collective-permute-start(bf16[4,4,64,256]{3,2,1,0:T(8,128)(2,1)S(1)} %get-tuple-element.53), channel_id=1, source_target_pairs={{0,32},{1,9},{2,34},{3,11},{4,36},{5,13},{6,38},{7,15},{8,40},{9,1... | collective-permute-start | bytes 1572872 | tf_op jit(solution)/shard_map/ppermute | solution.py:32
  13.8 12.5 %collective-permute-start.2 = (bf16[4,4,64,256]{3,2,1,0:T(8,128)(2,1)S(1)}, bf16[4,4,64,256]{3,2,1,0:T(8,128)(2,1)S(1)}, u32[]{:S(2)}, u32[]{:S(2)}) collective-permute-start(bf16[4,4,64,256]{3,2,1,0:T(8,128)(2,1)S(1)} %get-tuple-element.54), channel_id=1, source_target_pairs={{0,96},{1,25},{2,98},{3,27},{4,100},{5,29},{6,102},{7,31},{8,104},... | collective-permute-start | bytes 1572872 | tf_op jit(solution)/shard_map/ppermute | solution.py:32
  26.6 5.7 %collective-permute-start.3 = (bf16[4,64,256]{2,1,0:T(8,128)(2,1)S(1)}, bf16[4,64,256]{2,1,0:T(8,128)(2,1)S(1)}, u32[]{:S(2)}, u32[]{:S(2)}) collective-permute-start(bf16[4,64,256]{2,1,0:T(8,128)(2,1)S(1)} %get-tuple-element.98), channel_id=1, source_target_pairs={{0,16},{1,65},{2,18},{3,67},{4,20},{5,69},{6,22},{7,71},{8,24},{9,... | collective-permute-start | bytes 393224 | tf_op jit(solution)/shard_map/ppermute | solution.py:32
  29.6 5.0 %collective-permute-start.4 = (bf16[4,64,256]{2,1,0:T(8,128)(2,1)S(1)}, bf16[4,64,256]{2,1,0:T(8,128)(2,1)S(1)}, u32[]{:S(2)}, u32[]{:S(2)}) collective-permute-start(bf16[4,64,256]{2,1,0:T(8,128)(2,1)S(1)} %get-tuple-element.100), channel_id=1, source_target_pairs={{0,8},{1,33},{2,10},{3,35},{4,12},{5,37},{6,14},{7,39},{8,16},{9,4... | collective-permute-start | bytes 393224 | tf_op jit(solution)/shard_map/ppermute | solution.py:32
  30.0 4.6 %collective-permute-start.5 = (bf16[4,64,256]{2,1,0:T(8,128)(2,1)S(1)}, bf16[4,64,256]{2,1,0:T(8,128)(2,1)S(1)}, u32[]{:S(2)}, u32[]{:S(2)}) collective-permute-start(bf16[4,64,256]{2,1,0:T(8,128)(2,1)S(1)} %get-tuple-element.99), channel_id=1, source_target_pairs={{0,24},{1,97},{2,26},{3,99},{4,28},{5,101},{6,30},{7,103},{8,0},{9... | collective-permute-start | bytes 393224 | tf_op jit(solution)/shard_map/ppermute | solution.py:32
  34.8 4.0 %collective-permute-start.6 = (bf16[4,32,256]{2,1,0:T(8,128)(2,1)S(1)}, bf16[4,32,256]{2,1,0:T(8,128)(2,1)S(1)}, u32[]{:S(2)}, u32[]{:S(2)}) collective-permute-start(bf16[4,32,256]{2,1,0:T(8,128)(2,1)S(1)} %get-tuple-element.132), channel_id=1, source_target_pairs={{0,1},{1,0},{2,3},{3,2},{4,5},{5,4},{6,7},{7,6},{8,9},{9,8},{10,11... | collective-permute-start | bytes 196616 | tf_op jit(solution)/shard_map/ppermute | solution.py:32
  38.8 9.5 %collective-permute-start.7 = (bf16[256,256]{1,0:T(8,128)(2,1)S(1)}, bf16[256,256]{1,0:T(8,128)(2,1)S(1)}, u32[]{:S(2)}, u32[]{:S(2)}) collective-permute-start(bf16[256,256]{1,0:T(8,128)(2,1)S(1)} %bitcast.105), channel_id=1, source_target_pairs={{0,6},{1,7},{2,0},{3,1},{4,2},{5,3},{6,4},{7,5},{8,14},{9,15},{10,... | collective-permute-start | bytes 393224 | tf_op jit(solution)/shard_map/ppermute | solution.py:32
  42.7 6.0 %collective-permute-start.8 = (bf16[256,256]{1,0:T(8,128)(2,1)S(1)}, bf16[256,256]{1,0:T(8,128)(2,1)S(1)}, u32[]{:S(2)}, u32[]{:S(2)}) collective-permute-start(bf16[256,256]{1,0:T(8,128)(2,1)S(1)} %bitcast.106), channel_id=1, source_target_pairs={{0,4},{1,5},{2,6},{3,7},{4,0},{5,1},{6,2},{7,3},{8,12},{9,13},{10,... | collective-permute-start | bytes 393224 | tf_op jit(solution)/shard_map/ppermute | solution.py:32
  42.7 9.1 %collective-permute-start.9 = (bf16[256,256]{1,0:T(8,128)(2,1)S(1)}, bf16[256,256]{1,0:T(8,128)(2,1)S(1)}, u32[]{:S(2)}, u32[]{:S(2)}) collective-permute-start(bf16[256,256]{1,0:T(8,128)(2,1)S(1)} %bitcast.107), channel_id=1, source_target_pairs={{0,2},{1,3},{2,4},{3,5},{4,6},{5,7},{6,0},{7,1},{8,10},{9,11},{10,... | collective-permute-start | bytes 393224 | tf_op jit(solution)/shard_map/ppermute | solution.py:32
  57.0 5.7 %collective-permute-start.11 = (bf16[4,64,256]{2,1,0:T(8,128)(2,1)S(1)}, bf16[4,64,256]{2,1,0:T(8,128)(2,1)S(1)}, u32[]{:S(2)}, u32[]{:S(2)}) collective-permute-start(bf16[4,64,256]{2,1,0:T(8,128)(2,1)S(1)} %bitcast.125), channel_id=1, source_target_pairs={{0,24},{1,97},{2,26},{3,99},{4,28},{5,101},{6,30},{7,103},{8,0},{9... | collective-permute-start | bytes 393224 | tf_op jit(solution)/shard_map/ppermute | solution.py:32
  59.4 5.4 %collective-permute-start.12 = (bf16[4,64,256]{2,1,0:T(8,128)(2,1)S(1)}, bf16[4,64,256]{2,1,0:T(8,128)(2,1)S(1)}, u32[]{:S(2)}, u32[]{:S(2)}) collective-permute-start(bf16[4,64,256]{2,1,0:T(8,128)(2,1)S(1)} %bitcast.126), channel_id=1, source_target_pairs={{0,16},{1,65},{2,18},{3,67},{4,20},{5,69},{6,22},{7,71},{8,24},{9,... | collective-permute-start | bytes 393224 | tf_op jit(solution)/shard_map/ppermute | solution.py:32
  59.9 6.5 %collective-permute-start.13 = (bf16[4,64,256]{2,1,0:T(8,128)(2,1)S(1)}, bf16[4,64,256]{2,1,0:T(8,128)(2,1)S(1)}, u32[]{:S(2)}, u32[]{:S(2)}) collective-permute-start(bf16[4,64,256]{2,1,0:T(8,128)(2,1)S(1)} %bitcast.127), channel_id=1, source_target_pairs={{0,8},{1,33},{2,10},{3,35},{4,12},{5,37},{6,14},{7,39},{8,16},{9,4... | collective-permute-start | bytes 393224 | tf_op jit(solution)/shard_map/ppermute | solution.py:32
  66.5 8.2 %collective-permute-start.14 = (bf16[4,2,64,256]{3,2,1,0:T(8,128)(2,1)S(1)}, bf16[4,2,64,256]{3,2,1,0:T(8,128)(2,1)S(1)}, u32[]{:S(2)}, u32[]{:S(2)}) collective-permute-start(bf16[4,2,64,256]{3,2,1,0:T(8,128)(2,1)S(1)} %pad_maximum_fusion.1.refs_2_), channel_id=1, source_target_pairs={{0,96},{1,25},{2,98},{3,27},{4,100},{5,29},{6,102},{7,31},{8,104},... | collective-permute-start | bytes 786440 | tf_op jit(solution)/shard_map/ppermute | solution.py:32
  69.2 9.5 %collective-permute-start.15 = (bf16[4,2,64,256]{3,2,1,0:T(8,128)(2,1)S(1)}, bf16[4,2,64,256]{3,2,1,0:T(8,128)(2,1)S(1)}, u32[]{:S(2)}, u32[]{:S(2)}) collective-permute-start(bf16[4,2,64,256]{3,2,1,0:T(8,128)(2,1)S(1)} %pad_maximum_fusion.1.refs_2_), channel_id=1, source_target_pairs={{0,32},{1,9},{2,34},{3,11},{4,36},{5,13},{6,38},{7,15},{8,40},{9,1... | collective-permute-start | bytes 786440 | tf_op jit(solution)/shard_map/ppermute | solution.py:32
  69.2 9.5 %collective-permute-start.16 = (bf16[4,2,64,256]{3,2,1,0:T(8,128)(2,1)S(1)}, bf16[4,2,64,256]{3,2,1,0:T(8,128)(2,1)S(1)}, u32[]{:S(2)}, u32[]{:S(2)}) collective-permute-start(bf16[4,2,64,256]{3,2,1,0:T(8,128)(2,1)S(1)} %pad_maximum_fusion.1.refs_2_), channel_id=1, source_target_pairs={{0,64},{1,17},{2,66},{3,19},{4,68},{5,21},{6,70},{7,23},{8,72},{9,... | collective-permute-start | bytes 786440 | tf_op jit(solution)/shard_map/ppermute | solution.py:32
  71.6 12.0 %collective-permute-start.21 = (bf16[4,2,64,256]{3,2,1,0:T(8,128)(2,1)S(1)}, bf16[4,2,64,256]{3,2,1,0:T(8,128)(2,1)S(1)}, u32[]{:S(2)}, u32[]{:S(2)}) collective-permute-start(bf16[4,2,64,256]{3,2,1,0:T(8,128)(2,1)S(1)} %pad_maximum_fusion.refs_2_), channel_id=1, source_target_pairs={{0,96},{1,25},{2,98},{3,27},{4,100},{5,29},{6,102},{7,31},{8,104},... | collective-permute-start | bytes 786440 | tf_op jit(solution)/shard_map/ppermute | solution.py:32
  73.0 12.7 %collective-permute-start.22 = (bf16[4,2,64,256]{3,2,1,0:T(8,128)(2,1)S(1)}, bf16[4,2,64,256]{3,2,1,0:T(8,128)(2,1)S(1)}, u32[]{:S(2)}, u32[]{:S(2)}) collective-permute-start(bf16[4,2,64,256]{3,2,1,0:T(8,128)(2,1)S(1)} %pad_maximum_fusion.refs_2_), channel_id=1, source_target_pairs={{0,32},{1,9},{2,34},{3,11},{4,36},{5,13},{6,38},{7,15},{8,40},{9,1... | collective-permute-start | bytes 786440 | tf_op jit(solution)/shard_map/ppermute | solution.py:32
  74.7 12.4 %collective-permute-start.20 = (bf16[4,2,64,256]{3,2,1,0:T(8,128)(2,1)S(1)}, bf16[4,2,64,256]{3,2,1,0:T(8,128)(2,1)S(1)}, u32[]{:S(2)}, u32[]{:S(2)}) collective-permute-start(bf16[4,2,64,256]{3,2,1,0:T(8,128)(2,1)S(1)} %pad_maximum_fusion.refs_2_), channel_id=1, source_target_pairs={{0,64},{1,17},{2,66},{3,19},{4,68},{5,21},{6,70},{7,23},{8,72},{9,... | collective-permute-start | bytes 786440 | tf_op jit(solution)/shard_map/ppermute | solution.py:32
  82.7 9.2 %collective-permute-start.17 = (bf16[4,2,64,256]{3,2,1,0:T(8,128)(2,1)S(1)}, bf16[4,2,64,256]{3,2,1,0:T(8,128)(2,1)S(1)}, u32[]{:S(2)}, u32[]{:S(2)}) collective-permute-start(bf16[4,2,64,256]{3,2,1,0:T(8,128)(2,1)S(1)} %get-tuple-element.63), channel_id=1, source_target_pairs={{0,64},{1,17},{2,66},{3,19},{4,68},{5,21},{6,70},{7,23},{8,72},{9,... | collective-permute-start | bytes 786440 | tf_op jit(solution)/shard_map/ppermute | solution.py:32
  83.0 11.5 %collective-permute-start.18 = (bf16[4,2,64,256]{3,2,1,0:T(8,128)(2,1)S(1)}, bf16[4,2,64,256]{3,2,1,0:T(8,128)(2,1)S(1)}, u32[]{:S(2)}, u32[]{:S(2)}) collective-permute-start(bf16[4,2,64,256]{3,2,1,0:T(8,128)(2,1)S(1)} %get-tuple-element.64), channel_id=1, source_target_pairs={{0,32},{1,9},{2,34},{3,11},{4,36},{5,13},{6,38},{7,15},{8,40},{9,1... | collective-permute-start | bytes 786440 | tf_op jit(solution)/shard_map/ppermute | solution.py:32
  83.5 11.0 %collective-permute-start.19 = (bf16[4,2,64,256]{3,2,1,0:T(8,128)(2,1)S(1)}, bf16[4,2,64,256]{3,2,1,0:T(8,128)(2,1)S(1)}, u32[]{:S(2)}, u32[]{:S(2)}) collective-permute-start(bf16[4,2,64,256]{3,2,1,0:T(8,128)(2,1)S(1)} %get-tuple-element.65), channel_id=1, source_target_pairs={{0,96},{1,25},{2,98},{3,27},{4,100},{5,29},{6,102},{7,31},{8,104},... | collective-permute-start | bytes 786440 | tf_op jit(solution)/shard_map/ppermute | solution.py:32
  90.3 6.9 %collective-permute-start.23 = (bf16[4,2,64,256]{3,2,1,0:T(8,128)(2,1)S(1)}, bf16[4,2,64,256]{3,2,1,0:T(8,128)(2,1)S(1)}, u32[]{:S(2)}, u32[]{:S(2)}) collective-permute-start(bf16[4,2,64,256]{3,2,1,0:T(8,128)(2,1)S(1)} %get-tuple-element.71), channel_id=1, source_target_pairs={{0,64},{1,17},{2,66},{3,19},{4,68},{5,21},{6,70},{7,23},{8,72},{9,... | collective-permute-start | bytes 786440 | tf_op jit(solution)/shard_map/ppermute | solution.py:32
  91.8 8.4 %collective-permute-start.24 = (bf16[4,2,64,256]{3,2,1,0:T(8,128)(2,1)S(1)}, bf16[4,2,64,256]{3,2,1,0:T(8,128)(2,1)S(1)}, u32[]{:S(2)}, u32[]{:S(2)}) collective-permute-start(bf16[4,2,64,256]{3,2,1,0:T(8,128)(2,1)S(1)} %get-tuple-element.72), channel_id=1, source_target_pairs={{0,32},{1,9},{2,34},{3,11},{4,36},{5,13},{6,38},{7,15},{8,40},{9,1... | collective-permute-start | bytes 786440 | tf_op jit(solution)/shard_map/ppermute | solution.py:32
  91.8 8.4 %collective-permute-start.25 = (bf16[4,2,64,256]{3,2,1,0:T(8,128)(2,1)S(1)}, bf16[4,2,64,256]{3,2,1,0:T(8,128)(2,1)S(1)}, u32[]{:S(2)}, u32[]{:S(2)}) collective-permute-start(bf16[4,2,64,256]{3,2,1,0:T(8,128)(2,1)S(1)} %get-tuple-element.73), channel_id=1, source_target_pairs={{0,96},{1,25},{2,98},{3,27},{4,100},{5,29},{6,102},{7,31},{8,104},... | collective-permute-start | bytes 786440 | tf_op jit(solution)/shard_map/ppermute | solution.py:32
  100.4 5.5 %collective-permute-start.26 = (bf16[4,64,256]{2,1,0:T(8,128)(2,1)S(1)}, bf16[4,64,256]{2,1,0:T(8,128)(2,1)S(1)}, u32[]{:S(2)}, u32[]{:S(2)}) collective-permute-start(bf16[4,64,256]{2,1,0:T(8,128)(2,1)S(1)} %pad_maximum_fusion.7), channel_id=1, source_target_pairs={{0,16},{1,65},{2,18},{3,67},{4,20},{5,69},{6,22},{7,71},{8,24},{9,... | collective-permute-start | bytes 393224 | tf_op jit(solution)/shard_map/ppermute | solution.py:32
  101.1 6.1 %collective-permute-start.27 = (bf16[4,64,256]{2,1,0:T(8,128)(2,1)S(1)}, bf16[4,64,256]{2,1,0:T(8,128)(2,1)S(1)}, u32[]{:S(2)}, u32[]{:S(2)}) collective-permute-start(bf16[4,64,256]{2,1,0:T(8,128)(2,1)S(1)} %pad_maximum_fusion.8), channel_id=1, source_target_pairs={{0,8},{1,33},{2,10},{3,35},{4,12},{5,37},{6,14},{7,39},{8,16},{9,4... | collective-permute-start | bytes 393224 | tf_op jit(solution)/shard_map/ppermute | solution.py:32
  101.7 5.5 %collective-permute-start.28 = (bf16[4,64,256]{2,1,0:T(8,128)(2,1)S(1)}, bf16[4,64,256]{2,1,0:T(8,128)(2,1)S(1)}, u32[]{:S(2)}, u32[]{:S(2)}) collective-permute-start(bf16[4,64,256]{2,1,0:T(8,128)(2,1)S(1)} %pad_maximum_fusion.9), channel_id=1, source_target_pairs={{0,24},{1,97},{2,26},{3,99},{4,28},{5,101},{6,30},{7,103},{8,0},{9... | collective-permute-start | bytes 393224 | tf_op jit(solution)/shard_map/ppermute | solution.py:32
  107.3 6.2 %collective-permute-start.29 = (bf16[4,32,256]{2,1,0:T(8,128)(2,1)S(1)}, bf16[4,32,256]{2,1,0:T(8,128)(2,1)S(1)}, u32[]{:S(2)}, u32[]{:S(2)}) collective-permute-start(bf16[4,32,256]{2,1,0:T(8,128)(2,1)S(1)} %get-tuple-element.120), channel_id=1, source_target_pairs={{0,1},{1,0},{2,3},{3,2},{4,5},{5,4},{6,7},{7,6},{8,9},{9,8},{10,11... | collective-permute-start | bytes 196616 | tf_op jit(solution)/shard_map/ppermute | solution.py:32
  113.5 4.8 %collective-permute-start.30 = (bf16[256,256]{1,0:T(8,128)(2,1)S(1)}, bf16[256,256]{1,0:T(8,128)(2,1)S(1)}, u32[]{:S(2)}, u32[]{:S(2)}) collective-permute-start(bf16[256,256]{1,0:T(8,128)(2,1)S(1)} %bitcast.101), channel_id=1, source_target_pairs={{0,6},{1,7},{2,0},{3,1},{4,2},{5,3},{6,4},{7,5},{8,14},{9,15},{10,... | collective-permute-start | bytes 393224 | tf_op jit(solution)/shard_map/ppermute | solution.py:32
  114.2 5.9 %collective-permute-start.31 = (bf16[256,256]{1,0:T(8,128)(2,1)S(1)}, bf16[256,256]{1,0:T(8,128)(2,1)S(1)}, u32[]{:S(2)}, u32[]{:S(2)}) collective-permute-start(bf16[256,256]{1,0:T(8,128)(2,1)S(1)} %bitcast.102), channel_id=1, source_target_pairs={{0,4},{1,5},{2,6},{3,7},{4,0},{5,1},{6,2},{7,3},{8,12},{9,13},{10,... | collective-permute-start | bytes 393224 | tf_op jit(solution)/shard_map/ppermute | solution.py:32
  114.2 9.7 %collective-permute-start.32 = (bf16[256,256]{1,0:T(8,128)(2,1)S(1)}, bf16[256,256]{1,0:T(8,128)(2,1)S(1)}, u32[]{:S(2)}, u32[]{:S(2)}) collective-permute-start(bf16[256,256]{1,0:T(8,128)(2,1)S(1)} %bitcast.103), channel_id=1, source_target_pairs={{0,2},{1,3},{2,4},{3,5},{4,6},{5,7},{6,0},{7,1},{8,10},{9,11},{10,... | collective-permute-start | bytes 393224 | tf_op jit(solution)/shard_map/ppermute | solution.py:32
  128.8 6.5 %collective-permute-start.34 = (bf16[4,64,256]{2,1,0:T(8,128)(2,1)S(1)}, bf16[4,64,256]{2,1,0:T(8,128)(2,1)S(1)}, u32[]{:S(2)}, u32[]{:S(2)}) collective-permute-start(bf16[4,64,256]{2,1,0:T(8,128)(2,1)S(1)} %bitcast.128), channel_id=1, source_target_pairs={{0,24},{1,97},{2,26},{3,99},{4,28},{5,101},{6,30},{7,103},{8,0},{9... | collective-permute-start | bytes 393224 | tf_op jit(solution)/shard_map/ppermute | solution.py:32
  132.0 5.7 %collective-permute-start.35 = (bf16[4,64,256]{2,1,0:T(8,128)(2,1)S(1)}, bf16[4,64,256]{2,1,0:T(8,128)(2,1)S(1)}, u32[]{:S(2)}, u32[]{:S(2)}) collective-permute-start(bf16[4,64,256]{2,1,0:T(8,128)(2,1)S(1)} %bitcast.129), channel_id=1, source_target_pairs={{0,16},{1,65},{2,18},{3,67},{4,20},{5,69},{6,22},{7,71},{8,24},{9,... | collective-permute-start | bytes 393224 | tf_op jit(solution)/shard_map/ppermute | solution.py:32
  132.0 6.7 %collective-permute-start.36 = (bf16[4,64,256]{2,1,0:T(8,128)(2,1)S(1)}, bf16[4,64,256]{2,1,0:T(8,128)(2,1)S(1)}, u32[]{:S(2)}, u32[]{:S(2)}) collective-permute-start(bf16[4,64,256]{2,1,0:T(8,128)(2,1)S(1)} %bitcast.130), channel_id=1, source_target_pairs={{0,8},{1,33},{2,10},{3,35},{4,12},{5,37},{6,14},{7,39},{8,16},{9,4... | collective-permute-start | bytes 393224 | tf_op jit(solution)/shard_map/ppermute | solution.py:32
  138.7 6.9 %collective-permute-start.40 = (bf16[4,2,64,256]{3,2,1,0:T(8,128)(2,1)S(1)}, bf16[4,2,64,256]{3,2,1,0:T(8,128)(2,1)S(1)}, u32[]{:S(2)}, u32[]{:S(2)}) collective-permute-start(bf16[4,2,64,256]{3,2,1,0:T(8,128)(2,1)S(1)} %pad_maximum_fusion.3.refs_2_), channel_id=1, source_target_pairs={{0,96},{1,25},{2,98},{3,27},{4,100},{5,29},{6,102},{7,31},{8,104},... | collective-permute-start | bytes 786440 | tf_op jit(solution)/shard_map/ppermute | solution.py:32
  140.1 9.5 %collective-permute-start.41 = (bf16[4,2,64,256]{3,2,1,0:T(8,128)(2,1)S(1)}, bf16[4,2,64,256]{3,2,1,0:T(8,128)(2,1)S(1)}, u32[]{:S(2)}, u32[]{:S(2)}) collective-permute-start(bf16[4,2,64,256]{3,2,1,0:T(8,128)(2,1)S(1)} %pad_maximum_fusion.3.refs_2_), channel_id=1, source_target_pairs={{0,32},{1,9},{2,34},{3,11},{4,36},{5,13},{6,38},{7,15},{8,40},{9,1... | collective-permute-start | bytes 786440 | tf_op jit(solution)/shard_map/ppermute | solution.py:32
  140.3 9.4 %collective-permute-start.42 = (bf16[4,2,64,256]{3,2,1,0:T(8,128)(2,1)S(1)}, bf16[4,2,64,256]{3,2,1,0:T(8,128)(2,1)S(1)}, u32[]{:S(2)}, u32[]{:S(2)}) collective-permute-start(bf16[4,2,64,256]{3,2,1,0:T(8,128)(2,1)S(1)} %pad_maximum_fusion.3.refs_2_), channel_id=1, source_target_pairs={{0,64},{1,17},{2,66},{3,19},{4,68},{5,21},{6,70},{7,23},{8,72},{9,... | collective-permute-start | bytes 786440 | tf_op jit(solution)/shard_map/ppermute | solution.py:32
  142.5 9.0 %collective-permute-start.38 = (bf16[4,2,64,256]{3,2,1,0:T(8,128)(2,1)S(1)}, bf16[4,2,64,256]{3,2,1,0:T(8,128)(2,1)S(1)}, u32[]{:S(2)}, u32[]{:S(2)}) collective-permute-start(bf16[4,2,64,256]{3,2,1,0:T(8,128)(2,1)S(1)} %pad_maximum_fusion.2.refs_2_), channel_id=1, source_target_pairs={{0,96},{1,25},{2,98},{3,27},{4,100},{5,29},{6,102},{7,31},{8,104},... | collective-permute-start | bytes 786440 | tf_op jit(solution)/shard_map/ppermute | solution.py:32
  144.2 11.1 %collective-permute-start.39 = (bf16[4,2,64,256]{3,2,1,0:T(8,128)(2,1)S(1)}, bf16[4,2,64,256]{3,2,1,0:T(8,128)(2,1)S(1)}, u32[]{:S(2)}, u32[]{:S(2)}) collective-permute-start(bf16[4,2,64,256]{3,2,1,0:T(8,128)(2,1)S(1)} %pad_maximum_fusion.2.refs_2_), channel_id=1, source_target_pairs={{0,32},{1,9},{2,34},{3,11},{4,36},{5,13},{6,38},{7,15},{8,40},{9,1... | collective-permute-start | bytes 786440 | tf_op jit(solution)/shard_map/ppermute | solution.py:32
  145.7 11.0 %collective-permute-start.37 = (bf16[4,2,64,256]{3,2,1,0:T(8,128)(2,1)S(1)}, bf16[4,2,64,256]{3,2,1,0:T(8,128)(2,1)S(1)}, u32[]{:S(2)}, u32[]{:S(2)}) collective-permute-start(bf16[4,2,64,256]{3,2,1,0:T(8,128)(2,1)S(1)} %pad_maximum_fusion.2.refs_2_), channel_id=1, source_target_pairs={{0,64},{1,17},{2,66},{3,19},{4,68},{5,21},{6,70},{7,23},{8,72},{9,... | collective-permute-start | bytes 786440 | tf_op jit(solution)/shard_map/ppermute | solution.py:32
  157.8 4.1 %collective-permute-start.43 = (f32[8,128]{1,0:T(8,128)S(1)}, f32[8,128]{1,0:T(8,128)S(1)}, u32[]{:S(2)}, u32[]{:S(2)}) collective-permute-start(f32[8,128]{1,0:T(8,128)S(1)} %get-tuple-element.92), channel_id=1, source_target_pairs={{0,1},{1,0},{2,3},{3,2},{4,5},{5,4},{6,7},{7,6},{8,9},{9,8},{10,11... | collective-permute-start | bytes 12296 | tf_op jit(solution)/shard_map/ppermute | solution.py:32
  166.5 5.3 %collective-permute-start.47 = (f32[8,128]{1,0:T(8,128)S(1)}, f32[8,128]{1,0:T(8,128)S(1)}, u32[]{:S(2)}, u32[]{:S(2)}) collective-permute-start(f32[8,128]{1,0:T(8,128)S(1)} %add_add_fusion.2), channel_id=1, source_target_pairs={{0,8},{1,33},{2,10},{3,35},{4,12},{5,37},{6,14},{7,39},{8,16},{9,4... | collective-permute-start | bytes 12296 | tf_op jit(solution)/shard_map/ppermute | solution.py:32
  166.5 5.3 %collective-permute-start.48 = (f32[8,128]{1,0:T(8,128)S(1)}, f32[8,128]{1,0:T(8,128)S(1)}, u32[]{:S(2)}, u32[]{:S(2)}) collective-permute-start(f32[8,128]{1,0:T(8,128)S(1)} %add_add_fusion.2), channel_id=1, source_target_pairs={{0,16},{1,65},{2,18},{3,67},{4,20},{5,69},{6,22},{7,71},{8,24},{9,... | collective-permute-start | bytes 12296 | tf_op jit(solution)/shard_map/ppermute | solution.py:32
  166.9 4.9 %collective-permute-start.49 = (f32[8,128]{1,0:T(8,128)S(1)}, f32[8,128]{1,0:T(8,128)S(1)}, u32[]{:S(2)}, u32[]{:S(2)}) collective-permute-start(f32[8,128]{1,0:T(8,128)S(1)} %add_add_fusion.2), channel_id=1, source_target_pairs={{0,24},{1,97},{2,26},{3,99},{4,28},{5,101},{6,30},{7,103},{8,0},{9... | collective-permute-start | bytes 12296 | tf_op jit(solution)/shard_map/ppermute | solution.py:32
  169.2 7.9 %collective-permute-start.53 = (f32[128,256]{1,0:T(8,128)S(1)}, f32[128,256]{1,0:T(8,128)S(1)}, u32[]{:S(2)}, u32[]{:S(2)}) collective-permute-start(f32[128,256]{1,0:T(8,128)S(1)} %slice_bitcast_fusion.1), channel_id=1, source_target_pairs={{0,1},{1,0},{2,3},{3,2},{4,5},{5,4},{6,7},{7,6},{8,9},{9,8},{10,11... | collective-permute-start | bytes 393224 | tf_op jit(solution)/shard_map/ppermute | solution.py:32
  171.8 5.2 %collective-permute-start.50 = (f32[8,128]{1,0:T(8,128)S(1)}, f32[8,128]{1,0:T(8,128)S(1)}, u32[]{:S(2)}, u32[]{:S(2)}) collective-permute-start(f32[8,128]{1,0:T(8,128)S(1)} %add_add_fusion.1), channel_id=1, source_target_pairs={{0,32},{1,9},{2,34},{3,11},{4,36},{5,13},{6,38},{7,15},{8,40},{9,1... | collective-permute-start | bytes 12296 | tf_op jit(solution)/shard_map/ppermute | solution.py:32
  171.9 5.1 %collective-permute-start.51 = (f32[8,128]{1,0:T(8,128)S(1)}, f32[8,128]{1,0:T(8,128)S(1)}, u32[]{:S(2)}, u32[]{:S(2)}) collective-permute-start(f32[8,128]{1,0:T(8,128)S(1)} %add_add_fusion.1), channel_id=1, source_target_pairs={{0,64},{1,17},{2,66},{3,19},{4,68},{5,21},{6,70},{7,23},{8,72},{9,... | collective-permute-start | bytes 12296 | tf_op jit(solution)/shard_map/ppermute | solution.py:32
  (11 other events, 184.5 us)

commit v4 on v3

--- a/solution.py
+++ b/solution.py
@@ -11,6 +11,7 @@
 NT = 1024
 F = 32
 AXES = ("rcv", "freq")
+OFFSETS = (0, 2, 1, 3)
 BF = jnp.bfloat16
 F32 = jnp.float32
 VMEM = pl.BlockSpec(memory_space=pltpu.VMEM)
@@ -253,7 +254,7 @@
     def swap(half):
         return half + core - 2 * half * core
 
-    for k, a in enumerate((a0, a1, a2, a3)):
+    for k, a in zip(OFFSETS, (a0, a1, a2, a3)):
         for half in range(2):
             at = (lax.rem(z + k, 4) * 2 + swap(half)) * size
             rows = pl.ds(pl.multiple_of(at, size), size)
@@ -388,7 +389,7 @@
 def total(values):
     values = values + move(values, other_core)
     for axis in (along_z, along_small, along_big):
-        values = values + move(values, axis(1)) + move(values, axis(2)) + move(values, axis(3))
+        values = values + move(values, axis(2)) + move(values, axis(1)) + move(values, axis(3))
     return values
 
 
@@ -398,7 +399,7 @@
     yy, xx, zz, core = rcv // 4, rcv % 4, freq // 2, freq % 2
     place = jnp.stack([zz, core]).astype(jnp.int32)
     far = jnp.arange(16, dtype=jnp.int32) // 4
-    near = jnp.arange(16, dtype=jnp.int32) % 4
+    near = jnp.asarray(np.array(OFFSETS * 4, np.int32))
     off_y = jnp.where(core == 0, far, near)
     off_x = jnp.where(core == 0, near, far)
     table = (yy + off_y) % 4 * 4 + (xx + off_x) % 4
@@ -424,15 +425,15 @@
         return [summed([own[0][ks]] + [part[ks] for part in got]) for ks in range(4)]
 
     def gather_terms(row):
-        mine = summed([row[0]] + [move(row[ks], along_small(ks)) for ks in (2, 1, 3)])
+        mine = summed([row[0]] + [move(row[n], along_small(OFFSETS[n])) for n in (1, 2, 3)])
         mine = mine.reshape(4, 2, 32, 256)
         mine = jnp.stack([mine[:, 0], move(mine[:, 1], other_core)]).reshape(256, 256)
-        return [mine] + [move(mine, along_z(-k)) for k in (1, 2, 3)]
+        return [mine] + [move(mine, along_z(-k)) for k in OFFSETS[1:]]
 
     def image_of(shaped, i0=(None, None), early=()):
         shaped = shaped.reshape(2, 4, 32, 256)
         shaped = jnp.stack([shaped[0], move(shaped[1], other_core)], axis=1).reshape(4, 64, 256)
-        row = [shaped] + [move(shaped, along_small(-ks)) for ks in (1, 2, 3)]
+        row = [shaped] + [move(shaped, along_small(-ks)) for ks in OFFSETS[1:]]
         one, two = [jnp.stack([part[k : k + 2] for part in row]) for k in (0, 2)]
         near = [move(one, along_big(-kb)) for kb in (1, 3)]
         far = move(one, along_big(-2))
@@ -443,12 +444,13 @@
         (out_two,) = forward((0,), table, turned[1], [two])
         out, sums = forward((1, 3, 2), table, turned[0], near + [far], out, True, i0[0])
         out_two, out = lax.optimization_barrier((out_two, out))
-        (out_two,) = forward((1, 3), table, turned[1], near_two, out_two)
         if early:
             early = (*early, sums)
-        out_two, sums_two = forward(
-            (2,), table, turned[1], [far_two], out_two, True, i0[1], early
-        )
+            (out_two,) = forward((1, 3), table, turned[1], near_two, out_two)
+            kbs, blocks = (2,), [far_two]
+        else:
+            kbs, blocks = (1, 3, 2), [*near_two, far_two]
+        out_two, sums_two = forward(kbs, table, turned[1], blocks, out_two, True, i0[1], early)
         return (out, out_two), (sums, sums_two)
 
     start = jnp.swapaxes(data, 2, 3)

time: 181 us -> 177 us (0.978)
  waiting for transfers between devices: 66.1 us -> 56.8 us
  starting transfers between devices: 76.8 us -> 83.6 us
    ppermute x55, waiting for transfers between devices: 66.1 us -> 56.8 us  [move(): return lax.ppermute(value, AXES, pairs)]
    ppermute x55, starting transfers between devices: 76.8 us -> 83.6 us  [move(): return lax.ppermute(value, AXES, pairs)]
    pallas_call x10 -> x9, Pallas kernels: 12.4 us -> 11.8 us  [forward(): pl.pallas_call(lambda *refs: forward_kernel(*flags, *refs), in_specs=[SME...]
  transfers between devices with their start and end apart: 55 -> 55, of which waited for: 32 -> 29; matrix products, arithmetic and copies ran while one was open for 0% -> 0% of each run, Pallas kernels for 9% -> 8%
where the time goes in v4:
time: 177 us
  starting transfers between devices  83.6 us (47%)
  waiting for transfers between devices  56.8 us (32%)
  Pallas kernels  33.4 us (19%)
  other arithmetic  1.99 us (1%)
    ppermute x55, starting transfers between devices, move(): return lax.ppermute(value, AXES, pairs)  83.6 us
    ppermute x55, waiting for transfers between devices, move(): return lax.ppermute(value, AXES, pairs)  56.8 us
    pallas_call x9, Pallas kernels, forward(): pl.pallas_call(lambda *refs: forward_kernel(*flags, *refs), in_specs=[SME...  11.8 us
    pallas_call x1, Pallas kernels, first_adjoint(): pl.pallas_call(first_kernel, in_specs=[SMEM, SMEM, HBM, HBM], out_specs=[...  9.09 us
    pallas_call x2, Pallas kernels, window(): pl.pallas_call(lambda *refs: window_kernel(len(more) > 0, *refs), in_spec...  6.75 us
    pallas_call x2, Pallas kernels, adjoint(): pl.pallas_call(adjoint_kernel, in_specs=[SMEM, VMEM, VMEM], out_specs=[VM...  4.25 us
  transfers between devices with their start and end apart: 55, of which 29 were waited for; matrix products, arithmetic and copies ran while one was open for 0% of the time, Pallas kernels for 8%

profile of v4, /device:TPU:1, one launch (start us, length us, event | category | flops | bytes accessed | tf_op | source)
XLA Modules:
  0.0 177.0 jit_solution(7631243669420487336)
XLA Ops:
  1.4 9.1 %first_adjoint.1 = (bf16[2,2,256,4096]{3,2,1,0:T(8,128)(2,1)S(1)}, bf16[2,2,256,4096]{3,2,1,0:T(8,128)(2,1)S(1)}, bf16[2,2,4096,256]{3,2,1,0:T(8,128)(2,1)S(1)},...) custom-call(s32[2]{0:T(128)S(1)} %pad_add_fusion.place_ref.refs_0_, ...), custom_call_target="tpu_custom_call" | custom-call | flops 8589934592 | bytes 4194304 | tf_op jit(solution)/shard_map/first_adjoint/pallas_call | solution.py:135
  10.5 3.7 %collective-permute-start = (bf16[4,4,64,256]{3,2,1,0:T(8,128)(2,1)S(1)}, bf16[4,4,64,256]{3,2,1,0:T(8,128)(2,1)S(1)}, u32[]{:S(2)}, u32[]{:S(2)}) collective-permute-start(bf16[4,4,64,256]{3,2,1,0:T(8,128)(2,1)S(1)} %get-tuple-element.52), channel_id=1, source_target_pairs={{0,64},{1,17},{2,66},{3,19},{4,68},{5,21},{6,70},{7,23},{8,72},{9,... | collective-permute-start | bytes 1572872 | tf_op jit(solution)/shard_map/ppermute | solution.py:33
  14.5 2.4 %collective-permute-start.2 = (bf16[4,4,64,256]{3,2,1,0:T(8,128)(2,1)S(1)}, bf16[4,4,64,256]{3,2,1,0:T(8,128)(2,1)S(1)}, u32[]{:S(2)}, u32[]{:S(2)}) collective-permute-start(bf16[4,4,64,256]{3,2,1,0:T(8,128)(2,1)S(1)} %get-tuple-element.54), channel_id=1, source_target_pairs={{0,96},{1,25},{2,98},{3,27},{4,100},{5,29},{6,102},{7,31},{8,104},... | collective-permute-start | bytes 1572872 | tf_op jit(solution)/shard_map/ppermute | solution.py:33
  16.9 4.2 %collective-permute-done = bf16[4,4,64,256]{3,2,1,0:T(8,128)(2,1)S(1)} collective-permute-done((bf16[4,4,64,256]{3,2,1,0:T(8,128)(2,1)S(1)}, bf16[4,4,64,256]{3,2,1,0:T(8,128)(2,1)S(1)}, u32[]{:S(2)}, u32[]{:S(2)}) %collective-permute-start) | collective-permute-done | bytes 524320 | tf_op jit(solution)/shard_map/ppermute | solution.py:33
  21.1 5.6 %collective-permute-done.1 = bf16[4,4,64,256]{3,2,1,0:T(8,128)(2,1)S(1)} collective-permute-done((bf16[4,4,64,256]{3,2,1,0:T(8,128)(2,1)S(1)}, bf16[4,4,64,256]{3,2,1,0:T(8,128)(2,1)S(1)}, u32[]{:S(2)}, u32[]{:S(2)}) %collective-permute-start.1) | collective-permute-done | bytes 524320 | tf_op jit(solution)/shard_map/ppermute | solution.py:33
  27.3 3.0 %collective-permute-start.3 = (bf16[4,64,256]{2,1,0:T(8,128)(2,1)S(1)}, bf16[4,64,256]{2,1,0:T(8,128)(2,1)S(1)}, u32[]{:S(2)}, u32[]{:S(2)}) collective-permute-start(bf16[4,64,256]{2,1,0:T(8,128)(2,1)S(1)} %get-tuple-element.98), channel_id=1, source_target_pairs={{0,16},{1,65},{2,18},{3,67},{4,20},{5,69},{6,22},{7,71},{8,24},{9,... | collective-permute-start | bytes 393224 | tf_op jit(solution)/shard_map/ppermute | solution.py:33
  30.6 2.3 %collective-permute-start.5 = (bf16[4,64,256]{2,1,0:T(8,128)(2,1)S(1)}, bf16[4,64,256]{2,1,0:T(8,128)(2,1)S(1)}, u32[]{:S(2)}, u32[]{:S(2)}) collective-permute-start(bf16[4,64,256]{2,1,0:T(8,128)(2,1)S(1)} %get-tuple-element.99), channel_id=1, source_target_pairs={{0,24},{1,97},{2,26},{3,99},{4,28},{5,101},{6,30},{7,103},{8,0},{9... | collective-permute-start | bytes 393224 | tf_op jit(solution)/shard_map/ppermute | solution.py:33
  32.9 2.3 %collective-permute-done.4 = bf16[4,64,256]{2,1,0:T(8,128)(2,1)S(1)} collective-permute-done((bf16[4,64,256]{2,1,0:T(8,128)(2,1)S(1)}, bf16[4,64,256]{2,1,0:T(8,128)(2,1)S(1)}, u32[]{:S(2)}, u32[]{:S(2)}) %collective-permute-start.4) | collective-permute-done | bytes 131104 | tf_op jit(solution)/shard_map/ppermute | solution.py:33
  35.4 3.0 %collective-permute-start.6 = (bf16[4,32,256]{2,1,0:T(8,128)(2,1)S(1)}, bf16[4,32,256]{2,1,0:T(8,128)(2,1)S(1)}, u32[]{:S(2)}, u32[]{:S(2)}) collective-permute-start(bf16[4,32,256]{2,1,0:T(8,128)(2,1)S(1)} %get-tuple-element.132), channel_id=1, source_target_pairs={{0,1},{1,0},{2,3},{3,2},{4,5},{5,4},{6,7},{7,6},{8,9},{9,8},{10,11... | collective-permute-start | bytes 196616 | tf_op jit(solution)/shard_map/ppermute | solution.py:33
  39.4 3.7 %collective-permute-start.7 = (bf16[256,256]{1,0:T(8,128)(2,1)S(1)}, bf16[256,256]{1,0:T(8,128)(2,1)S(1)}, u32[]{:S(2)}, u32[]{:S(2)}) collective-permute-start(bf16[256,256]{1,0:T(8,128)(2,1)S(1)} %bitcast.105), channel_id=1, source_target_pairs={{0,4},{1,5},{2,6},{3,7},{4,0},{5,1},{6,2},{7,3},{8,12},{9,13},{10,... | collective-permute-start | bytes 393224 | tf_op jit(solution)/shard_map/ppermute | solution.py:33
  44.5 2.1 %collective-permute-done.7.refs_2_ = bf16[256,256]{1,0:T(8,128)(2,1)S(1)} collective-permute-done((bf16[256,256]{1,0:T(8,128)(2,1)S(1)}, bf16[256,256]{1,0:T(8,128)(2,1)S(1)}, u32[]{:S(2)}, u32[]{:S(2)}) %collective-permute-start.7) | collective-permute-done | bytes 131104 | tf_op jit(solution)/shard_map/ppermute | solution.py:33
  46.7 3.3 %collective-permute-done.8.refs_3_ = bf16[256,256]{1,0:T(8,128)(2,1)S(1)} collective-permute-done((bf16[256,256]{1,0:T(8,128)(2,1)S(1)}, bf16[256,256]{1,0:T(8,128)(2,1)S(1)}, u32[]{:S(2)}, u32[]{:S(2)}) %collective-permute-start.8) | collective-permute-done | bytes 131104 | tf_op jit(solution)/shard_map/ppermute | solution.py:33
  49.9 3.4 %window.2 = (f32[2,128,256]{2,1,0:T(8,128)S(1)}, bf16[2,128,256]{2,1,0:T(8,128)(2,1)S(1)}, f32[8,128]{1,0:T(8,128)S(1)}) custom-call(s32[2]{0:T(128)S(1)} %pad_add_fusion.place_ref.refs_0_, bf16[256,256]{1,0:T(8,128)(2,1)S(1)} %bitcast.108, bf16[256,256]{1,0:T(8,128)(2,1)S(1)} %collective-permute-done.7.refs_2_, ...), custom_call_target="tpu_custom_call" | custom-call | flops 1073741824 | bytes 4194304 | tf_op jit(solution)/shard_map/window/pallas_call | solution.py:332
  55.5 1.8 %collective-permute-start.11 = (bf16[4,64,256]{2,1,0:T(8,128)(2,1)S(1)}, bf16[4,64,256]{2,1,0:T(8,128)(2,1)S(1)}, u32[]{:S(2)}, u32[]{:S(2)}) collective-permute-start(bf16[4,64,256]{2,1,0:T(8,128)(2,1)S(1)} %bitcast.125), channel_id=1, source_target_pairs={{0,16},{1,65},{2,18},{3,67},{4,20},{5,69},{6,22},{7,71},{8,24},{9,... | collective-permute-start | bytes 393224 | tf_op jit(solution)/shard_map/ppermute | solution.py:33
  59.1 2.1 %collective-permute-done.11 = bf16[4,64,256]{2,1,0:T(8,128)(2,1)S(1)} collective-permute-done((bf16[4,64,256]{2,1,0:T(8,128)(2,1)S(1)}, bf16[4,64,256]{2,1,0:T(8,128)(2,1)S(1)}, u32[]{:S(2)}, u32[]{:S(2)}) %collective-permute-start.11) | collective-permute-done | bytes 131104 | tf_op jit(solution)/shard_map/ppermute | solution.py:33
  62.3 2.1 %collective-permute-done.13 = bf16[4,64,256]{2,1,0:T(8,128)(2,1)S(1)} collective-permute-done((bf16[4,64,256]{2,1,0:T(8,128)(2,1)S(1)}, bf16[4,64,256]{2,1,0:T(8,128)(2,1)S(1)}, u32[]{:S(2)}, u32[]{:S(2)}) %collective-permute-start.13) | collective-permute-done | bytes 131104 | tf_op jit(solution)/shard_map/ppermute | solution.py:33
  64.5 2.7 %collective-permute-start.14 = (bf16[4,2,64,256]{3,2,1,0:T(8,128)(2,1)S(1)}, bf16[4,2,64,256]{3,2,1,0:T(8,128)(2,1)S(1)}, u32[]{:S(2)}, u32[]{:S(2)}) collective-permute-start(bf16[4,2,64,256]{3,2,1,0:T(8,128)(2,1)S(1)} %pad_maximum_fusion.1.refs_2_), channel_id=1, source_target_pairs={{0,96},{1,25},{2,98},{3,27},{4,100},{5,29},{6,102},{7,31},{8,104},... | collective-permute-start | bytes 786440 | tf_op jit(solution)/shard_map/ppermute | solution.py:33
  72.7 1.8 %collective-permute-start.22 = (bf16[4,2,64,256]{3,2,1,0:T(8,128)(2,1)S(1)}, bf16[4,2,64,256]{3,2,1,0:T(8,128)(2,1)S(1)}, u32[]{:S(2)}, u32[]{:S(2)}) collective-permute-start(bf16[4,2,64,256]{3,2,1,0:T(8,128)(2,1)S(1)} %pad_maximum_fusion.refs_2_), channel_id=1, source_target_pairs={{0,64},{1,17},{2,66},{3,19},{4,68},{5,21},{6,70},{7,23},{8,72},{9,... | collective-permute-start | bytes 786440 | tf_op jit(solution)/shard_map/ppermute | solution.py:33
  74.5 2.2 %collective-permute-done.15.refs_3_ = bf16[4,2,64,256]{3,2,1,0:T(8,128)(2,1)S(1)} collective-permute-done((bf16[4,2,64,256]{3,2,1,0:T(8,128)(2,1)S(1)}, bf16[4,2,64,256]{3,2,1,0:T(8,128)(2,1)S(1)}, u32[]{:S(2)}, u32[]{:S(2)}) %collective-permute-start.15) | collective-permute-done | bytes 262176 | tf_op jit(solution)/shard_map/ppermute | solution.py:33
  76.7 1.8 forward.11
  78.5 2.1 %adjoint.2 = (bf16[4,2,64,256]{3,2,1,0:T(8,128)(2,1)S(1)}, bf16[4,2,64,256]{3,2,1,0:T(8,128)(2,1)S(1)}, bf16[4,2,64,256]{3,2,1,0:T(8,128)(2,1)S(1)}, bf16[4,2,64,256]{3,2,1,0:T(8,128)(2,1)S(1)}) custom-call(s32[16]{0:T(128)S(1)} %fusion.24.j_ref.refs_0_, f32[2,64,256]{2,1,0:T(8,128)S(1)} %get-tuple-element.60.u_ref.refs_6_.i0a, ...), custom_call_target="tpu_custom_call" | custom-call | flops 2147483648 | bytes 4194304 | tf_op jit(solution)/shard_map/adjoint/pallas_call | solution.py:169
  81.5 2.2 %collective-permute-start.19 = (bf16[4,2,64,256]{3,2,1,0:T(8,128)(2,1)S(1)}, bf16[4,2,64,256]{3,2,1,0:T(8,128)(2,1)S(1)}, u32[]{:S(2)}, u32[]{:S(2)}) collective-permute-start(bf16[4,2,64,256]{3,2,1,0:T(8,128)(2,1)S(1)} %get-tuple-element.65), channel_id=1, source_target_pairs={{0,96},{1,25},{2,98},{3,27},{4,100},{5,29},{6,102},{7,31},{8,104},... | collective-permute-start | bytes 786440 | tf_op jit(solution)/shard_map/ppermute | solution.py:33
  83.7 1.8 forward.12
  85.4 2.1 %adjoint.3 = (bf16[4,2,64,256]{3,2,1,0:T(8,128)(2,1)S(1)}, bf16[4,2,64,256]{3,2,1,0:T(8,128)(2,1)S(1)}, bf16[4,2,64,256]{3,2,1,0:T(8,128)(2,1)S(1)}, bf16[4,2,64,256]{3,2,1,0:T(8,128)(2,1)S(1)}) custom-call(s32[16]{0:T(128)S(1)} %fusion.24.j_ref.refs_0_, f32[2,64,256]{2,1,0:T(8,128)S(1)} %get-tuple-element.68.u_ref.refs_4_.i0b, ...), custom_call_target="tpu_custom_call" | custom-call | flops 2147483648 | bytes 4194304 | tf_op jit(solution)/shard_map/adjoint/pallas_call | solution.py:169
  89.1 2.7 %collective-permute-start.25 = (bf16[4,2,64,256]{3,2,1,0:T(8,128)(2,1)S(1)}, bf16[4,2,64,256]{3,2,1,0:T(8,128)(2,1)S(1)}, u32[]{:S(2)}, u32[]{:S(2)}) collective-permute-start(bf16[4,2,64,256]{3,2,1,0:T(8,128)(2,1)S(1)} %get-tuple-element.73), channel_id=1, source_target_pairs={{0,96},{1,25},{2,98},{3,27},{4,100},{5,29},{6,102},{7,31},{8,104},... | collective-permute-start | bytes 786440 | tf_op jit(solution)/shard_map/ppermute | solution.py:33
  92.0 2.5 %collective-permute-done.23 = bf16[4,2,64,256]{3,2,1,0:T(8,128)(2,1)S(1)} collective-permute-done((bf16[4,2,64,256]{3,2,1,0:T(8,128)(2,1)S(1)}, bf16[4,2,64,256]{3,2,1,0:T(8,128)(2,1)S(1)}, u32[]{:S(2)}, u32[]{:S(2)}) %collective-permute-start.23) | collective-permute-done | bytes 262176 | tf_op jit(solution)/shard_map/ppermute | solution.py:33
  94.5 3.0 %collective-permute-done.24 = bf16[4,2,64,256]{3,2,1,0:T(8,128)(2,1)S(1)} collective-permute-done((bf16[4,2,64,256]{3,2,1,0:T(8,128)(2,1)S(1)}, bf16[4,2,64,256]{3,2,1,0:T(8,128)(2,1)S(1)}, u32[]{:S(2)}, u32[]{:S(2)}) %collective-permute-start.24) | collective-permute-done | bytes 262176 | tf_op jit(solution)/shard_map/ppermute | solution.py:33
  99.0 1.7 collective-permute-start.28
  100.8 2.4 %collective-permute-done.26 = bf16[4,64,256]{2,1,0:T(8,128)(2,1)S(1)} collective-permute-done((bf16[4,64,256]{2,1,0:T(8,128)(2,1)S(1)}, bf16[4,64,256]{2,1,0:T(8,128)(2,1)S(1)}, u32[]{:S(2)}, u32[]{:S(2)}) %collective-permute-start.26) | collective-permute-done | bytes 131104 | tf_op jit(solution)/shard_map/ppermute | solution.py:33
  104.5 4.6 %collective-permute-start.29 = (bf16[4,32,256]{2,1,0:T(8,128)(2,1)S(1)}, bf16[4,32,256]{2,1,0:T(8,128)(2,1)S(1)}, u32[]{:S(2)}, u32[]{:S(2)}) collective-permute-start(bf16[4,32,256]{2,1,0:T(8,128)(2,1)S(1)} %get-tuple-element.120), channel_id=1, source_target_pairs={{0,1},{1,0},{2,3},{3,2},{4,5},{5,4},{6,7},{7,6},{8,9},{9,8},{10,11... | collective-permute-start | bytes 196616 | tf_op jit(solution)/shard_map/ppermute | solution.py:33
  110.0 2.3 %collective-permute-start.30 = (bf16[256,256]{1,0:T(8,128)(2,1)S(1)}, bf16[256,256]{1,0:T(8,128)(2,1)S(1)}, u32[]{:S(2)}, u32[]{:S(2)}) collective-permute-start(bf16[256,256]{1,0:T(8,128)(2,1)S(1)} %bitcast.101), channel_id=1, source_target_pairs={{0,4},{1,5},{2,6},{3,7},{4,0},{5,1},{6,2},{7,3},{8,12},{9,13},{10,... | collective-permute-start | bytes 393224 | tf_op jit(solution)/shard_map/ppermute | solution.py:33
  113.8 2.6 %collective-permute-done.30.refs_2_ = bf16[256,256]{1,0:T(8,128)(2,1)S(1)} collective-permute-done((bf16[256,256]{1,0:T(8,128)(2,1)S(1)}, bf16[256,256]{1,0:T(8,128)(2,1)S(1)}, u32[]{:S(2)}, u32[]{:S(2)}) %collective-permute-start.30) | collective-permute-done | bytes 131104 | tf_op jit(solution)/shard_map/ppermute | solution.py:33
  116.3 2.8 %collective-permute-done.31.refs_3_ = bf16[256,256]{1,0:T(8,128)(2,1)S(1)} collective-permute-done((bf16[256,256]{1,0:T(8,128)(2,1)S(1)}, bf16[256,256]{1,0:T(8,128)(2,1)S(1)}, u32[]{:S(2)}, u32[]{:S(2)}) %collective-permute-start.31) | collective-permute-done | bytes 131104 | tf_op jit(solution)/shard_map/ppermute | solution.py:33
  119.3 3.4 %window.3 = (f32[2,128,256]{2,1,0:T(8,128)S(1)}, bf16[2,128,256]{2,1,0:T(8,128)(2,1)S(1)}, f32[8,128]{1,0:T(8,128)S(1)}) custom-call(s32[2]{0:T(128)S(1)} %pad_add_fusion.place_ref.refs_0_, bf16[256,256]{1,0:T(8,128)(2,1)S(1)} %bitcast.104, bf16[256,256]{1,0:T(8,128)(2,1)S(1)} %collective-permute-done.30.refs_2_, ...), custom_call_target="tpu_custom_call" | custom-call | flops 1073741824 | bytes 4194304 | tf_op jit(solution)/shard_map/window/pallas_call | solution.py:332
  125.1 1.8 %collective-permute-start.34 = (bf16[4,64,256]{2,1,0:T(8,128)(2,1)S(1)}, bf16[4,64,256]{2,1,0:T(8,128)(2,1)S(1)}, u32[]{:S(2)}, u32[]{:S(2)}) collective-permute-start(bf16[4,64,256]{2,1,0:T(8,128)(2,1)S(1)} %bitcast.128), channel_id=1, source_target_pairs={{0,16},{1,65},{2,18},{3,67},{4,20},{5,69},{6,22},{7,71},{8,24},{9,... | collective-permute-start | bytes 393224 | tf_op jit(solution)/shard_map/ppermute | solution.py:33
  128.4 2.4 %collective-permute-done.34 = bf16[4,64,256]{2,1,0:T(8,128)(2,1)S(1)} collective-permute-done((bf16[4,64,256]{2,1,0:T(8,128)(2,1)S(1)}, bf16[4,64,256]{2,1,0:T(8,128)(2,1)S(1)}, u32[]{:S(2)}, u32[]{:S(2)}) %collective-permute-start.34) | collective-permute-done | bytes 131104 | tf_op jit(solution)/shard_map/ppermute | solution.py:33
  133.0 3.2 %collective-permute-start.40 = (bf16[4,2,64,256]{3,2,1,0:T(8,128)(2,1)S(1)}, bf16[4,2,64,256]{3,2,1,0:T(8,128)(2,1)S(1)}, u32[]{:S(2)}, u32[]{:S(2)}) collective-permute-start(bf16[4,2,64,256]{3,2,1,0:T(8,128)(2,1)S(1)} %pad_maximum_fusion.3.refs_2_), channel_id=1, source_target_pairs={{0,96},{1,25},{2,98},{3,27},{4,100},{5,29},{6,102},{7,31},{8,104},... | collective-permute-start | bytes 786440 | tf_op jit(solution)/shard_map/ppermute | solution.py:33
  141.7 1.8 %collective-permute-start.37 = (bf16[4,2,64,256]{3,2,1,0:T(8,128)(2,1)S(1)}, bf16[4,2,64,256]{3,2,1,0:T(8,128)(2,1)S(1)}, u32[]{:S(2)}, u32[]{:S(2)}) collective-permute-start(bf16[4,2,64,256]{3,2,1,0:T(8,128)(2,1)S(1)} %pad_maximum_fusion.2.refs_2_), channel_id=1, source_target_pairs={{0,64},{1,17},{2,66},{3,19},{4,68},{5,21},{6,70},{7,23},{8,72},{9,... | collective-permute-start | bytes 786440 | tf_op jit(solution)/shard_map/ppermute | solution.py:33
  143.5 2.2 %collective-permute-done.41.refs_3_ = bf16[4,2,64,256]{3,2,1,0:T(8,128)(2,1)S(1)} collective-permute-done((bf16[4,2,64,256]{3,2,1,0:T(8,128)(2,1)S(1)}, bf16[4,2,64,256]{3,2,1,0:T(8,128)(2,1)S(1)}, u32[]{:S(2)}, u32[]{:S(2)}) %collective-permute-start.41) | collective-permute-done | bytes 262176 | tf_op jit(solution)/shard_map/ppermute | solution.py:33
  145.7 1.8 forward.15
  147.5 3.8 %collective-permute-done.39.refs_3_ = bf16[4,2,64,256]{3,2,1,0:T(8,128)(2,1)S(1)} collective-permute-done((bf16[4,2,64,256]{3,2,1,0:T(8,128)(2,1)S(1)}, bf16[4,2,64,256]{3,2,1,0:T(8,128)(2,1)S(1)}, u32[]{:S(2)}, u32[]{:S(2)}) %collective-permute-start.39) | collective-permute-done | bytes 262176 | tf_op jit(solution)/shard_map/ppermute | solution.py:33
  153.8 2.4 %collective-permute-start.43 = (f32[8,128]{1,0:T(8,128)S(1)}, f32[8,128]{1,0:T(8,128)S(1)}, u32[]{:S(2)}, u32[]{:S(2)}) collective-permute-start(f32[8,128]{1,0:T(8,128)S(1)} %get-tuple-element.92), channel_id=1, source_target_pairs={{0,1},{1,0},{2,3},{3,2},{4,5},{5,4},{6,7},{7,6},{8,9},{9,8},{10,11... | collective-permute-start | bytes 12296 | tf_op jit(solution)/shard_map/ppermute | solution.py:33
  157.0 1.8 %collective-permute-start.44 = (f32[8,128]{1,0:T(8,128)S(1)}, f32[8,128]{1,0:T(8,128)S(1)}, u32[]{:S(2)}, u32[]{:S(2)}) collective-permute-start(f32[8,128]{1,0:T(8,128)S(1)} %add.333), channel_id=1, source_target_pairs={{0,4},{1,5},{2,6},{3,7},{4,0},{5,1},{6,2},{7,3},{8,12},{9,13},{10,... | collective-permute-start | bytes 12296 | tf_op jit(solution)/shard_map/ppermute | solution.py:33
  159.5 1.9 %collective-permute-start.46 = (f32[8,128]{1,0:T(8,128)S(1)}, f32[8,128]{1,0:T(8,128)S(1)}, u32[]{:S(2)}, u32[]{:S(2)}) collective-permute-start(f32[8,128]{1,0:T(8,128)S(1)} %add.333), channel_id=1, source_target_pairs={{0,6},{1,7},{2,0},{3,1},{4,2},{5,3},{6,4},{7,5},{8,14},{9,15},{10,... | collective-permute-start | bytes 12296 | tf_op jit(solution)/shard_map/ppermute | solution.py:33
  162.8 2.7 %collective-permute-start.49 = (f32[8,128]{1,0:T(8,128)S(1)}, f32[8,128]{1,0:T(8,128)S(1)}, u32[]{:S(2)}, u32[]{:S(2)}) collective-permute-start(f32[8,128]{1,0:T(8,128)S(1)} %add_add_fusion.2), channel_id=1, source_target_pairs={{0,24},{1,97},{2,26},{3,99},{4,28},{5,101},{6,30},{7,103},{8,0},{9... | collective-permute-start | bytes 12296 | tf_op jit(solution)/shard_map/ppermute | solution.py:33
  165.5 3.6 %collective-permute-start.53 = (f32[128,256]{1,0:T(8,128)S(1)}, f32[128,256]{1,0:T(8,128)S(1)}, u32[]{:S(2)}, u32[]{:S(2)}) collective-permute-start(f32[128,256]{1,0:T(8,128)S(1)} %slice_bitcast_fusion.1), channel_id=1, source_target_pairs={{0,1},{1,0},{2,3},{3,2},{4,5},{5,4},{6,7},{7,6},{8,9},{9,8},{10,11... | collective-permute-start | bytes 393224 | tf_op jit(solution)/shard_map/ppermute | solution.py:33
  169.8 2.7 %collective-permute-start.52 = (f32[8,128]{1,0:T(8,128)S(1)}, f32[8,128]{1,0:T(8,128)S(1)}, u32[]{:S(2)}, u32[]{:S(2)}) collective-permute-start(f32[8,128]{1,0:T(8,128)S(1)} %add_add_fusion.1), channel_id=1, source_target_pairs={{0,96},{1,25},{2,98},{3,27},{4,100},{5,29},{6,102},{7,31},{8,104},... | collective-permute-start | bytes 12296 | tf_op jit(solution)/shard_map/ppermute | solution.py:33
  172.5 2.0 %collective-permute-start.54 = (f32[128,256]{1,0:T(8,128)S(1)}, f32[128,256]{1,0:T(8,128)S(1)}, u32[]{:S(2)}, u32[]{:S(2)}) collective-permute-start(f32[128,256]{1,0:T(8,128)S(1)} %slice_bitcast_fusion), channel_id=1, source_target_pairs={{0,1},{1,0},{2,3},{3,2},{4,5},{5,4},{6,7},{7,6},{8,9},{9,8},{10,11... | collective-permute-start | bytes 393224 | tf_op jit(solution)/shard_map/ppermute | solution.py:33
  (124 shorter events, 43.1 us)
Async XLA Ops:
  10.5 10.6 %collective-permute-start = (bf16[4,4,64,256]{3,2,1,0:T(8,128)(2,1)S(1)}, bf16[4,4,64,256]{3,2,1,0:T(8,128)(2,1)S(1)}, u32[]{:S(2)}, u32[]{:S(2)}) collective-permute-start(bf16[4,4,64,256]{3,2,1,0:T(8,128)(2,1)S(1)} %get-tuple-element.52), channel_id=1, source_target_pairs={{0,64},{1,17},{2,66},{3,19},{4,68},{5,21},{6,70},{7,23},{8,72},{9,... | collective-permute-start | bytes 1572872 | tf_op jit(solution)/shard_map/ppermute | solution.py:33
  14.2 12.5 %collective-permute-start.1 = (bf16[4,4,64,256]{3,2,1,0:T(8,128)(2,1)S(1)}, bf16[4,4,64,256]{3,2,1,0:T(8,128)(2,1)S(1)}, u32[]{:S(2)}, u32[]{:S(2)}) collective-permute-start(bf16[4,4,64,256]{3,2,1,0:T(8,128)(2,1)S(1)} %get-tuple-element.53), channel_id=1, source_target_pairs={{0,32},{1,9},{2,34},{3,11},{4,36},{5,13},{6,38},{7,15},{8,40},{9,1... | collective-permute-start | bytes 1572872 | tf_op jit(solution)/shard_map/ppermute | solution.py:33
  14.5 12.5 %collective-permute-start.2 = (bf16[4,4,64,256]{3,2,1,0:T(8,128)(2,1)S(1)}, bf16[4,4,64,256]{3,2,1,0:T(8,128)(2,1)S(1)}, u32[]{:S(2)}, u32[]{:S(2)}) collective-permute-start(bf16[4,4,64,256]{3,2,1,0:T(8,128)(2,1)S(1)} %get-tuple-element.54), channel_id=1, source_target_pairs={{0,96},{1,25},{2,98},{3,27},{4,100},{5,29},{6,102},{7,31},{8,104},... | collective-permute-start | bytes 1572872 | tf_op jit(solution)/shard_map/ppermute | solution.py:33
  27.3 5.7 %collective-permute-start.3 = (bf16[4,64,256]{2,1,0:T(8,128)(2,1)S(1)}, bf16[4,64,256]{2,1,0:T(8,128)(2,1)S(1)}, u32[]{:S(2)}, u32[]{:S(2)}) collective-permute-start(bf16[4,64,256]{2,1,0:T(8,128)(2,1)S(1)} %get-tuple-element.98), channel_id=1, source_target_pairs={{0,16},{1,65},{2,18},{3,67},{4,20},{5,69},{6,22},{7,71},{8,24},{9,... | collective-permute-start | bytes 393224 | tf_op jit(solution)/shard_map/ppermute | solution.py:33
  30.2 5.0 %collective-permute-start.4 = (bf16[4,64,256]{2,1,0:T(8,128)(2,1)S(1)}, bf16[4,64,256]{2,1,0:T(8,128)(2,1)S(1)}, u32[]{:S(2)}, u32[]{:S(2)}) collective-permute-start(bf16[4,64,256]{2,1,0:T(8,128)(2,1)S(1)} %get-tuple-element.100), channel_id=1, source_target_pairs={{0,8},{1,33},{2,10},{3,35},{4,12},{5,37},{6,14},{7,39},{8,16},{9,4... | collective-permute-start | bytes 393224 | tf_op jit(solution)/shard_map/ppermute | solution.py:33
  30.6 4.6 %collective-permute-start.5 = (bf16[4,64,256]{2,1,0:T(8,128)(2,1)S(1)}, bf16[4,64,256]{2,1,0:T(8,128)(2,1)S(1)}, u32[]{:S(2)}, u32[]{:S(2)}) collective-permute-start(bf16[4,64,256]{2,1,0:T(8,128)(2,1)S(1)} %get-tuple-element.99), channel_id=1, source_target_pairs={{0,24},{1,97},{2,26},{3,99},{4,28},{5,101},{6,30},{7,103},{8,0},{9... | collective-permute-start | bytes 393224 | tf_op jit(solution)/shard_map/ppermute | solution.py:33
  39.4 7.3 %collective-permute-start.7 = (bf16[256,256]{1,0:T(8,128)(2,1)S(1)}, bf16[256,256]{1,0:T(8,128)(2,1)S(1)}, u32[]{:S(2)}, u32[]{:S(2)}) collective-permute-start(bf16[256,256]{1,0:T(8,128)(2,1)S(1)} %bitcast.105), channel_id=1, source_target_pairs={{0,4},{1,5},{2,6},{3,7},{4,0},{5,1},{6,2},{7,3},{8,12},{9,13},{10,... | collective-permute-start | bytes 393224 | tf_op jit(solution)/shard_map/ppermute | solution.py:33
  43.1 6.9 %collective-permute-start.8 = (bf16[256,256]{1,0:T(8,128)(2,1)S(1)}, bf16[256,256]{1,0:T(8,128)(2,1)S(1)}, u32[]{:S(2)}, u32[]{:S(2)}) collective-permute-start(bf16[256,256]{1,0:T(8,128)(2,1)S(1)} %bitcast.106), channel_id=1, source_target_pairs={{0,6},{1,7},{2,0},{3,1},{4,2},{5,3},{6,4},{7,5},{8,14},{9,15},{10,... | collective-permute-start | bytes 393224 | tf_op jit(solution)/shard_map/ppermute | solution.py:33
  43.5 6.4 %collective-permute-start.9 = (bf16[256,256]{1,0:T(8,128)(2,1)S(1)}, bf16[256,256]{1,0:T(8,128)(2,1)S(1)}, u32[]{:S(2)}, u32[]{:S(2)}) collective-permute-start(bf16[256,256]{1,0:T(8,128)(2,1)S(1)} %bitcast.107), channel_id=1, source_target_pairs={{0,2},{1,3},{2,4},{3,5},{4,6},{5,7},{6,0},{7,1},{8,10},{9,11},{10,... | collective-permute-start | bytes 393224 | tf_op jit(solution)/shard_map/ppermute | solution.py:33
  55.5 5.7 %collective-permute-start.11 = (bf16[4,64,256]{2,1,0:T(8,128)(2,1)S(1)}, bf16[4,64,256]{2,1,0:T(8,128)(2,1)S(1)}, u32[]{:S(2)}, u32[]{:S(2)}) collective-permute-start(bf16[4,64,256]{2,1,0:T(8,128)(2,1)S(1)} %bitcast.125), channel_id=1, source_target_pairs={{0,16},{1,65},{2,18},{3,67},{4,20},{5,69},{6,22},{7,71},{8,24},{9,... | collective-permute-start | bytes 393224 | tf_op jit(solution)/shard_map/ppermute | solution.py:33
  57.4 4.9 %collective-permute-start.12 = (bf16[4,64,256]{2,1,0:T(8,128)(2,1)S(1)}, bf16[4,64,256]{2,1,0:T(8,128)(2,1)S(1)}, u32[]{:S(2)}, u32[]{:S(2)}) collective-permute-start(bf16[4,64,256]{2,1,0:T(8,128)(2,1)S(1)} %bitcast.126), channel_id=1, source_target_pairs={{0,24},{1,97},{2,26},{3,99},{4,28},{5,101},{6,30},{7,103},{8,0},{9... | collective-permute-start | bytes 393224 | tf_op jit(solution)/shard_map/ppermute | solution.py:33
  59.1 5.3 %collective-permute-start.13 = (bf16[4,64,256]{2,1,0:T(8,128)(2,1)S(1)}, bf16[4,64,256]{2,1,0:T(8,128)(2,1)S(1)}, u32[]{:S(2)}, u32[]{:S(2)}) collective-permute-start(bf16[4,64,256]{2,1,0:T(8,128)(2,1)S(1)} %bitcast.127), channel_id=1, source_target_pairs={{0,8},{1,33},{2,10},{3,35},{4,12},{5,37},{6,14},{7,39},{8,16},{9,4... | collective-permute-start | bytes 393224 | tf_op jit(solution)/shard_map/ppermute | solution.py:33
  64.5 8.2 %collective-permute-start.14 = (bf16[4,2,64,256]{3,2,1,0:T(8,128)(2,1)S(1)}, bf16[4,2,64,256]{3,2,1,0:T(8,128)(2,1)S(1)}, u32[]{:S(2)}, u32[]{:S(2)}) collective-permute-start(bf16[4,2,64,256]{3,2,1,0:T(8,128)(2,1)S(1)} %pad_maximum_fusion.1.refs_2_), channel_id=1, source_target_pairs={{0,96},{1,25},{2,98},{3,27},{4,100},{5,29},{6,102},{7,31},{8,104},... | collective-permute-start | bytes 786440 | tf_op jit(solution)/shard_map/ppermute | solution.py:33
  67.2 9.5 %collective-permute-start.15 = (bf16[4,2,64,256]{3,2,1,0:T(8,128)(2,1)S(1)}, bf16[4,2,64,256]{3,2,1,0:T(8,128)(2,1)S(1)}, u32[]{:S(2)}, u32[]{:S(2)}) collective-permute-start(bf16[4,2,64,256]{3,2,1,0:T(8,128)(2,1)S(1)} %pad_maximum_fusion.1.refs_2_), channel_id=1, source_target_pairs={{0,32},{1,9},{2,34},{3,11},{4,36},{5,13},{6,38},{7,15},{8,40},{9,1... | collective-permute-start | bytes 786440 | tf_op jit(solution)/shard_map/ppermute | solution.py:33
  67.2 9.5 %collective-permute-start.16 = (bf16[4,2,64,256]{3,2,1,0:T(8,128)(2,1)S(1)}, bf16[4,2,64,256]{3,2,1,0:T(8,128)(2,1)S(1)}, u32[]{:S(2)}, u32[]{:S(2)}) collective-permute-start(bf16[4,2,64,256]{3,2,1,0:T(8,128)(2,1)S(1)} %pad_maximum_fusion.1.refs_2_), channel_id=1, source_target_pairs={{0,64},{1,17},{2,66},{3,19},{4,68},{5,21},{6,70},{7,23},{8,72},{9,... | collective-permute-start | bytes 786440 | tf_op jit(solution)/shard_map/ppermute | solution.py:33
  69.5 12.0 %collective-permute-start.20 = (bf16[4,2,64,256]{3,2,1,0:T(8,128)(2,1)S(1)}, bf16[4,2,64,256]{3,2,1,0:T(8,128)(2,1)S(1)}, u32[]{:S(2)}, u32[]{:S(2)}) collective-permute-start(bf16[4,2,64,256]{3,2,1,0:T(8,128)(2,1)S(1)} %pad_maximum_fusion.refs_2_), channel_id=1, source_target_pairs={{0,96},{1,25},{2,98},{3,27},{4,100},{5,29},{6,102},{7,31},{8,104},... | collective-permute-start | bytes 786440 | tf_op jit(solution)/shard_map/ppermute | solution.py:33
  71.0 12.7 %collective-permute-start.21 = (bf16[4,2,64,256]{3,2,1,0:T(8,128)(2,1)S(1)}, bf16[4,2,64,256]{3,2,1,0:T(8,128)(2,1)S(1)}, u32[]{:S(2)}, u32[]{:S(2)}) collective-permute-start(bf16[4,2,64,256]{3,2,1,0:T(8,128)(2,1)S(1)} %pad_maximum_fusion.refs_2_), channel_id=1, source_target_pairs={{0,32},{1,9},{2,34},{3,11},{4,36},{5,13},{6,38},{7,15},{8,40},{9,1... | collective-permute-start | bytes 786440 | tf_op jit(solution)/shard_map/ppermute | solution.py:33
  72.7 11.0 %collective-permute-start.22 = (bf16[4,2,64,256]{3,2,1,0:T(8,128)(2,1)S(1)}, bf16[4,2,64,256]{3,2,1,0:T(8,128)(2,1)S(1)}, u32[]{:S(2)}, u32[]{:S(2)}) collective-permute-start(bf16[4,2,64,256]{3,2,1,0:T(8,128)(2,1)S(1)} %pad_maximum_fusion.refs_2_), channel_id=1, source_target_pairs={{0,64},{1,17},{2,66},{3,19},{4,68},{5,21},{6,70},{7,23},{8,72},{9,... | collective-permute-start | bytes 786440 | tf_op jit(solution)/shard_map/ppermute | solution.py:33
  80.6 8.5 %collective-permute-start.17 = (bf16[4,2,64,256]{3,2,1,0:T(8,128)(2,1)S(1)}, bf16[4,2,64,256]{3,2,1,0:T(8,128)(2,1)S(1)}, u32[]{:S(2)}, u32[]{:S(2)}) collective-permute-start(bf16[4,2,64,256]{3,2,1,0:T(8,128)(2,1)S(1)} %get-tuple-element.63), channel_id=1, source_target_pairs={{0,64},{1,17},{2,66},{3,19},{4,68},{5,21},{6,70},{7,23},{8,72},{9,... | collective-permute-start | bytes 786440 | tf_op jit(solution)/shard_map/ppermute | solution.py:33
  81.0 10.8 %collective-permute-start.18 = (bf16[4,2,64,256]{3,2,1,0:T(8,128)(2,1)S(1)}, bf16[4,2,64,256]{3,2,1,0:T(8,128)(2,1)S(1)}, u32[]{:S(2)}, u32[]{:S(2)}) collective-permute-start(bf16[4,2,64,256]{3,2,1,0:T(8,128)(2,1)S(1)} %get-tuple-element.64), channel_id=1, source_target_pairs={{0,32},{1,9},{2,34},{3,11},{4,36},{5,13},{6,38},{7,15},{8,40},{9,1... | collective-permute-start | bytes 786440 | tf_op jit(solution)/shard_map/ppermute | solution.py:33
  81.5 10.3 %collective-permute-start.19 = (bf16[4,2,64,256]{3,2,1,0:T(8,128)(2,1)S(1)}, bf16[4,2,64,256]{3,2,1,0:T(8,128)(2,1)S(1)}, u32[]{:S(2)}, u32[]{:S(2)}) collective-permute-start(bf16[4,2,64,256]{3,2,1,0:T(8,128)(2,1)S(1)} %get-tuple-element.65), channel_id=1, source_target_pairs={{0,96},{1,25},{2,98},{3,27},{4,100},{5,29},{6,102},{7,31},{8,104},... | collective-permute-start | bytes 786440 | tf_op jit(solution)/shard_map/ppermute | solution.py:33
  87.6 6.9 %collective-permute-start.23 = (bf16[4,2,64,256]{3,2,1,0:T(8,128)(2,1)S(1)}, bf16[4,2,64,256]{3,2,1,0:T(8,128)(2,1)S(1)}, u32[]{:S(2)}, u32[]{:S(2)}) collective-permute-start(bf16[4,2,64,256]{3,2,1,0:T(8,128)(2,1)S(1)} %get-tuple-element.71), channel_id=1, source_target_pairs={{0,64},{1,17},{2,66},{3,19},{4,68},{5,21},{6,70},{7,23},{8,72},{9,... | collective-permute-start | bytes 786440 | tf_op jit(solution)/shard_map/ppermute | solution.py:33
  89.1 8.4 %collective-permute-start.24 = (bf16[4,2,64,256]{3,2,1,0:T(8,128)(2,1)S(1)}, bf16[4,2,64,256]{3,2,1,0:T(8,128)(2,1)S(1)}, u32[]{:S(2)}, u32[]{:S(2)}) collective-permute-start(bf16[4,2,64,256]{3,2,1,0:T(8,128)(2,1)S(1)} %get-tuple-element.72), channel_id=1, source_target_pairs={{0,32},{1,9},{2,34},{3,11},{4,36},{5,13},{6,38},{7,15},{8,40},{9,1... | collective-permute-start | bytes 786440 | tf_op jit(solution)/shard_map/ppermute | solution.py:33
  89.1 8.4 %collective-permute-start.25 = (bf16[4,2,64,256]{3,2,1,0:T(8,128)(2,1)S(1)}, bf16[4,2,64,256]{3,2,1,0:T(8,128)(2,1)S(1)}, u32[]{:S(2)}, u32[]{:S(2)}) collective-permute-start(bf16[4,2,64,256]{3,2,1,0:T(8,128)(2,1)S(1)} %get-tuple-element.73), channel_id=1, source_target_pairs={{0,96},{1,25},{2,98},{3,27},{4,100},{5,29},{6,102},{7,31},{8,104},... | collective-permute-start | bytes 786440 | tf_op jit(solution)/shard_map/ppermute | solution.py:33
  97.7 5.5 %collective-permute-start.26 = (bf16[4,64,256]{2,1,0:T(8,128)(2,1)S(1)}, bf16[4,64,256]{2,1,0:T(8,128)(2,1)S(1)}, u32[]{:S(2)}, u32[]{:S(2)}) collective-permute-start(bf16[4,64,256]{2,1,0:T(8,128)(2,1)S(1)} %pad_maximum_fusion.7), channel_id=1, source_target_pairs={{0,16},{1,65},{2,18},{3,67},{4,20},{5,69},{6,22},{7,71},{8,24},{9,... | collective-permute-start | bytes 393224 | tf_op jit(solution)/shard_map/ppermute | solution.py:33
  97.9 6.5 %collective-permute-start.27 = (bf16[4,64,256]{2,1,0:T(8,128)(2,1)S(1)}, bf16[4,64,256]{2,1,0:T(8,128)(2,1)S(1)}, u32[]{:S(2)}, u32[]{:S(2)}) collective-permute-start(bf16[4,64,256]{2,1,0:T(8,128)(2,1)S(1)} %pad_maximum_fusion.8), channel_id=1, source_target_pairs={{0,8},{1,33},{2,10},{3,35},{4,12},{5,37},{6,14},{7,39},{8,16},{9,4... | collective-permute-start | bytes 393224 | tf_op jit(solution)/shard_map/ppermute | solution.py:33
  99.0 5.4 %collective-permute-start.28 = (bf16[4,64,256]{2,1,0:T(8,128)(2,1)S(1)}, bf16[4,64,256]{2,1,0:T(8,128)(2,1)S(1)}, u32[]{:S(2)}, u32[]{:S(2)}) collective-permute-start(bf16[4,64,256]{2,1,0:T(8,128)(2,1)S(1)} %pad_maximum_fusion.9), channel_id=1, source_target_pairs={{0,24},{1,97},{2,26},{3,99},{4,28},{5,101},{6,30},{7,103},{8,0},{9... | collective-permute-start | bytes 393224 | tf_op jit(solution)/shard_map/ppermute | solution.py:33
  104.5 5.5 %collective-permute-start.29 = (bf16[4,32,256]{2,1,0:T(8,128)(2,1)S(1)}, bf16[4,32,256]{2,1,0:T(8,128)(2,1)S(1)}, u32[]{:S(2)}, u32[]{:S(2)}) collective-permute-start(bf16[4,32,256]{2,1,0:T(8,128)(2,1)S(1)} %get-tuple-element.120), channel_id=1, source_target_pairs={{0,1},{1,0},{2,3},{3,2},{4,5},{5,4},{6,7},{7,6},{8,9},{9,8},{10,11... | collective-permute-start | bytes 196616 | tf_op jit(solution)/shard_map/ppermute | solution.py:33
  110.0 6.3 %collective-permute-start.30 = (bf16[256,256]{1,0:T(8,128)(2,1)S(1)}, bf16[256,256]{1,0:T(8,128)(2,1)S(1)}, u32[]{:S(2)}, u32[]{:S(2)}) collective-permute-start(bf16[256,256]{1,0:T(8,128)(2,1)S(1)} %bitcast.101), channel_id=1, source_target_pairs={{0,4},{1,5},{2,6},{3,7},{4,0},{5,1},{6,2},{7,3},{8,12},{9,13},{10,... | collective-permute-start | bytes 393224 | tf_op jit(solution)/shard_map/ppermute | solution.py:33
  112.3 6.8 %collective-permute-start.31 = (bf16[256,256]{1,0:T(8,128)(2,1)S(1)}, bf16[256,256]{1,0:T(8,128)(2,1)S(1)}, u32[]{:S(2)}, u32[]{:S(2)}) collective-permute-start(bf16[256,256]{1,0:T(8,128)(2,1)S(1)} %bitcast.102), channel_id=1, source_target_pairs={{0,6},{1,7},{2,0},{3,1},{4,2},{5,3},{6,4},{7,5},{8,14},{9,15},{10,... | collective-permute-start | bytes 393224 | tf_op jit(solution)/shard_map/ppermute | solution.py:33
  113.2 6.1 %collective-permute-start.32 = (bf16[256,256]{1,0:T(8,128)(2,1)S(1)}, bf16[256,256]{1,0:T(8,128)(2,1)S(1)}, u32[]{:S(2)}, u32[]{:S(2)}) collective-permute-start(bf16[256,256]{1,0:T(8,128)(2,1)S(1)} %bitcast.103), channel_id=1, source_target_pairs={{0,2},{1,3},{2,4},{3,5},{4,6},{5,7},{6,0},{7,1},{8,10},{9,11},{10,... | collective-permute-start | bytes 393224 | tf_op jit(solution)/shard_map/ppermute | solution.py:33
  125.1 5.7 %collective-permute-start.34 = (bf16[4,64,256]{2,1,0:T(8,128)(2,1)S(1)}, bf16[4,64,256]{2,1,0:T(8,128)(2,1)S(1)}, u32[]{:S(2)}, u32[]{:S(2)}) collective-permute-start(bf16[4,64,256]{2,1,0:T(8,128)(2,1)S(1)} %bitcast.128), channel_id=1, source_target_pairs={{0,16},{1,65},{2,18},{3,67},{4,20},{5,69},{6,22},{7,71},{8,24},{9,... | collective-permute-start | bytes 393224 | tf_op jit(solution)/shard_map/ppermute | solution.py:33
  126.9 4.7 %collective-permute-start.35 = (bf16[4,64,256]{2,1,0:T(8,128)(2,1)S(1)}, bf16[4,64,256]{2,1,0:T(8,128)(2,1)S(1)}, u32[]{:S(2)}, u32[]{:S(2)}) collective-permute-start(bf16[4,64,256]{2,1,0:T(8,128)(2,1)S(1)} %bitcast.129), channel_id=1, source_target_pairs={{0,24},{1,97},{2,26},{3,99},{4,28},{5,101},{6,30},{7,103},{8,0},{9... | collective-permute-start | bytes 393224 | tf_op jit(solution)/shard_map/ppermute | solution.py:33
  127.9 5.0 %collective-permute-start.36 = (bf16[4,64,256]{2,1,0:T(8,128)(2,1)S(1)}, bf16[4,64,256]{2,1,0:T(8,128)(2,1)S(1)}, u32[]{:S(2)}, u32[]{:S(2)}) collective-permute-start(bf16[4,64,256]{2,1,0:T(8,128)(2,1)S(1)} %bitcast.130), channel_id=1, source_target_pairs={{0,8},{1,33},{2,10},{3,35},{4,12},{5,37},{6,14},{7,39},{8,16},{9,4... | collective-permute-start | bytes 393224 | tf_op jit(solution)/shard_map/ppermute | solution.py:33
  133.0 8.7 %collective-permute-start.40 = (bf16[4,2,64,256]{3,2,1,0:T(8,128)(2,1)S(1)}, bf16[4,2,64,256]{3,2,1,0:T(8,128)(2,1)S(1)}, u32[]{:S(2)}, u32[]{:S(2)}) collective-permute-start(bf16[4,2,64,256]{3,2,1,0:T(8,128)(2,1)S(1)} %pad_maximum_fusion.3.refs_2_), channel_id=1, source_target_pairs={{0,96},{1,25},{2,98},{3,27},{4,100},{5,29},{6,102},{7,31},{8,104},... | collective-permute-start | bytes 786440 | tf_op jit(solution)/shard_map/ppermute | solution.py:33
  136.2 9.5 %collective-permute-start.41 = (bf16[4,2,64,256]{3,2,1,0:T(8,128)(2,1)S(1)}, bf16[4,2,64,256]{3,2,1,0:T(8,128)(2,1)S(1)}, u32[]{:S(2)}, u32[]{:S(2)}) collective-permute-start(bf16[4,2,64,256]{3,2,1,0:T(8,128)(2,1)S(1)} %pad_maximum_fusion.3.refs_2_), channel_id=1, source_target_pairs={{0,32},{1,9},{2,34},{3,11},{4,36},{5,13},{6,38},{7,15},{8,40},{9,1... | collective-permute-start | bytes 786440 | tf_op jit(solution)/shard_map/ppermute | solution.py:33
  136.2 9.5 %collective-permute-start.42 = (bf16[4,2,64,256]{3,2,1,0:T(8,128)(2,1)S(1)}, bf16[4,2,64,256]{3,2,1,0:T(8,128)(2,1)S(1)}, u32[]{:S(2)}, u32[]{:S(2)}) collective-permute-start(bf16[4,2,64,256]{3,2,1,0:T(8,128)(2,1)S(1)} %pad_maximum_fusion.3.refs_2_), channel_id=1, source_target_pairs={{0,64},{1,17},{2,66},{3,19},{4,68},{5,21},{6,70},{7,23},{8,72},{9,... | collective-permute-start | bytes 786440 | tf_op jit(solution)/shard_map/ppermute | solution.py:33
  138.5 9.0 %collective-permute-start.38 = (bf16[4,2,64,256]{3,2,1,0:T(8,128)(2,1)S(1)}, bf16[4,2,64,256]{3,2,1,0:T(8,128)(2,1)S(1)}, u32[]{:S(2)}, u32[]{:S(2)}) collective-permute-start(bf16[4,2,64,256]{3,2,1,0:T(8,128)(2,1)S(1)} %pad_maximum_fusion.2.refs_2_), channel_id=1, source_target_pairs={{0,96},{1,25},{2,98},{3,27},{4,100},{5,29},{6,102},{7,31},{8,104},... | collective-permute-start | bytes 786440 | tf_op jit(solution)/shard_map/ppermute | solution.py:33
  140.0 11.3 %collective-permute-start.39 = (bf16[4,2,64,256]{3,2,1,0:T(8,128)(2,1)S(1)}, bf16[4,2,64,256]{3,2,1,0:T(8,128)(2,1)S(1)}, u32[]{:S(2)}, u32[]{:S(2)}) collective-permute-start(bf16[4,2,64,256]{3,2,1,0:T(8,128)(2,1)S(1)} %pad_maximum_fusion.2.refs_2_), channel_id=1, source_target_pairs={{0,32},{1,9},{2,34},{3,11},{4,36},{5,13},{6,38},{7,15},{8,40},{9,1... | collective-permute-start | bytes 786440 | tf_op jit(solution)/shard_map/ppermute | solution.py:33
  141.7 11.0 %collective-permute-start.37 = (bf16[4,2,64,256]{3,2,1,0:T(8,128)(2,1)S(1)}, bf16[4,2,64,256]{3,2,1,0:T(8,128)(2,1)S(1)}, u32[]{:S(2)}, u32[]{:S(2)}) collective-permute-start(bf16[4,2,64,256]{3,2,1,0:T(8,128)(2,1)S(1)} %pad_maximum_fusion.2.refs_2_), channel_id=1, source_target_pairs={{0,64},{1,17},{2,66},{3,19},{4,68},{5,21},{6,70},{7,23},{8,72},{9,... | collective-permute-start | bytes 786440 | tf_op jit(solution)/shard_map/ppermute | solution.py:33
  157.0 4.5 %collective-permute-start.44 = (f32[8,128]{1,0:T(8,128)S(1)}, f32[8,128]{1,0:T(8,128)S(1)}, u32[]{:S(2)}, u32[]{:S(2)}) collective-permute-start(f32[8,128]{1,0:T(8,128)S(1)} %add.333), channel_id=1, source_target_pairs={{0,4},{1,5},{2,6},{3,7},{4,0},{5,1},{6,2},{7,3},{8,12},{9,13},{10,... | collective-permute-start | bytes 12296 | tf_op jit(solution)/shard_map/ppermute | solution.py:33
  162.5 6.6 %collective-permute-start.47 = (f32[8,128]{1,0:T(8,128)S(1)}, f32[8,128]{1,0:T(8,128)S(1)}, u32[]{:S(2)}, u32[]{:S(2)}) collective-permute-start(f32[8,128]{1,0:T(8,128)S(1)} %add_add_fusion.2), channel_id=1, source_target_pairs={{0,16},{1,65},{2,18},{3,67},{4,20},{5,69},{6,22},{7,71},{8,24},{9,... | collective-permute-start | bytes 12296 | tf_op jit(solution)/shard_map/ppermute | solution.py:33
  162.8 6.3 %collective-permute-start.48 = (f32[8,128]{1,0:T(8,128)S(1)}, f32[8,128]{1,0:T(8,128)S(1)}, u32[]{:S(2)}, u32[]{:S(2)}) collective-permute-start(f32[8,128]{1,0:T(8,128)S(1)} %add_add_fusion.2), channel_id=1, source_target_pairs={{0,8},{1,33},{2,10},{3,35},{4,12},{5,37},{6,14},{7,39},{8,16},{9,4... | collective-permute-start | bytes 12296 | tf_op jit(solution)/shard_map/ppermute | solution.py:33
  162.8 6.3 %collective-permute-start.49 = (f32[8,128]{1,0:T(8,128)S(1)}, f32[8,128]{1,0:T(8,128)S(1)}, u32[]{:S(2)}, u32[]{:S(2)}) collective-permute-start(f32[8,128]{1,0:T(8,128)S(1)} %add_add_fusion.2), channel_id=1, source_target_pairs={{0,24},{1,97},{2,26},{3,99},{4,28},{5,101},{6,30},{7,103},{8,0},{9... | collective-permute-start | bytes 12296 | tf_op jit(solution)/shard_map/ppermute | solution.py:33
  165.5 9.0 %collective-permute-start.53 = (f32[128,256]{1,0:T(8,128)S(1)}, f32[128,256]{1,0:T(8,128)S(1)}, u32[]{:S(2)}, u32[]{:S(2)}) collective-permute-start(f32[128,256]{1,0:T(8,128)S(1)} %slice_bitcast_fusion.1), channel_id=1, source_target_pairs={{0,1},{1,0},{2,3},{3,2},{4,5},{5,4},{6,7},{7,6},{8,9},{9,8},{10,11... | collective-permute-start | bytes 393224 | tf_op jit(solution)/shard_map/ppermute | solution.py:33
  169.1 5.4 %collective-permute-start.50 = (f32[8,128]{1,0:T(8,128)S(1)}, f32[8,128]{1,0:T(8,128)S(1)}, u32[]{:S(2)}, u32[]{:S(2)}) collective-permute-start(f32[8,128]{1,0:T(8,128)S(1)} %add_add_fusion.1), channel_id=1, source_target_pairs={{0,64},{1,17},{2,66},{3,19},{4,68},{5,21},{6,70},{7,23},{8,72},{9,... | collective-permute-start | bytes 12296 | tf_op jit(solution)/shard_map/ppermute | solution.py:33
  169.8 4.7 %collective-permute-start.51 = (f32[8,128]{1,0:T(8,128)S(1)}, f32[8,128]{1,0:T(8,128)S(1)}, u32[]{:S(2)}, u32[]{:S(2)}) collective-permute-start(f32[8,128]{1,0:T(8,128)S(1)} %add_add_fusion.1), channel_id=1, source_target_pairs={{0,32},{1,9},{2,34},{3,11},{4,36},{5,13},{6,38},{7,15},{8,40},{9,1... | collective-permute-start | bytes 12296 | tf_op jit(solution)/shard_map/ppermute | solution.py:33
  169.8 4.7 %collective-permute-start.52 = (f32[8,128]{1,0:T(8,128)S(1)}, f32[8,128]{1,0:T(8,128)S(1)}, u32[]{:S(2)}, u32[]{:S(2)}) collective-permute-start(f32[8,128]{1,0:T(8,128)S(1)} %add_add_fusion.1), channel_id=1, source_target_pairs={{0,96},{1,25},{2,98},{3,27},{4,100},{5,29},{6,102},{7,31},{8,104},... | collective-permute-start | bytes 12296 | tf_op jit(solution)/shard_map/ppermute | solution.py:33
  (11 other events, 183.3 us)

commit v5 on v4

--- a/solution.py
+++ b/solution.py
@@ -399,7 +399,8 @@
     yy, xx, zz, core = rcv // 4, rcv % 4, freq // 2, freq % 2
     place = jnp.stack([zz, core]).astype(jnp.int32)
     far = jnp.arange(16, dtype=jnp.int32) // 4
-    near = jnp.asarray(np.array(OFFSETS * 4, np.int32))
+    near = jnp.arange(16, dtype=jnp.int32) % 4
+    near = near % 2 * 2 + near // 2
     off_y = jnp.where(core == 0, far, near)
     off_x = jnp.where(core == 0, near, far)
     table = (yy + off_y) % 4 * 4 + (xx + off_x) % 4

time: 177 us -> 176 us (level)
  no operation moved by 1% of the time
where the time goes in v5:
time: 176 us
  starting transfers between devices  83.6 us (48%)
  waiting for transfers between devices  56.8 us (32%)
  Pallas kernels  33.4 us (19%)
    ppermute x55, starting transfers between devices, move(): return lax.ppermute(value, AXES, pairs)  83.6 us
    ppermute x55, waiting for transfers between devices, move(): return lax.ppermute(value, AXES, pairs)  56.8 us
    pallas_call x9, Pallas kernels, forward(): pl.pallas_call(lambda *refs: forward_kernel(*flags, *refs), in_specs=[SME...  11.8 us
    pallas_call x1, Pallas kernels, first_adjoint(): pl.pallas_call(first_kernel, in_specs=[SMEM, SMEM, HBM, HBM], out_specs=[...  9.09 us
    pallas_call x2, Pallas kernels, window(): pl.pallas_call(lambda *refs: window_kernel(len(more) > 0, *refs), in_spec...  6.75 us
    pallas_call x2, Pallas kernels, adjoint(): pl.pallas_call(adjoint_kernel, in_specs=[SMEM, VMEM, VMEM], out_specs=[VM...  4.25 us
  transfers between devices with their start and end apart: 55, of which 29 were waited for; matrix products, arithmetic and copies ran while one was open for 0% of the time, Pallas kernels for 8%

profile of v5, /device:TPU:1, one launch (start us, length us, event | category | flops | bytes accessed | tf_op | source)
XLA Modules:
  0.0 176.4 jit_solution(8771137456581436952)
XLA Ops:
  0.8 9.1 %first_adjoint.1 = (bf16[2,2,256,4096]{3,2,1,0:T(8,128)(2,1)S(1)}, bf16[2,2,256,4096]{3,2,1,0:T(8,128)(2,1)S(1)}, bf16[2,2,4096,256]{3,2,1,0:T(8,128)(2,1)S(1)},...) custom-call(s32[2]{0:T(128)S(1)} %pad_add_fusion.place_ref.refs_0_, ...), custom_call_target="tpu_custom_call" | custom-call | flops 8589934592 | bytes 4194304 | tf_op jit(solution)/shard_map/first_adjoint/pallas_call | solution.py:135
  9.9 3.7 %collective-permute-start = (bf16[4,4,64,256]{3,2,1,0:T(8,128)(2,1)S(1)}, bf16[4,4,64,256]{3,2,1,0:T(8,128)(2,1)S(1)}, u32[]{:S(2)}, u32[]{:S(2)}) collective-permute-start(bf16[4,4,64,256]{3,2,1,0:T(8,128)(2,1)S(1)} %get-tuple-element.52), channel_id=1, source_target_pairs={{0,64},{1,17},{2,66},{3,19},{4,68},{5,21},{6,70},{7,23},{8,72},{9,... | collective-permute-start | bytes 1572872 | tf_op jit(solution)/shard_map/ppermute | solution.py:33
  13.9 2.4 %collective-permute-start.2 = (bf16[4,4,64,256]{3,2,1,0:T(8,128)(2,1)S(1)}, bf16[4,4,64,256]{3,2,1,0:T(8,128)(2,1)S(1)}, u32[]{:S(2)}, u32[]{:S(2)}) collective-permute-start(bf16[4,4,64,256]{3,2,1,0:T(8,128)(2,1)S(1)} %get-tuple-element.54), channel_id=1, source_target_pairs={{0,96},{1,25},{2,98},{3,27},{4,100},{5,29},{6,102},{7,31},{8,104},... | collective-permute-start | bytes 1572872 | tf_op jit(solution)/shard_map/ppermute | solution.py:33
  16.2 4.2 %collective-permute-done = bf16[4,4,64,256]{3,2,1,0:T(8,128)(2,1)S(1)} collective-permute-done((bf16[4,4,64,256]{3,2,1,0:T(8,128)(2,1)S(1)}, bf16[4,4,64,256]{3,2,1,0:T(8,128)(2,1)S(1)}, u32[]{:S(2)}, u32[]{:S(2)}) %collective-permute-start) | collective-permute-done | bytes 524320 | tf_op jit(solution)/shard_map/ppermute | solution.py:33
  20.5 5.6 %collective-permute-done.1 = bf16[4,4,64,256]{3,2,1,0:T(8,128)(2,1)S(1)} collective-permute-done((bf16[4,4,64,256]{3,2,1,0:T(8,128)(2,1)S(1)}, bf16[4,4,64,256]{3,2,1,0:T(8,128)(2,1)S(1)}, u32[]{:S(2)}, u32[]{:S(2)}) %collective-permute-start.1) | collective-permute-done | bytes 524320 | tf_op jit(solution)/shard_map/ppermute | solution.py:33
  26.6 3.0 %collective-permute-start.3 = (bf16[4,64,256]{2,1,0:T(8,128)(2,1)S(1)}, bf16[4,64,256]{2,1,0:T(8,128)(2,1)S(1)}, u32[]{:S(2)}, u32[]{:S(2)}) collective-permute-start(bf16[4,64,256]{2,1,0:T(8,128)(2,1)S(1)} %get-tuple-element.98), channel_id=1, source_target_pairs={{0,16},{1,65},{2,18},{3,67},{4,20},{5,69},{6,22},{7,71},{8,24},{9,... | collective-permute-start | bytes 393224 | tf_op jit(solution)/shard_map/ppermute | solution.py:33
  30.0 2.3 %collective-permute-start.5 = (bf16[4,64,256]{2,1,0:T(8,128)(2,1)S(1)}, bf16[4,64,256]{2,1,0:T(8,128)(2,1)S(1)}, u32[]{:S(2)}, u32[]{:S(2)}) collective-permute-start(bf16[4,64,256]{2,1,0:T(8,128)(2,1)S(1)} %get-tuple-element.99), channel_id=1, source_target_pairs={{0,24},{1,97},{2,26},{3,99},{4,28},{5,101},{6,30},{7,103},{8,0},{9... | collective-permute-start | bytes 393224 | tf_op jit(solution)/shard_map/ppermute | solution.py:33
  32.3 2.3 %collective-permute-done.4 = bf16[4,64,256]{2,1,0:T(8,128)(2,1)S(1)} collective-permute-done((bf16[4,64,256]{2,1,0:T(8,128)(2,1)S(1)}, bf16[4,64,256]{2,1,0:T(8,128)(2,1)S(1)}, u32[]{:S(2)}, u32[]{:S(2)}) %collective-permute-start.4) | collective-permute-done | bytes 131104 | tf_op jit(solution)/shard_map/ppermute | solution.py:33
  34.8 3.1 %collective-permute-start.6 = (bf16[4,32,256]{2,1,0:T(8,128)(2,1)S(1)}, bf16[4,32,256]{2,1,0:T(8,128)(2,1)S(1)}, u32[]{:S(2)}, u32[]{:S(2)}) collective-permute-start(bf16[4,32,256]{2,1,0:T(8,128)(2,1)S(1)} %get-tuple-element.132), channel_id=1, source_target_pairs={{0,1},{1,0},{2,3},{3,2},{4,5},{5,4},{6,7},{7,6},{8,9},{9,8},{10,11... | collective-permute-start | bytes 196616 | tf_op jit(solution)/shard_map/ppermute | solution.py:33
  38.8 3.7 %collective-permute-start.7 = (bf16[256,256]{1,0:T(8,128)(2,1)S(1)}, bf16[256,256]{1,0:T(8,128)(2,1)S(1)}, u32[]{:S(2)}, u32[]{:S(2)}) collective-permute-start(bf16[256,256]{1,0:T(8,128)(2,1)S(1)} %bitcast.105), channel_id=1, source_target_pairs={{0,4},{1,5},{2,6},{3,7},{4,0},{5,1},{6,2},{7,3},{8,12},{9,13},{10,... | collective-permute-start | bytes 393224 | tf_op jit(solution)/shard_map/ppermute | solution.py:33
  43.9 2.1 %collective-permute-done.7.refs_2_ = bf16[256,256]{1,0:T(8,128)(2,1)S(1)} collective-permute-done((bf16[256,256]{1,0:T(8,128)(2,1)S(1)}, bf16[256,256]{1,0:T(8,128)(2,1)S(1)}, u32[]{:S(2)}, u32[]{:S(2)}) %collective-permute-start.7) | collective-permute-done | bytes 131104 | tf_op jit(solution)/shard_map/ppermute | solution.py:33
  46.0 3.3 %collective-permute-done.8.refs_3_ = bf16[256,256]{1,0:T(8,128)(2,1)S(1)} collective-permute-done((bf16[256,256]{1,0:T(8,128)(2,1)S(1)}, bf16[256,256]{1,0:T(8,128)(2,1)S(1)}, u32[]{:S(2)}, u32[]{:S(2)}) %collective-permute-start.8) | collective-permute-done | bytes 131104 | tf_op jit(solution)/shard_map/ppermute | solution.py:33
  49.3 3.4 %window.2 = (f32[2,128,256]{2,1,0:T(8,128)S(1)}, bf16[2,128,256]{2,1,0:T(8,128)(2,1)S(1)}, f32[8,128]{1,0:T(8,128)S(1)}) custom-call(s32[2]{0:T(128)S(1)} %pad_add_fusion.place_ref.refs_0_, bf16[256,256]{1,0:T(8,128)(2,1)S(1)} %bitcast.108, bf16[256,256]{1,0:T(8,128)(2,1)S(1)} %collective-permute-done.7.refs_2_, ...), custom_call_target="tpu_custom_call" | custom-call | flops 1073741824 | bytes 4194304 | tf_op jit(solution)/shard_map/window/pallas_call | solution.py:332
  54.9 1.8 %collective-permute-start.11 = (bf16[4,64,256]{2,1,0:T(8,128)(2,1)S(1)}, bf16[4,64,256]{2,1,0:T(8,128)(2,1)S(1)}, u32[]{:S(2)}, u32[]{:S(2)}) collective-permute-start(bf16[4,64,256]{2,1,0:T(8,128)(2,1)S(1)} %bitcast.125), channel_id=1, source_target_pairs={{0,16},{1,65},{2,18},{3,67},{4,20},{5,69},{6,22},{7,71},{8,24},{9,... | collective-permute-start | bytes 393224 | tf_op jit(solution)/shard_map/ppermute | solution.py:33
  58.4 2.1 %collective-permute-done.11 = bf16[4,64,256]{2,1,0:T(8,128)(2,1)S(1)} collective-permute-done((bf16[4,64,256]{2,1,0:T(8,128)(2,1)S(1)}, bf16[4,64,256]{2,1,0:T(8,128)(2,1)S(1)}, u32[]{:S(2)}, u32[]{:S(2)}) %collective-permute-start.11) | collective-permute-done | bytes 131104 | tf_op jit(solution)/shard_map/ppermute | solution.py:33
  61.7 2.1 %collective-permute-done.13 = bf16[4,64,256]{2,1,0:T(8,128)(2,1)S(1)} collective-permute-done((bf16[4,64,256]{2,1,0:T(8,128)(2,1)S(1)}, bf16[4,64,256]{2,1,0:T(8,128)(2,1)S(1)}, u32[]{:S(2)}, u32[]{:S(2)}) %collective-permute-start.13) | collective-permute-done | bytes 131104 | tf_op jit(solution)/shard_map/ppermute | solution.py:33
  63.8 2.7 %collective-permute-start.14 = (bf16[4,2,64,256]{3,2,1,0:T(8,128)(2,1)S(1)}, bf16[4,2,64,256]{3,2,1,0:T(8,128)(2,1)S(1)}, u32[]{:S(2)}, u32[]{:S(2)}) collective-permute-start(bf16[4,2,64,256]{3,2,1,0:T(8,128)(2,1)S(1)} %pad_maximum_fusion.1.refs_2_), channel_id=1, source_target_pairs={{0,96},{1,25},{2,98},{3,27},{4,100},{5,29},{6,102},{7,31},{8,104},... | collective-permute-start | bytes 786440 | tf_op jit(solution)/shard_map/ppermute | solution.py:33
  72.0 1.8 %collective-permute-start.22 = (bf16[4,2,64,256]{3,2,1,0:T(8,128)(2,1)S(1)}, bf16[4,2,64,256]{3,2,1,0:T(8,128)(2,1)S(1)}, u32[]{:S(2)}, u32[]{:S(2)}) collective-permute-start(bf16[4,2,64,256]{3,2,1,0:T(8,128)(2,1)S(1)} %pad_maximum_fusion.refs_2_), channel_id=1, source_target_pairs={{0,64},{1,17},{2,66},{3,19},{4,68},{5,21},{6,70},{7,23},{8,72},{9,... | collective-permute-start | bytes 786440 | tf_op jit(solution)/shard_map/ppermute | solution.py:33
  73.8 2.2 %collective-permute-done.15.refs_3_ = bf16[4,2,64,256]{3,2,1,0:T(8,128)(2,1)S(1)} collective-permute-done((bf16[4,2,64,256]{3,2,1,0:T(8,128)(2,1)S(1)}, bf16[4,2,64,256]{3,2,1,0:T(8,128)(2,1)S(1)}, u32[]{:S(2)}, u32[]{:S(2)}) %collective-permute-start.15) | collective-permute-done | bytes 262176 | tf_op jit(solution)/shard_map/ppermute | solution.py:33
  76.1 1.8 forward.11
  77.8 2.1 %adjoint.2 = (bf16[4,2,64,256]{3,2,1,0:T(8,128)(2,1)S(1)}, bf16[4,2,64,256]{3,2,1,0:T(8,128)(2,1)S(1)}, bf16[4,2,64,256]{3,2,1,0:T(8,128)(2,1)S(1)}, bf16[4,2,64,256]{3,2,1,0:T(8,128)(2,1)S(1)}) custom-call(s32[16]{0:T(128)S(1)} %fusion.24.j_ref.refs_0_, f32[2,64,256]{2,1,0:T(8,128)S(1)} %get-tuple-element.60.u_ref.refs_6_.i0a, ...), custom_call_target="tpu_custom_call" | custom-call | flops 2147483648 | bytes 4194304 | tf_op jit(solution)/shard_map/adjoint/pallas_call | solution.py:169
  80.8 2.2 %collective-permute-start.19 = (bf16[4,2,64,256]{3,2,1,0:T(8,128)(2,1)S(1)}, bf16[4,2,64,256]{3,2,1,0:T(8,128)(2,1)S(1)}, u32[]{:S(2)}, u32[]{:S(2)}) collective-permute-start(bf16[4,2,64,256]{3,2,1,0:T(8,128)(2,1)S(1)} %get-tuple-element.65), channel_id=1, source_target_pairs={{0,96},{1,25},{2,98},{3,27},{4,100},{5,29},{6,102},{7,31},{8,104},... | collective-permute-start | bytes 786440 | tf_op jit(solution)/shard_map/ppermute | solution.py:33
  83.0 1.8 forward.12
  84.8 2.1 %adjoint.3 = (bf16[4,2,64,256]{3,2,1,0:T(8,128)(2,1)S(1)}, bf16[4,2,64,256]{3,2,1,0:T(8,128)(2,1)S(1)}, bf16[4,2,64,256]{3,2,1,0:T(8,128)(2,1)S(1)}, bf16[4,2,64,256]{3,2,1,0:T(8,128)(2,1)S(1)}) custom-call(s32[16]{0:T(128)S(1)} %fusion.24.j_ref.refs_0_, f32[2,64,256]{2,1,0:T(8,128)S(1)} %get-tuple-element.68.u_ref.refs_4_.i0b, ...), custom_call_target="tpu_custom_call" | custom-call | flops 2147483648 | bytes 4194304 | tf_op jit(solution)/shard_map/adjoint/pallas_call | solution.py:169
  88.5 2.7 %collective-permute-start.25 = (bf16[4,2,64,256]{3,2,1,0:T(8,128)(2,1)S(1)}, bf16[4,2,64,256]{3,2,1,0:T(8,128)(2,1)S(1)}, u32[]{:S(2)}, u32[]{:S(2)}) collective-permute-start(bf16[4,2,64,256]{3,2,1,0:T(8,128)(2,1)S(1)} %get-tuple-element.73), channel_id=1, source_target_pairs={{0,96},{1,25},{2,98},{3,27},{4,100},{5,29},{6,102},{7,31},{8,104},... | collective-permute-start | bytes 786440 | tf_op jit(solution)/shard_map/ppermute | solution.py:33
  91.3 2.5 %collective-permute-done.23 = bf16[4,2,64,256]{3,2,1,0:T(8,128)(2,1)S(1)} collective-permute-done((bf16[4,2,64,256]{3,2,1,0:T(8,128)(2,1)S(1)}, bf16[4,2,64,256]{3,2,1,0:T(8,128)(2,1)S(1)}, u32[]{:S(2)}, u32[]{:S(2)}) %collective-permute-start.23) | collective-permute-done | bytes 262176 | tf_op jit(solution)/shard_map/ppermute | solution.py:33
  93.8 3.0 %collective-permute-done.24 = bf16[4,2,64,256]{3,2,1,0:T(8,128)(2,1)S(1)} collective-permute-done((bf16[4,2,64,256]{3,2,1,0:T(8,128)(2,1)S(1)}, bf16[4,2,64,256]{3,2,1,0:T(8,128)(2,1)S(1)}, u32[]{:S(2)}, u32[]{:S(2)}) %collective-permute-start.24) | collective-permute-done | bytes 262176 | tf_op jit(solution)/shard_map/ppermute | solution.py:33
  98.4 1.7 collective-permute-start.28
  100.1 2.4 %collective-permute-done.26 = bf16[4,64,256]{2,1,0:T(8,128)(2,1)S(1)} collective-permute-done((bf16[4,64,256]{2,1,0:T(8,128)(2,1)S(1)}, bf16[4,64,256]{2,1,0:T(8,128)(2,1)S(1)}, u32[]{:S(2)}, u32[]{:S(2)}) %collective-permute-start.26) | collective-permute-done | bytes 131104 | tf_op jit(solution)/shard_map/ppermute | solution.py:33
  103.9 4.6 %collective-permute-start.29 = (bf16[4,32,256]{2,1,0:T(8,128)(2,1)S(1)}, bf16[4,32,256]{2,1,0:T(8,128)(2,1)S(1)}, u32[]{:S(2)}, u32[]{:S(2)}) collective-permute-start(bf16[4,32,256]{2,1,0:T(8,128)(2,1)S(1)} %get-tuple-element.120), channel_id=1, source_target_pairs={{0,1},{1,0},{2,3},{3,2},{4,5},{5,4},{6,7},{7,6},{8,9},{9,8},{10,11... | collective-permute-start | bytes 196616 | tf_op jit(solution)/shard_map/ppermute | solution.py:33
  109.4 2.3 %collective-permute-start.30 = (bf16[256,256]{1,0:T(8,128)(2,1)S(1)}, bf16[256,256]{1,0:T(8,128)(2,1)S(1)}, u32[]{:S(2)}, u32[]{:S(2)}) collective-permute-start(bf16[256,256]{1,0:T(8,128)(2,1)S(1)} %bitcast.101), channel_id=1, source_target_pairs={{0,4},{1,5},{2,6},{3,7},{4,0},{5,1},{6,2},{7,3},{8,12},{9,13},{10,... | collective-permute-start | bytes 393224 | tf_op jit(solution)/shard_map/ppermute | solution.py:33
  113.1 2.6 %collective-permute-done.30.refs_2_ = bf16[256,256]{1,0:T(8,128)(2,1)S(1)} collective-permute-done((bf16[256,256]{1,0:T(8,128)(2,1)S(1)}, bf16[256,256]{1,0:T(8,128)(2,1)S(1)}, u32[]{:S(2)}, u32[]{:S(2)}) %collective-permute-start.30) | collective-permute-done | bytes 131104 | tf_op jit(solution)/shard_map/ppermute | solution.py:33
  115.7 2.8 %collective-permute-done.31.refs_3_ = bf16[256,256]{1,0:T(8,128)(2,1)S(1)} collective-permute-done((bf16[256,256]{1,0:T(8,128)(2,1)S(1)}, bf16[256,256]{1,0:T(8,128)(2,1)S(1)}, u32[]{:S(2)}, u32[]{:S(2)}) %collective-permute-start.31) | collective-permute-done | bytes 131104 | tf_op jit(solution)/shard_map/ppermute | solution.py:33
  118.7 3.4 %window.3 = (f32[2,128,256]{2,1,0:T(8,128)S(1)}, bf16[2,128,256]{2,1,0:T(8,128)(2,1)S(1)}, f32[8,128]{1,0:T(8,128)S(1)}) custom-call(s32[2]{0:T(128)S(1)} %pad_add_fusion.place_ref.refs_0_, bf16[256,256]{1,0:T(8,128)(2,1)S(1)} %bitcast.104, bf16[256,256]{1,0:T(8,128)(2,1)S(1)} %collective-permute-done.30.refs_2_, ...), custom_call_target="tpu_custom_call" | custom-call | flops 1073741824 | bytes 4194304 | tf_op jit(solution)/shard_map/window/pallas_call | solution.py:332
  124.5 1.8 %collective-permute-start.34 = (bf16[4,64,256]{2,1,0:T(8,128)(2,1)S(1)}, bf16[4,64,256]{2,1,0:T(8,128)(2,1)S(1)}, u32[]{:S(2)}, u32[]{:S(2)}) collective-permute-start(bf16[4,64,256]{2,1,0:T(8,128)(2,1)S(1)} %bitcast.128), channel_id=1, source_target_pairs={{0,16},{1,65},{2,18},{3,67},{4,20},{5,69},{6,22},{7,71},{8,24},{9,... | collective-permute-start | bytes 393224 | tf_op jit(solution)/shard_map/ppermute | solution.py:33
  127.8 2.4 %collective-permute-done.34 = bf16[4,64,256]{2,1,0:T(8,128)(2,1)S(1)} collective-permute-done((bf16[4,64,256]{2,1,0:T(8,128)(2,1)S(1)}, bf16[4,64,256]{2,1,0:T(8,128)(2,1)S(1)}, u32[]{:S(2)}, u32[]{:S(2)}) %collective-permute-start.34) | collective-permute-done | bytes 131104 | tf_op jit(solution)/shard_map/ppermute | solution.py:33
  132.3 3.2 %collective-permute-start.40 = (bf16[4,2,64,256]{3,2,1,0:T(8,128)(2,1)S(1)}, bf16[4,2,64,256]{3,2,1,0:T(8,128)(2,1)S(1)}, u32[]{:S(2)}, u32[]{:S(2)}) collective-permute-start(bf16[4,2,64,256]{3,2,1,0:T(8,128)(2,1)S(1)} %pad_maximum_fusion.3.refs_2_), channel_id=1, source_target_pairs={{0,96},{1,25},{2,98},{3,27},{4,100},{5,29},{6,102},{7,31},{8,104},... | collective-permute-start | bytes 786440 | tf_op jit(solution)/shard_map/ppermute | solution.py:33
  141.1 1.8 %collective-permute-start.37 = (bf16[4,2,64,256]{3,2,1,0:T(8,128)(2,1)S(1)}, bf16[4,2,64,256]{3,2,1,0:T(8,128)(2,1)S(1)}, u32[]{:S(2)}, u32[]{:S(2)}) collective-permute-start(bf16[4,2,64,256]{3,2,1,0:T(8,128)(2,1)S(1)} %pad_maximum_fusion.2.refs_2_), channel_id=1, source_target_pairs={{0,64},{1,17},{2,66},{3,19},{4,68},{5,21},{6,70},{7,23},{8,72},{9,... | collective-permute-start | bytes 786440 | tf_op jit(solution)/shard_map/ppermute | solution.py:33
  142.9 2.2 %collective-permute-done.41.refs_3_ = bf16[4,2,64,256]{3,2,1,0:T(8,128)(2,1)S(1)} collective-permute-done((bf16[4,2,64,256]{3,2,1,0:T(8,128)(2,1)S(1)}, bf16[4,2,64,256]{3,2,1,0:T(8,128)(2,1)S(1)}, u32[]{:S(2)}, u32[]{:S(2)}) %collective-permute-start.41) | collective-permute-done | bytes 262176 | tf_op jit(solution)/shard_map/ppermute | solution.py:33
  145.1 1.8 forward.15
  146.9 3.8 %collective-permute-done.39.refs_3_ = bf16[4,2,64,256]{3,2,1,0:T(8,128)(2,1)S(1)} collective-permute-done((bf16[4,2,64,256]{3,2,1,0:T(8,128)(2,1)S(1)}, bf16[4,2,64,256]{3,2,1,0:T(8,128)(2,1)S(1)}, u32[]{:S(2)}, u32[]{:S(2)}) %collective-permute-start.39) | collective-permute-done | bytes 262176 | tf_op jit(solution)/shard_map/ppermute | solution.py:33
  153.2 2.4 %collective-permute-start.43 = (f32[8,128]{1,0:T(8,128)S(1)}, f32[8,128]{1,0:T(8,128)S(1)}, u32[]{:S(2)}, u32[]{:S(2)}) collective-permute-start(f32[8,128]{1,0:T(8,128)S(1)} %get-tuple-element.92), channel_id=1, source_target_pairs={{0,1},{1,0},{2,3},{3,2},{4,5},{5,4},{6,7},{7,6},{8,9},{9,8},{10,11... | collective-permute-start | bytes 12296 | tf_op jit(solution)/shard_map/ppermute | solution.py:33
  156.4 1.8 %collective-permute-start.44 = (f32[8,128]{1,0:T(8,128)S(1)}, f32[8,128]{1,0:T(8,128)S(1)}, u32[]{:S(2)}, u32[]{:S(2)}) collective-permute-start(f32[8,128]{1,0:T(8,128)S(1)} %add.354), channel_id=1, source_target_pairs={{0,4},{1,5},{2,6},{3,7},{4,0},{5,1},{6,2},{7,3},{8,12},{9,13},{10,... | collective-permute-start | bytes 12296 | tf_op jit(solution)/shard_map/ppermute | solution.py:33
  158.9 1.9 %collective-permute-start.46 = (f32[8,128]{1,0:T(8,128)S(1)}, f32[8,128]{1,0:T(8,128)S(1)}, u32[]{:S(2)}, u32[]{:S(2)}) collective-permute-start(f32[8,128]{1,0:T(8,128)S(1)} %add.354), channel_id=1, source_target_pairs={{0,6},{1,7},{2,0},{3,1},{4,2},{5,3},{6,4},{7,5},{8,14},{9,15},{10,... | collective-permute-start | bytes 12296 | tf_op jit(solution)/shard_map/ppermute | solution.py:33
  162.1 2.7 %collective-permute-start.49 = (f32[8,128]{1,0:T(8,128)S(1)}, f32[8,128]{1,0:T(8,128)S(1)}, u32[]{:S(2)}, u32[]{:S(2)}) collective-permute-start(f32[8,128]{1,0:T(8,128)S(1)} %add_add_fusion.2), channel_id=1, source_target_pairs={{0,24},{1,97},{2,26},{3,99},{4,28},{5,101},{6,30},{7,103},{8,0},{9... | collective-permute-start | bytes 12296 | tf_op jit(solution)/shard_map/ppermute | solution.py:33
  164.8 3.6 %collective-permute-start.53 = (f32[128,256]{1,0:T(8,128)S(1)}, f32[128,256]{1,0:T(8,128)S(1)}, u32[]{:S(2)}, u32[]{:S(2)}) collective-permute-start(f32[128,256]{1,0:T(8,128)S(1)} %slice_bitcast_fusion.1), channel_id=1, source_target_pairs={{0,1},{1,0},{2,3},{3,2},{4,5},{5,4},{6,7},{7,6},{8,9},{9,8},{10,11... | collective-permute-start | bytes 393224 | tf_op jit(solution)/shard_map/ppermute | solution.py:33
  169.2 2.7 %collective-permute-start.52 = (f32[8,128]{1,0:T(8,128)S(1)}, f32[8,128]{1,0:T(8,128)S(1)}, u32[]{:S(2)}, u32[]{:S(2)}) collective-permute-start(f32[8,128]{1,0:T(8,128)S(1)} %add_add_fusion.1), channel_id=1, source_target_pairs={{0,96},{1,25},{2,98},{3,27},{4,100},{5,29},{6,102},{7,31},{8,104},... | collective-permute-start | bytes 12296 | tf_op jit(solution)/shard_map/ppermute | solution.py:33
  171.9 2.0 %collective-permute-start.54 = (f32[128,256]{1,0:T(8,128)S(1)}, f32[128,256]{1,0:T(8,128)S(1)}, u32[]{:S(2)}, u32[]{:S(2)}) collective-permute-start(f32[128,256]{1,0:T(8,128)S(1)} %slice_bitcast_fusion), channel_id=1, source_target_pairs={{0,1},{1,0},{2,3},{3,2},{4,5},{5,4},{6,7},{7,6},{8,9},{9,8},{10,11... | collective-permute-start | bytes 393224 | tf_op jit(solution)/shard_map/ppermute | solution.py:33
  (124 shorter events, 42.5 us)
Async XLA Ops:
  9.9 10.6 %collective-permute-start = (bf16[4,4,64,256]{3,2,1,0:T(8,128)(2,1)S(1)}, bf16[4,4,64,256]{3,2,1,0:T(8,128)(2,1)S(1)}, u32[]{:S(2)}, u32[]{:S(2)}) collective-permute-start(bf16[4,4,64,256]{3,2,1,0:T(8,128)(2,1)S(1)} %get-tuple-element.52), channel_id=1, source_target_pairs={{0,64},{1,17},{2,66},{3,19},{4,68},{5,21},{6,70},{7,23},{8,72},{9,... | collective-permute-start | bytes 1572872 | tf_op jit(solution)/shard_map/ppermute | solution.py:33
  13.6 12.5 %collective-permute-start.1 = (bf16[4,4,64,256]{3,2,1,0:T(8,128)(2,1)S(1)}, bf16[4,4,64,256]{3,2,1,0:T(8,128)(2,1)S(1)}, u32[]{:S(2)}, u32[]{:S(2)}) collective-permute-start(bf16[4,4,64,256]{3,2,1,0:T(8,128)(2,1)S(1)} %get-tuple-element.53), channel_id=1, source_target_pairs={{0,32},{1,9},{2,34},{3,11},{4,36},{5,13},{6,38},{7,15},{8,40},{9,1... | collective-permute-start | bytes 1572872 | tf_op jit(solution)/shard_map/ppermute | solution.py:33
  13.9 12.5 %collective-permute-start.2 = (bf16[4,4,64,256]{3,2,1,0:T(8,128)(2,1)S(1)}, bf16[4,4,64,256]{3,2,1,0:T(8,128)(2,1)S(1)}, u32[]{:S(2)}, u32[]{:S(2)}) collective-permute-start(bf16[4,4,64,256]{3,2,1,0:T(8,128)(2,1)S(1)} %get-tuple-element.54), channel_id=1, source_target_pairs={{0,96},{1,25},{2,98},{3,27},{4,100},{5,29},{6,102},{7,31},{8,104},... | collective-permute-start | bytes 1572872 | tf_op jit(solution)/shard_map/ppermute | solution.py:33
  26.6 5.7 %collective-permute-start.3 = (bf16[4,64,256]{2,1,0:T(8,128)(2,1)S(1)}, bf16[4,64,256]{2,1,0:T(8,128)(2,1)S(1)}, u32[]{:S(2)}, u32[]{:S(2)}) collective-permute-start(bf16[4,64,256]{2,1,0:T(8,128)(2,1)S(1)} %get-tuple-element.98), channel_id=1, source_target_pairs={{0,16},{1,65},{2,18},{3,67},{4,20},{5,69},{6,22},{7,71},{8,24},{9,... | collective-permute-start | bytes 393224 | tf_op jit(solution)/shard_map/ppermute | solution.py:33
  29.6 5.0 %collective-permute-start.4 = (bf16[4,64,256]{2,1,0:T(8,128)(2,1)S(1)}, bf16[4,64,256]{2,1,0:T(8,128)(2,1)S(1)}, u32[]{:S(2)}, u32[]{:S(2)}) collective-permute-start(bf16[4,64,256]{2,1,0:T(8,128)(2,1)S(1)} %get-tuple-element.100), channel_id=1, source_target_pairs={{0,8},{1,33},{2,10},{3,35},{4,12},{5,37},{6,14},{7,39},{8,16},{9,4... | collective-permute-start | bytes 393224 | tf_op jit(solution)/shard_map/ppermute | solution.py:33
  30.0 4.6 %collective-permute-start.5 = (bf16[4,64,256]{2,1,0:T(8,128)(2,1)S(1)}, bf16[4,64,256]{2,1,0:T(8,128)(2,1)S(1)}, u32[]{:S(2)}, u32[]{:S(2)}) collective-permute-start(bf16[4,64,256]{2,1,0:T(8,128)(2,1)S(1)} %get-tuple-element.99), channel_id=1, source_target_pairs={{0,24},{1,97},{2,26},{3,99},{4,28},{5,101},{6,30},{7,103},{8,0},{9... | collective-permute-start | bytes 393224 | tf_op jit(solution)/shard_map/ppermute | solution.py:33
  38.8 7.3 %collective-permute-start.7 = (bf16[256,256]{1,0:T(8,128)(2,1)S(1)}, bf16[256,256]{1,0:T(8,128)(2,1)S(1)}, u32[]{:S(2)}, u32[]{:S(2)}) collective-permute-start(bf16[256,256]{1,0:T(8,128)(2,1)S(1)} %bitcast.105), channel_id=1, source_target_pairs={{0,4},{1,5},{2,6},{3,7},{4,0},{5,1},{6,2},{7,3},{8,12},{9,13},{10,... | collective-permute-start | bytes 393224 | tf_op jit(solution)/shard_map/ppermute | solution.py:33
  42.4 6.9 %collective-permute-start.8 = (bf16[256,256]{1,0:T(8,128)(2,1)S(1)}, bf16[256,256]{1,0:T(8,128)(2,1)S(1)}, u32[]{:S(2)}, u32[]{:S(2)}) collective-permute-start(bf16[256,256]{1,0:T(8,128)(2,1)S(1)} %bitcast.106), channel_id=1, source_target_pairs={{0,6},{1,7},{2,0},{3,1},{4,2},{5,3},{6,4},{7,5},{8,14},{9,15},{10,... | collective-permute-start | bytes 393224 | tf_op jit(solution)/shard_map/ppermute | solution.py:33
  42.9 6.4 %collective-permute-start.9 = (bf16[256,256]{1,0:T(8,128)(2,1)S(1)}, bf16[256,256]{1,0:T(8,128)(2,1)S(1)}, u32[]{:S(2)}, u32[]{:S(2)}) collective-permute-start(bf16[256,256]{1,0:T(8,128)(2,1)S(1)} %bitcast.107), channel_id=1, source_target_pairs={{0,2},{1,3},{2,4},{3,5},{4,6},{5,7},{6,0},{7,1},{8,10},{9,11},{10,... | collective-permute-start | bytes 393224 | tf_op jit(solution)/shard_map/ppermute | solution.py:33
  54.9 5.7 %collective-permute-start.11 = (bf16[4,64,256]{2,1,0:T(8,128)(2,1)S(1)}, bf16[4,64,256]{2,1,0:T(8,128)(2,1)S(1)}, u32[]{:S(2)}, u32[]{:S(2)}) collective-permute-start(bf16[4,64,256]{2,1,0:T(8,128)(2,1)S(1)} %bitcast.125), channel_id=1, source_target_pairs={{0,16},{1,65},{2,18},{3,67},{4,20},{5,69},{6,22},{7,71},{8,24},{9,... | collective-permute-start | bytes 393224 | tf_op jit(solution)/shard_map/ppermute | solution.py:33
  56.7 4.9 %collective-permute-start.12 = (bf16[4,64,256]{2,1,0:T(8,128)(2,1)S(1)}, bf16[4,64,256]{2,1,0:T(8,128)(2,1)S(1)}, u32[]{:S(2)}, u32[]{:S(2)}) collective-permute-start(bf16[4,64,256]{2,1,0:T(8,128)(2,1)S(1)} %bitcast.126), channel_id=1, source_target_pairs={{0,24},{1,97},{2,26},{3,99},{4,28},{5,101},{6,30},{7,103},{8,0},{9... | collective-permute-start | bytes 393224 | tf_op jit(solution)/shard_map/ppermute | solution.py:33
  58.4 5.3 %collective-permute-start.13 = (bf16[4,64,256]{2,1,0:T(8,128)(2,1)S(1)}, bf16[4,64,256]{2,1,0:T(8,128)(2,1)S(1)}, u32[]{:S(2)}, u32[]{:S(2)}) collective-permute-start(bf16[4,64,256]{2,1,0:T(8,128)(2,1)S(1)} %bitcast.127), channel_id=1, source_target_pairs={{0,8},{1,33},{2,10},{3,35},{4,12},{5,37},{6,14},{7,39},{8,16},{9,4... | collective-permute-start | bytes 393224 | tf_op jit(solution)/shard_map/ppermute | solution.py:33
  63.8 8.2 %collective-permute-start.14 = (bf16[4,2,64,256]{3,2,1,0:T(8,128)(2,1)S(1)}, bf16[4,2,64,256]{3,2,1,0:T(8,128)(2,1)S(1)}, u32[]{:S(2)}, u32[]{:S(2)}) collective-permute-start(bf16[4,2,64,256]{3,2,1,0:T(8,128)(2,1)S(1)} %pad_maximum_fusion.1.refs_2_), channel_id=1, source_target_pairs={{0,96},{1,25},{2,98},{3,27},{4,100},{5,29},{6,102},{7,31},{8,104},... | collective-permute-start | bytes 786440 | tf_op jit(solution)/shard_map/ppermute | solution.py:33
  66.5 9.5 %collective-permute-start.15 = (bf16[4,2,64,256]{3,2,1,0:T(8,128)(2,1)S(1)}, bf16[4,2,64,256]{3,2,1,0:T(8,128)(2,1)S(1)}, u32[]{:S(2)}, u32[]{:S(2)}) collective-permute-start(bf16[4,2,64,256]{3,2,1,0:T(8,128)(2,1)S(1)} %pad_maximum_fusion.1.refs_2_), channel_id=1, source_target_pairs={{0,32},{1,9},{2,34},{3,11},{4,36},{5,13},{6,38},{7,15},{8,40},{9,1... | collective-permute-start | bytes 786440 | tf_op jit(solution)/shard_map/ppermute | solution.py:33
  66.5 9.5 %collective-permute-start.16 = (bf16[4,2,64,256]{3,2,1,0:T(8,128)(2,1)S(1)}, bf16[4,2,64,256]{3,2,1,0:T(8,128)(2,1)S(1)}, u32[]{:S(2)}, u32[]{:S(2)}) collective-permute-start(bf16[4,2,64,256]{3,2,1,0:T(8,128)(2,1)S(1)} %pad_maximum_fusion.1.refs_2_), channel_id=1, source_target_pairs={{0,64},{1,17},{2,66},{3,19},{4,68},{5,21},{6,70},{7,23},{8,72},{9,... | collective-permute-start | bytes 786440 | tf_op jit(solution)/shard_map/ppermute | solution.py:33
  68.9 12.0 %collective-permute-start.20 = (bf16[4,2,64,256]{3,2,1,0:T(8,128)(2,1)S(1)}, bf16[4,2,64,256]{3,2,1,0:T(8,128)(2,1)S(1)}, u32[]{:S(2)}, u32[]{:S(2)}) collective-permute-start(bf16[4,2,64,256]{3,2,1,0:T(8,128)(2,1)S(1)} %pad_maximum_fusion.refs_2_), channel_id=1, source_target_pairs={{0,96},{1,25},{2,98},{3,27},{4,100},{5,29},{6,102},{7,31},{8,104},... | collective-permute-start | bytes 786440 | tf_op jit(solution)/shard_map/ppermute | solution.py:33
  70.4 12.7 %collective-permute-start.21 = (bf16[4,2,64,256]{3,2,1,0:T(8,128)(2,1)S(1)}, bf16[4,2,64,256]{3,2,1,0:T(8,128)(2,1)S(1)}, u32[]{:S(2)}, u32[]{:S(2)}) collective-permute-start(bf16[4,2,64,256]{3,2,1,0:T(8,128)(2,1)S(1)} %pad_maximum_fusion.refs_2_), channel_id=1, source_target_pairs={{0,32},{1,9},{2,34},{3,11},{4,36},{5,13},{6,38},{7,15},{8,40},{9,1... | collective-permute-start | bytes 786440 | tf_op jit(solution)/shard_map/ppermute | solution.py:33
  72.0 11.0 %collective-permute-start.22 = (bf16[4,2,64,256]{3,2,1,0:T(8,128)(2,1)S(1)}, bf16[4,2,64,256]{3,2,1,0:T(8,128)(2,1)S(1)}, u32[]{:S(2)}, u32[]{:S(2)}) collective-permute-start(bf16[4,2,64,256]{3,2,1,0:T(8,128)(2,1)S(1)} %pad_maximum_fusion.refs_2_), channel_id=1, source_target_pairs={{0,64},{1,17},{2,66},{3,19},{4,68},{5,21},{6,70},{7,23},{8,72},{9,... | collective-permute-start | bytes 786440 | tf_op jit(solution)/shard_map/ppermute | solution.py:33
  80.0 8.5 %collective-permute-start.17 = (bf16[4,2,64,256]{3,2,1,0:T(8,128)(2,1)S(1)}, bf16[4,2,64,256]{3,2,1,0:T(8,128)(2,1)S(1)}, u32[]{:S(2)}, u32[]{:S(2)}) collective-permute-start(bf16[4,2,64,256]{3,2,1,0:T(8,128)(2,1)S(1)} %get-tuple-element.63), channel_id=1, source_target_pairs={{0,64},{1,17},{2,66},{3,19},{4,68},{5,21},{6,70},{7,23},{8,72},{9,... | collective-permute-start | bytes 786440 | tf_op jit(solution)/shard_map/ppermute | solution.py:33
  80.3 10.8 %collective-permute-start.18 = (bf16[4,2,64,256]{3,2,1,0:T(8,128)(2,1)S(1)}, bf16[4,2,64,256]{3,2,1,0:T(8,128)(2,1)S(1)}, u32[]{:S(2)}, u32[]{:S(2)}) collective-permute-start(bf16[4,2,64,256]{3,2,1,0:T(8,128)(2,1)S(1)} %get-tuple-element.64), channel_id=1, source_target_pairs={{0,32},{1,9},{2,34},{3,11},{4,36},{5,13},{6,38},{7,15},{8,40},{9,1... | collective-permute-start | bytes 786440 | tf_op jit(solution)/shard_map/ppermute | solution.py:33
  80.8 10.3 %collective-permute-start.19 = (bf16[4,2,64,256]{3,2,1,0:T(8,128)(2,1)S(1)}, bf16[4,2,64,256]{3,2,1,0:T(8,128)(2,1)S(1)}, u32[]{:S(2)}, u32[]{:S(2)}) collective-permute-start(bf16[4,2,64,256]{3,2,1,0:T(8,128)(2,1)S(1)} %get-tuple-element.65), channel_id=1, source_target_pairs={{0,96},{1,25},{2,98},{3,27},{4,100},{5,29},{6,102},{7,31},{8,104},... | collective-permute-start | bytes 786440 | tf_op jit(solution)/shard_map/ppermute | solution.py:33
  86.9 6.9 %collective-permute-start.23 = (bf16[4,2,64,256]{3,2,1,0:T(8,128)(2,1)S(1)}, bf16[4,2,64,256]{3,2,1,0:T(8,128)(2,1)S(1)}, u32[]{:S(2)}, u32[]{:S(2)}) collective-permute-start(bf16[4,2,64,256]{3,2,1,0:T(8,128)(2,1)S(1)} %get-tuple-element.71), channel_id=1, source_target_pairs={{0,64},{1,17},{2,66},{3,19},{4,68},{5,21},{6,70},{7,23},{8,72},{9,... | collective-permute-start | bytes 786440 | tf_op jit(solution)/shard_map/ppermute | solution.py:33
  88.5 8.4 %collective-permute-start.24 = (bf16[4,2,64,256]{3,2,1,0:T(8,128)(2,1)S(1)}, bf16[4,2,64,256]{3,2,1,0:T(8,128)(2,1)S(1)}, u32[]{:S(2)}, u32[]{:S(2)}) collective-permute-start(bf16[4,2,64,256]{3,2,1,0:T(8,128)(2,1)S(1)} %get-tuple-element.72), channel_id=1, source_target_pairs={{0,32},{1,9},{2,34},{3,11},{4,36},{5,13},{6,38},{7,15},{8,40},{9,1... | collective-permute-start | bytes 786440 | tf_op jit(solution)/shard_map/ppermute | solution.py:33
  88.5 8.4 %collective-permute-start.25 = (bf16[4,2,64,256]{3,2,1,0:T(8,128)(2,1)S(1)}, bf16[4,2,64,256]{3,2,1,0:T(8,128)(2,1)S(1)}, u32[]{:S(2)}, u32[]{:S(2)}) collective-permute-start(bf16[4,2,64,256]{3,2,1,0:T(8,128)(2,1)S(1)} %get-tuple-element.73), channel_id=1, source_target_pairs={{0,96},{1,25},{2,98},{3,27},{4,100},{5,29},{6,102},{7,31},{8,104},... | collective-permute-start | bytes 786440 | tf_op jit(solution)/shard_map/ppermute | solution.py:33
  97.0 5.5 %collective-permute-start.26 = (bf16[4,64,256]{2,1,0:T(8,128)(2,1)S(1)}, bf16[4,64,256]{2,1,0:T(8,128)(2,1)S(1)}, u32[]{:S(2)}, u32[]{:S(2)}) collective-permute-start(bf16[4,64,256]{2,1,0:T(8,128)(2,1)S(1)} %pad_maximum_fusion.7), channel_id=1, source_target_pairs={{0,16},{1,65},{2,18},{3,67},{4,20},{5,69},{6,22},{7,71},{8,24},{9,... | collective-permute-start | bytes 393224 | tf_op jit(solution)/shard_map/ppermute | solution.py:33
  97.3 6.5 %collective-permute-start.27 = (bf16[4,64,256]{2,1,0:T(8,128)(2,1)S(1)}, bf16[4,64,256]{2,1,0:T(8,128)(2,1)S(1)}, u32[]{:S(2)}, u32[]{:S(2)}) collective-permute-start(bf16[4,64,256]{2,1,0:T(8,128)(2,1)S(1)} %pad_maximum_fusion.8), channel_id=1, source_target_pairs={{0,8},{1,33},{2,10},{3,35},{4,12},{5,37},{6,14},{7,39},{8,16},{9,4... | collective-permute-start | bytes 393224 | tf_op jit(solution)/shard_map/ppermute | solution.py:33
  98.4 5.4 %collective-permute-start.28 = (bf16[4,64,256]{2,1,0:T(8,128)(2,1)S(1)}, bf16[4,64,256]{2,1,0:T(8,128)(2,1)S(1)}, u32[]{:S(2)}, u32[]{:S(2)}) collective-permute-start(bf16[4,64,256]{2,1,0:T(8,128)(2,1)S(1)} %pad_maximum_fusion.9), channel_id=1, source_target_pairs={{0,24},{1,97},{2,26},{3,99},{4,28},{5,101},{6,30},{7,103},{8,0},{9... | collective-permute-start | bytes 393224 | tf_op jit(solution)/shard_map/ppermute | solution.py:33
  103.9 5.5 %collective-permute-start.29 = (bf16[4,32,256]{2,1,0:T(8,128)(2,1)S(1)}, bf16[4,32,256]{2,1,0:T(8,128)(2,1)S(1)}, u32[]{:S(2)}, u32[]{:S(2)}) collective-permute-start(bf16[4,32,256]{2,1,0:T(8,128)(2,1)S(1)} %get-tuple-element.120), channel_id=1, source_target_pairs={{0,1},{1,0},{2,3},{3,2},{4,5},{5,4},{6,7},{7,6},{8,9},{9,8},{10,11... | collective-permute-start | bytes 196616 | tf_op jit(solution)/shard_map/ppermute | solution.py:33
  109.4 6.3 %collective-permute-start.30 = (bf16[256,256]{1,0:T(8,128)(2,1)S(1)}, bf16[256,256]{1,0:T(8,128)(2,1)S(1)}, u32[]{:S(2)}, u32[]{:S(2)}) collective-permute-start(bf16[256,256]{1,0:T(8,128)(2,1)S(1)} %bitcast.101), channel_id=1, source_target_pairs={{0,4},{1,5},{2,6},{3,7},{4,0},{5,1},{6,2},{7,3},{8,12},{9,13},{10,... | collective-permute-start | bytes 393224 | tf_op jit(solution)/shard_map/ppermute | solution.py:33
  111.6 6.8 %collective-permute-start.31 = (bf16[256,256]{1,0:T(8,128)(2,1)S(1)}, bf16[256,256]{1,0:T(8,128)(2,1)S(1)}, u32[]{:S(2)}, u32[]{:S(2)}) collective-permute-start(bf16[256,256]{1,0:T(8,128)(2,1)S(1)} %bitcast.102), channel_id=1, source_target_pairs={{0,6},{1,7},{2,0},{3,1},{4,2},{5,3},{6,4},{7,5},{8,14},{9,15},{10,... | collective-permute-start | bytes 393224 | tf_op jit(solution)/shard_map/ppermute | solution.py:33
  112.5 6.1 %collective-permute-start.32 = (bf16[256,256]{1,0:T(8,128)(2,1)S(1)}, bf16[256,256]{1,0:T(8,128)(2,1)S(1)}, u32[]{:S(2)}, u32[]{:S(2)}) collective-permute-start(bf16[256,256]{1,0:T(8,128)(2,1)S(1)} %bitcast.103), channel_id=1, source_target_pairs={{0,2},{1,3},{2,4},{3,5},{4,6},{5,7},{6,0},{7,1},{8,10},{9,11},{10,... | collective-permute-start | bytes 393224 | tf_op jit(solution)/shard_map/ppermute | solution.py:33
  124.5 5.7 %collective-permute-start.34 = (bf16[4,64,256]{2,1,0:T(8,128)(2,1)S(1)}, bf16[4,64,256]{2,1,0:T(8,128)(2,1)S(1)}, u32[]{:S(2)}, u32[]{:S(2)}) collective-permute-start(bf16[4,64,256]{2,1,0:T(8,128)(2,1)S(1)} %bitcast.128), channel_id=1, source_target_pairs={{0,16},{1,65},{2,18},{3,67},{4,20},{5,69},{6,22},{7,71},{8,24},{9,... | collective-permute-start | bytes 393224 | tf_op jit(solution)/shard_map/ppermute | solution.py:33
  126.3 4.7 %collective-permute-start.35 = (bf16[4,64,256]{2,1,0:T(8,128)(2,1)S(1)}, bf16[4,64,256]{2,1,0:T(8,128)(2,1)S(1)}, u32[]{:S(2)}, u32[]{:S(2)}) collective-permute-start(bf16[4,64,256]{2,1,0:T(8,128)(2,1)S(1)} %bitcast.129), channel_id=1, source_target_pairs={{0,24},{1,97},{2,26},{3,99},{4,28},{5,101},{6,30},{7,103},{8,0},{9... | collective-permute-start | bytes 393224 | tf_op jit(solution)/shard_map/ppermute | solution.py:33
  127.2 5.0 %collective-permute-start.36 = (bf16[4,64,256]{2,1,0:T(8,128)(2,1)S(1)}, bf16[4,64,256]{2,1,0:T(8,128)(2,1)S(1)}, u32[]{:S(2)}, u32[]{:S(2)}) collective-permute-start(bf16[4,64,256]{2,1,0:T(8,128)(2,1)S(1)} %bitcast.130), channel_id=1, source_target_pairs={{0,8},{1,33},{2,10},{3,35},{4,12},{5,37},{6,14},{7,39},{8,16},{9,4... | collective-permute-start | bytes 393224 | tf_op jit(solution)/shard_map/ppermute | solution.py:33
  132.3 8.7 %collective-permute-start.40 = (bf16[4,2,64,256]{3,2,1,0:T(8,128)(2,1)S(1)}, bf16[4,2,64,256]{3,2,1,0:T(8,128)(2,1)S(1)}, u32[]{:S(2)}, u32[]{:S(2)}) collective-permute-start(bf16[4,2,64,256]{3,2,1,0:T(8,128)(2,1)S(1)} %pad_maximum_fusion.3.refs_2_), channel_id=1, source_target_pairs={{0,96},{1,25},{2,98},{3,27},{4,100},{5,29},{6,102},{7,31},{8,104},... | collective-permute-start | bytes 786440 | tf_op jit(solution)/shard_map/ppermute | solution.py:33
  135.6 9.5 %collective-permute-start.41 = (bf16[4,2,64,256]{3,2,1,0:T(8,128)(2,1)S(1)}, bf16[4,2,64,256]{3,2,1,0:T(8,128)(2,1)S(1)}, u32[]{:S(2)}, u32[]{:S(2)}) collective-permute-start(bf16[4,2,64,256]{3,2,1,0:T(8,128)(2,1)S(1)} %pad_maximum_fusion.3.refs_2_), channel_id=1, source_target_pairs={{0,32},{1,9},{2,34},{3,11},{4,36},{5,13},{6,38},{7,15},{8,40},{9,1... | collective-permute-start | bytes 786440 | tf_op jit(solution)/shard_map/ppermute | solution.py:33
  135.6 9.5 %collective-permute-start.42 = (bf16[4,2,64,256]{3,2,1,0:T(8,128)(2,1)S(1)}, bf16[4,2,64,256]{3,2,1,0:T(8,128)(2,1)S(1)}, u32[]{:S(2)}, u32[]{:S(2)}) collective-permute-start(bf16[4,2,64,256]{3,2,1,0:T(8,128)(2,1)S(1)} %pad_maximum_fusion.3.refs_2_), channel_id=1, source_target_pairs={{0,64},{1,17},{2,66},{3,19},{4,68},{5,21},{6,70},{7,23},{8,72},{9,... | collective-permute-start | bytes 786440 | tf_op jit(solution)/shard_map/ppermute | solution.py:33
  137.9 9.0 %collective-permute-start.38 = (bf16[4,2,64,256]{3,2,1,0:T(8,128)(2,1)S(1)}, bf16[4,2,64,256]{3,2,1,0:T(8,128)(2,1)S(1)}, u32[]{:S(2)}, u32[]{:S(2)}) collective-permute-start(bf16[4,2,64,256]{3,2,1,0:T(8,128)(2,1)S(1)} %pad_maximum_fusion.2.refs_2_), channel_id=1, source_target_pairs={{0,96},{1,25},{2,98},{3,27},{4,100},{5,29},{6,102},{7,31},{8,104},... | collective-permute-start | bytes 786440 | tf_op jit(solution)/shard_map/ppermute | solution.py:33
  139.4 11.3 %collective-permute-start.39 = (bf16[4,2,64,256]{3,2,1,0:T(8,128)(2,1)S(1)}, bf16[4,2,64,256]{3,2,1,0:T(8,128)(2,1)S(1)}, u32[]{:S(2)}, u32[]{:S(2)}) collective-permute-start(bf16[4,2,64,256]{3,2,1,0:T(8,128)(2,1)S(1)} %pad_maximum_fusion.2.refs_2_), channel_id=1, source_target_pairs={{0,32},{1,9},{2,34},{3,11},{4,36},{5,13},{6,38},{7,15},{8,40},{9,1... | collective-permute-start | bytes 786440 | tf_op jit(solution)/shard_map/ppermute | solution.py:33
  141.1 11.0 %collective-permute-start.37 = (bf16[4,2,64,256]{3,2,1,0:T(8,128)(2,1)S(1)}, bf16[4,2,64,256]{3,2,1,0:T(8,128)(2,1)S(1)}, u32[]{:S(2)}, u32[]{:S(2)}) collective-permute-start(bf16[4,2,64,256]{3,2,1,0:T(8,128)(2,1)S(1)} %pad_maximum_fusion.2.refs_2_), channel_id=1, source_target_pairs={{0,64},{1,17},{2,66},{3,19},{4,68},{5,21},{6,70},{7,23},{8,72},{9,... | collective-permute-start | bytes 786440 | tf_op jit(solution)/shard_map/ppermute | solution.py:33
  156.4 4.5 %collective-permute-start.44 = (f32[8,128]{1,0:T(8,128)S(1)}, f32[8,128]{1,0:T(8,128)S(1)}, u32[]{:S(2)}, u32[]{:S(2)}) collective-permute-start(f32[8,128]{1,0:T(8,128)S(1)} %add.354), channel_id=1, source_target_pairs={{0,4},{1,5},{2,6},{3,7},{4,0},{5,1},{6,2},{7,3},{8,12},{9,13},{10,... | collective-permute-start | bytes 12296 | tf_op jit(solution)/shard_map/ppermute | solution.py:33
  161.8 6.6 %collective-permute-start.47 = (f32[8,128]{1,0:T(8,128)S(1)}, f32[8,128]{1,0:T(8,128)S(1)}, u32[]{:S(2)}, u32[]{:S(2)}) collective-permute-start(f32[8,128]{1,0:T(8,128)S(1)} %add_add_fusion.2), channel_id=1, source_target_pairs={{0,16},{1,65},{2,18},{3,67},{4,20},{5,69},{6,22},{7,71},{8,24},{9,... | collective-permute-start | bytes 12296 | tf_op jit(solution)/shard_map/ppermute | solution.py:33
  162.1 6.3 %collective-permute-start.48 = (f32[8,128]{1,0:T(8,128)S(1)}, f32[8,128]{1,0:T(8,128)S(1)}, u32[]{:S(2)}, u32[]{:S(2)}) collective-permute-start(f32[8,128]{1,0:T(8,128)S(1)} %add_add_fusion.2), channel_id=1, source_target_pairs={{0,8},{1,33},{2,10},{3,35},{4,12},{5,37},{6,14},{7,39},{8,16},{9,4... | collective-permute-start | bytes 12296 | tf_op jit(solution)/shard_map/ppermute | solution.py:33
  162.1 6.3 %collective-permute-start.49 = (f32[8,128]{1,0:T(8,128)S(1)}, f32[8,128]{1,0:T(8,128)S(1)}, u32[]{:S(2)}, u32[]{:S(2)}) collective-permute-start(f32[8,128]{1,0:T(8,128)S(1)} %add_add_fusion.2), channel_id=1, source_target_pairs={{0,24},{1,97},{2,26},{3,99},{4,28},{5,101},{6,30},{7,103},{8,0},{9... | collective-permute-start | bytes 12296 | tf_op jit(solution)/shard_map/ppermute | solution.py:33
  164.8 9.0 %collective-permute-start.53 = (f32[128,256]{1,0:T(8,128)S(1)}, f32[128,256]{1,0:T(8,128)S(1)}, u32[]{:S(2)}, u32[]{:S(2)}) collective-permute-start(f32[128,256]{1,0:T(8,128)S(1)} %slice_bitcast_fusion.1), channel_id=1, source_target_pairs={{0,1},{1,0},{2,3},{3,2},{4,5},{5,4},{6,7},{7,6},{8,9},{9,8},{10,11... | collective-permute-start | bytes 393224 | tf_op jit(solution)/shard_map/ppermute | solution.py:33
  168.5 5.4 %collective-permute-start.50 = (f32[8,128]{1,0:T(8,128)S(1)}, f32[8,128]{1,0:T(8,128)S(1)}, u32[]{:S(2)}, u32[]{:S(2)}) collective-permute-start(f32[8,128]{1,0:T(8,128)S(1)} %add_add_fusion.1), channel_id=1, source_target_pairs={{0,64},{1,17},{2,66},{3,19},{4,68},{5,21},{6,70},{7,23},{8,72},{9,... | collective-permute-start | bytes 12296 | tf_op jit(solution)/shard_map/ppermute | solution.py:33
  169.2 4.7 %collective-permute-start.51 = (f32[8,128]{1,0:T(8,128)S(1)}, f32[8,128]{1,0:T(8,128)S(1)}, u32[]{:S(2)}, u32[]{:S(2)}) collective-permute-start(f32[8,128]{1,0:T(8,128)S(1)} %add_add_fusion.1), channel_id=1, source_target_pairs={{0,32},{1,9},{2,34},{3,11},{4,36},{5,13},{6,38},{7,15},{8,40},{9,1... | collective-permute-start | bytes 12296 | tf_op jit(solution)/shard_map/ppermute | solution.py:33
  169.2 4.7 %collective-permute-start.52 = (f32[8,128]{1,0:T(8,128)S(1)}, f32[8,128]{1,0:T(8,128)S(1)}, u32[]{:S(2)}, u32[]{:S(2)}) collective-permute-start(f32[8,128]{1,0:T(8,128)S(1)} %add_add_fusion.1), channel_id=1, source_target_pairs={{0,96},{1,25},{2,98},{3,27},{4,100},{5,29},{6,102},{7,31},{8,104},... | collective-permute-start | bytes 12296 | tf_op jit(solution)/shard_map/ppermute | solution.py:33
  (11 other events, 183.3 us)
